TPU v7x, 256 devices: a whole 4x4x8 slice. The times are simulated.
256 devices in a mesh: block: 16 (over y, x), space: 16 (over z, core).
Axes of the slice: x: 4, y: 4, z: 8, core: 2. Of those that a mesh axis runs over, the one named last changes fastest.
Arguments:
- video: bfloat16 [32, 4, 32, 128, 128], P('block', None, 'space'), may hold values from -6 to 6
- pred_slot: int32 [32], P('block'), may hold values from -1 to 30, as said below
- frames: int32 [32], P('block'), may hold values from 0 to 4, as said below
- gain_one: float32 [128], replicated, may hold values from 0.1 to 1.9
- conv_one: bfloat16 [3, 3, 3, 128, 128], replicated, may hold values from -0.109375 to 0.109375
- bias_one: float32 [128], replicated, may hold values from -3 to 3
- gain_two: float32 [128], replicated, may hold values from 0.1 to 1.9
- conv_two: bfloat16 [3, 3, 3, 128, 128], replicated, may hold values from -0.109375 to 0.109375
- bias_two: float32 [128], replicated, may hold values from -3 to 3
- down_weight: bfloat16 [3, 3, 3, 128, 256], replicated, may hold values from -0.109375 to 0.109375
- down_bias: float32 [256], replicated, may hold values from -3 to 3
Outputs:
- latent: bfloat16 [32, 2, 16, 64, 256], P('block', None, 'space')
Inputs may be any that keep to these rules, and one draw needn't show every extreme that they name: pred_slot[s] is -1 for the first block of a video and for empty slots; otherwise it is the previous live slot in slot order: slot s - 1 on the same index of block, or the last live slot of the previous index of block for the first slot of an index. A block that is some slot's predecessor has 4 live frames. Live slots come first on every index of block, and every index holds at least one; an empty slot has 0 frames, a block with a successor 4, a video's last block 1 to 4. Frames past the live ones hold padding.
All inputs are finite; a program needn't handle non-finite values.
Results may differ from a plain program's by a relative error of at most 0.0051.
Values may be sent and summed in bfloat16 or wider, within the bound.
No kernel may reach another device: no remote copies, remote signals or barrier semaphores. Data moves between devices by JAX's collectives and lax.ppermute only.
A program may use at most 64 MiB of HBM per device.

v0:
```python
import jax
import jax.numpy as jnp
from jax import lax
from jax.sharding import PartitionSpec as P


def shifted(block, axis, distance):
    devices = range(lax.axis_size(axis))
    route = [(i - distance, i) for i in devices if i - distance in devices]
    return lax.ppermute(block, axis, route)


def padded(x, sides, width):
    for axis, dim in sides:
        count, length = (lax.axis_size(axis), x.shape[dim])
        up = [(i, (i + 1) % count) for i in range(count - 1)]
        down = [(j, i) for i, j in up]
        last = lax.slice_in_dim(x, length - width, length, axis=dim)
        initial = lax.slice_in_dim(x, 0, width, axis=dim)
        before = lax.ppermute(last, axis, up)
        after = lax.ppermute(initial, axis, down)
        x = jnp.concatenate([before, x, after], axis=dim)
    return x


def activate(values, gain):
    values = values.astype(jnp.float32)
    scaled = values * lax.rsqrt(jnp.mean(values * values, axis=-1, keepdims=True) + 1e-06) * gain
    return jax.nn.silu(scaled)


def context(activity, pred_slot, first_slot):
    slot_count = activity.shape[0]
    length = activity.shape[1]
    tail_frames = activity[:, length - 2 :]
    received = shifted(tail_frames, "block", 1)
    candidates = jnp.concatenate([received, tail_frames], axis=0)
    target = pred_slot - (first_slot - slot_count)
    select = (target[:, None] == jnp.arange(2 * slot_count, dtype=jnp.int32)[None, :]) & (
        pred_slot >= 0
    )[:, None]
    picked = jnp.einsum(
        "ij,jtrwc->itrwc",
        select.astype(jnp.bfloat16),
        candidates,
        preferred_element_type=jnp.float32,
    )
    return picked.astype(jnp.bfloat16)


def run_conv(extended, weight, strides, pad):
    return lax.conv_general_dilated(
        extended,
        weight,
        strides,
        pad,
        dimension_numbers=("NDHWC", "DHWIO", "NDHWC"),
        preferred_element_type=jnp.float32,
    )


def full_layer(activity, pred_slot, first_slot, weight):
    extended = jnp.concatenate([context(activity, pred_slot, first_slot), activity], axis=1)
    extended = padded(extended, (("space", 2),), 1)
    return run_conv(extended, weight, (1, 1, 1), ((0, 0), (0, 0), (1, 1)))


def local(
    video,
    pred_slot,
    frames,
    gain_one,
    conv_one,
    bias_one,
    gain_two,
    conv_two,
    bias_two,
    down_weight,
    down_bias,
):
    slot_count = video.shape[0]
    length = video.shape[1]
    band_rows = video.shape[2]
    first_slot = lax.axis_index("block") * slot_count
    first_act = activate(video, gain_one).astype(jnp.bfloat16)
    hidden_one = full_layer(first_act, pred_slot, first_slot, conv_one) + bias_one
    second_act = activate(hidden_one, gain_two).astype(jnp.bfloat16)
    hidden_two = full_layer(second_act, pred_slot, first_slot, conv_two) + bias_two
    summed = (video.astype(jnp.float32) + hidden_two).astype(jnp.bfloat16)
    extended = jnp.concatenate([context(summed, pred_slot, first_slot), summed], axis=1)
    above = shifted(extended[:, :, band_rows - 1 : band_rows], "space", 1)
    extended = jnp.concatenate([above, extended], axis=2)
    down = run_conv(extended, down_weight, (2, 2, 2), ((0, 0), (0, 0), (1, 1))) + down_bias
    out_frames = jnp.arange(length // 2, dtype=jnp.int32)
    keep = (2 * out_frames)[None, :] < frames[:, None]
    down = jnp.where(keep[:, :, None, None, None], down, jnp.zeros_like(down))
    return down.astype(jnp.bfloat16)


def solution(mesh):
    return jax.shard_map(
        local,
        mesh=mesh,
        in_specs=(
            P("block", None, "space", None, None),
            P("block"),
            P("block"),
            P(),
            P(),
            P(),
            P(),
            P(),
            P(),
            P(),
            P(),
        ),
        out_specs=P("block", None, "space", None, None),
        check_vma=False,
    )
```

profile of v0, /device:TPU:136, one launch (start us, length us, event | category | flops | bytes accessed | tf_op | source)
XLA Modules:
  0.0 103.3 jit_solution(6586742518275830816)
XLA Ops:
  0.0 1.5 %fusion.38 = f32[2,4,2,128]{3,2,1,0:T(2,128)S(1)} fusion(bf16[2,4,2,128,128]{4,3,2,1,0:T(8,128)(2,1)} %param.11), kind=kLoop, calls=%fused_computation.31 | loop fusion | flops 784384 | bytes 532480 | tf_op jit(solution)/shard_map/reduce_sum | solution.py:28
  1.6 1.4 %fusion.45 = bf16[2,4,2,128,128]{4,3,2,1,0:T(8,128)(2,1)S(1)} fusion(bf16[2,4,2,128,128]{4,3,2,1,0:T(8,128)(2,1)} %param.11, f32[128]{0:T(128)} %param.14, f32[2,4,2,128]{3,2,1,0:T(2,128)S(1)} %copy.84), kind=kLoop, calls=%fused_computation.38 | loop fusion | flops 2097152 | bytes 1057280 | tf_op jit(solution)/shard_map/convert_element_type | solution.py:85
  3.0 3.4 %collective-permute-start = (bf16[2,2,2,128,128]{4,3,2,1,0:T(8,128)(2,1)S(1)}, bf16[2,2,2,128,128]{4,3,2,1,0:T(8,128)(2,1)S(1)}, u32[]{:S(2)}, u32[]{:S(2)}) collective-permute-start(bf16[2,2,2,128,128]{4,3,2,1,0:T(8,128)(2,1)S(1)} %slice.39), channel_id=1, source_target_pairs={{0,16},{16,32},{32,48},{48,64},{64,80},{80,96},{96,112},{112,128},... | collective-permute-start | bytes 786440 | tf_op jit(solution)/shard_map/ppermute | solution.py:10
  6.5 8.6 %collective-permute-done = bf16[2,2,2,128,128]{4,3,2,1,0:T(8,128)(2,1)S(1)} collective-permute-done((bf16[2,2,2,128,128]{4,3,2,1,0:T(8,128)(2,1)S(1)}, bf16[2,2,2,128,128]{4,3,2,1,0:T(8,128)(2,1)S(1)}, u32[]{:S(2)}, u32[]{:S(2)}) %collective-permute-start) | collective-permute-done | bytes 262176 | tf_op jit(solution)/shard_map/ppermute | solution.py:10
  15.1 0.5 fusion.53
  15.8 1.9 %collective-permute-start.1 = (bf16[2,6,1,128,128]{4,3,2,1,0:T(8,128)(2,1)S(1)}, bf16[2,6,1,128,128]{4,3,2,1,0:T(8,128)(2,1)S(1)}, u32[]{:S(2)}, u32[]{:S(2)}) collective-permute-start(bf16[2,6,1,128,128]{4,3,2,1,0:T(8,128)(2,1)S(1)} %get-tuple-element.7), channel_id=1, source_target_pairs={{0,1},{1,2},{2,3},{3,4},{4,5},{5,6},{6,7},{7,8},{8,9},{9,10},{10,1... | collective-permute-start | bytes 1179656 | tf_op jit(solution)/shard_map/ppermute | solution.py:20
  17.8 4.9 %collective-permute-start.2 = (bf16[2,6,1,128,128]{4,3,2,1,0:T(8,128)(2,1)S(1)}, bf16[2,6,1,128,128]{4,3,2,1,0:T(8,128)(2,1)S(1)}, u32[]{:S(2)}, u32[]{:S(2)}) collective-permute-start(bf16[2,6,1,128,128]{4,3,2,1,0:T(8,128)(2,1)S(1)} %get-tuple-element.8), channel_id=1, source_target_pairs={{1,0},{2,1},{3,2},{4,3},{5,4},{6,5},{7,6},{8,7},{9,8},{10,9},{11,1... | collective-permute-start | bytes 1179656 | tf_op jit(solution)/shard_map/ppermute | solution.py:21
  22.6 3.5 %collective-permute-done.1 = bf16[2,6,1,128,128]{4,3,2,1,0:T(8,128)(2,1)S(1)} collective-permute-done((bf16[2,6,1,128,128]{4,3,2,1,0:T(8,128)(2,1)S(1)}, bf16[2,6,1,128,128]{4,3,2,1,0:T(8,128)(2,1)S(1)}, u32[]{:S(2)}, u32[]{:S(2)}) %collective-permute-start.1) | collective-permute-done | bytes 393248 | tf_op jit(solution)/shard_map/ppermute | solution.py:20
  26.1 1.8 %collective-permute-done.2 = bf16[2,6,1,128,128]{4,3,2,1,0:T(8,128)(2,1)S(1)} collective-permute-done((bf16[2,6,1,128,128]{4,3,2,1,0:T(8,128)(2,1)S(1)}, bf16[2,6,1,128,128]{4,3,2,1,0:T(8,128)(2,1)S(1)}, u32[]{:S(2)}, u32[]{:S(2)}) %collective-permute-start.2) | collective-permute-done | bytes 393248 | tf_op jit(solution)/shard_map/ppermute | solution.py:21
  27.9 0.2 maximum_bitcast_fusion
  28.1 1.6 %copy.109 = bf16[6,4,2,128,128]{4,2,3,1,0:T(2,128)(2,1)S(1)} copy(bf16[6,4,2,128,128]{4,3,1,0,2:T(8,128)(2,1)S(1)} %maximum_bitcast_fusion) | data formatting | bytes 3145728
  29.7 1.3 %pad.clone = bf16[6,4,2,136,128]{4,2,3,1,0:T(2,128)(2,1)S(1)} pad(bf16[6,4,2,128,128]{4,2,3,1,0:T(2,128)(2,1)S(1)} %copy.109, bf16[]{:T(256)} %constant.28), padding=0_0x0_0x0_0x1_7x0_0 | pad | bytes 3244034 | tf_op jit(solution)/shard_map/concatenate | solution.py:22
  31.0 0.1 slice.42
  31.2 1.7 %fusion.2 = bf16[6,4,2,8,19,128]{5,2,4,3,1,0:T(2,128)(2,1)S(1)} fusion(bf16[6,4,2,7,2,128]{5,2,4,3,1,0:T(2,128)(2,1)S(1)} %slice.42, bf16[6,4,2,8,17,128]{5,2,4,3,1,0:T(2,128)(2,1)S(1)} %bitcast.76), kind=kLoop, calls=%fused_computation.4 | loop fusion | flops 5603328 | bytes 3710976 | tf_op jit(solution)/shard_map/conv_general_dilated | solution.py:52
  32.9 4.4 %multiply_reduce_fusion = (f32[4,2,16,17]{2,3,1,0:T(8,128)S(1)}, f32[4,2,16,17,128]{4,2,3,1,0:T(8,128)S(1)}) fusion(f32[128]{0:T(128)S(1)} %copy-done.7, bf16[3,3,3,128,128]{4,3,2,1,0:T(8,128)(2,1)S(1)} %copy-done.3, bf16[6,4,2,8,19,128]{5,2,4,3,1,0:T(2,128)(2,1)S(1)} %fusion.2, pred[16,17]{0,1:T(8,128)(4,1)S(1)} %copy-done.10), kind=kOutput, calls=%fused_computation.30 | convolution fusion | flops 1926297472 | bytes 3876112 | tf_op jit(solution)/shard_map/conv_general_dilated | solution.py:52
  37.3 0.6 copy.89
  38.0 0.1 copy.91
  38.1 0.1 reshape.67
  38.2 0.3 copy-done.2
  38.5 0.4 multiply_convert_fusion
  38.9 1.9 %collective-permute-start.3 = (bf16[2,2,2,128,128]{4,3,2,1,0:T(8,128)(2,1)S(1)}, bf16[2,2,2,128,128]{4,3,2,1,0:T(8,128)(2,1)S(1)}, u32[]{:S(2)}, u32[]{:S(2)}) collective-permute-start(bf16[2,2,2,128,128]{4,3,2,1,0:T(8,128)(2,1)S(1)} %slice.45), channel_id=1, source_target_pairs={{0,16},{16,32},{32,48},{48,64},{64,80},{80,96},{96,112},{112,128},... | collective-permute-start | bytes 786440 | tf_op jit(solution)/shard_map/ppermute | solution.py:10
  40.9 10.4 %collective-permute-done.3 = bf16[2,2,2,128,128]{4,3,2,1,0:T(8,128)(2,1)S(1)} collective-permute-done((bf16[2,2,2,128,128]{4,3,2,1,0:T(8,128)(2,1)S(1)}, bf16[2,2,2,128,128]{4,3,2,1,0:T(8,128)(2,1)S(1)}, u32[]{:S(2)}, u32[]{:S(2)}) %collective-permute-start.3) | collective-permute-done | bytes 262176 | tf_op jit(solution)/shard_map/ppermute | solution.py:10
  51.3 0.6 fusion.51
  52.0 1.9 %collective-permute-start.4 = (bf16[2,6,1,128,128]{4,3,2,1,0:T(8,128)(2,1)S(1)}, bf16[2,6,1,128,128]{4,3,2,1,0:T(8,128)(2,1)S(1)}, u32[]{:S(2)}, u32[]{:S(2)}) collective-permute-start(bf16[2,6,1,128,128]{4,3,2,1,0:T(8,128)(2,1)S(1)} %get-tuple-element.5), channel_id=1, source_target_pairs={{0,1},{1,2},{2,3},{3,4},{4,5},{5,6},{6,7},{7,8},{8,9},{9,10},{10,1... | collective-permute-start | bytes 1179656 | tf_op jit(solution)/shard_map/ppermute | solution.py:20
  53.9 5.0 %collective-permute-start.5 = (bf16[2,6,1,128,128]{4,3,2,1,0:T(8,128)(2,1)S(1)}, bf16[2,6,1,128,128]{4,3,2,1,0:T(8,128)(2,1)S(1)}, u32[]{:S(2)}, u32[]{:S(2)}) collective-permute-start(bf16[2,6,1,128,128]{4,3,2,1,0:T(8,128)(2,1)S(1)} %get-tuple-element.6), channel_id=1, source_target_pairs={{1,0},{2,1},{3,2},{4,3},{5,4},{6,5},{7,6},{8,7},{9,8},{10,9},{11,1... | collective-permute-start | bytes 1179656 | tf_op jit(solution)/shard_map/ppermute | solution.py:21
  58.9 3.3 %collective-permute-done.4 = bf16[2,6,1,128,128]{4,3,2,1,0:T(8,128)(2,1)S(1)} collective-permute-done((bf16[2,6,1,128,128]{4,3,2,1,0:T(8,128)(2,1)S(1)}, bf16[2,6,1,128,128]{4,3,2,1,0:T(8,128)(2,1)S(1)}, u32[]{:S(2)}, u32[]{:S(2)}) %collective-permute-start.4) | collective-permute-done | bytes 393248 | tf_op jit(solution)/shard_map/ppermute | solution.py:20
  62.3 1.8 %collective-permute-done.5 = bf16[2,6,1,128,128]{4,3,2,1,0:T(8,128)(2,1)S(1)} collective-permute-done((bf16[2,6,1,128,128]{4,3,2,1,0:T(8,128)(2,1)S(1)}, bf16[2,6,1,128,128]{4,3,2,1,0:T(8,128)(2,1)S(1)}, u32[]{:S(2)}, u32[]{:S(2)}) %collective-permute-start.5) | collective-permute-done | bytes 393248 | tf_op jit(solution)/shard_map/ppermute | solution.py:21
  64.0 0.2 maximum_bitcast_fusion.1
  64.2 1.6 %copy.110 = bf16[6,4,2,128,128]{4,2,3,1,0:T(2,128)(2,1)S(1)} copy(bf16[6,4,2,128,128]{4,3,1,0,2:T(8,128)(2,1)S(1)} %maximum_bitcast_fusion.1) | data formatting | bytes 3145728
  65.9 1.3 %pad.2.clone = bf16[6,4,2,136,128]{4,2,3,1,0:T(2,128)(2,1)S(1)} pad(bf16[6,4,2,128,128]{4,2,3,1,0:T(2,128)(2,1)S(1)} %copy.110, bf16[]{:T(256)} %constant.28), padding=0_0x0_0x0_0x1_7x0_0 | pad | bytes 3244034 | tf_op jit(solution)/shard_map/concatenate | solution.py:22
  67.1 0.1 slice.48
  67.3 1.7 %fusion.3 = bf16[6,4,2,8,19,128]{5,2,4,3,1,0:T(2,128)(2,1)S(1)} fusion(bf16[6,4,2,7,2,128]{5,2,4,3,1,0:T(2,128)(2,1)S(1)} %slice.48, bf16[6,4,2,8,17,128]{5,2,4,3,1,0:T(2,128)(2,1)S(1)} %bitcast.78), kind=kLoop, calls=%fused_computation.5 | loop fusion | flops 5603328 | bytes 3710976 | tf_op jit(solution)/shard_map/conv_general_dilated | solution.py:52
  69.0 4.3 %fusion.23 = f32[4,2,16,17,128]{4,2,3,1,0:T(8,128)S(1)} fusion(bf16[3,3,3,128,128]{4,3,2,1,0:T(8,128)(2,1)S(1)} %copy-done.4, bf16[6,4,2,8,19,128]{5,2,4,3,1,0:T(2,128)(2,1)S(1)} %fusion.3, f32[128]{0:T(128)S(1)} %copy-done.8, pred[16,17]{0,1:T(8,128)(4,1)S(1)} %copy-done.10), kind=kOutput, calls=%fused_computation.24 | convolution fusion | flops 1925742592 | bytes 3867408 | tf_op jit(solution)/shard_map/conv_general_dilated | solution.py:52
  73.3 0.6 copy.97
  74.0 1.0 copy-done.1
  75.0 0.1 fusion.46
  75.1 1.9 %collective-permute-start.6 = (bf16[2,2,2,128,128]{4,3,2,1,0:T(8,128)(2,1)S(1)}, bf16[2,2,2,128,128]{4,3,2,1,0:T(8,128)(2,1)S(1)}, u32[]{:S(2)}, u32[]{:S(2)}) collective-permute-start(bf16[2,2,2,128,128]{4,3,2,1,0:T(8,128)(2,1)S(1)} %slice.50), channel_id=1, source_target_pairs={{0,16},{16,32},{32,48},{48,64},{64,80},{80,96},{96,112},{112,128},... | collective-permute-start | bytes 786440 | tf_op jit(solution)/shard_map/ppermute | solution.py:10
  77.1 9.7 %collective-permute-done.6 = bf16[2,2,2,128,128]{4,3,2,1,0:T(8,128)(2,1)S(1)} collective-permute-done((bf16[2,2,2,128,128]{4,3,2,1,0:T(8,128)(2,1)S(1)}, bf16[2,2,2,128,128]{4,3,2,1,0:T(8,128)(2,1)S(1)}, u32[]{:S(2)}, u32[]{:S(2)}) %collective-permute-start.6) | collective-permute-done | bytes 262176 | tf_op jit(solution)/shard_map/ppermute | solution.py:10
  86.9 0.6 fusion.49
  87.5 2.1 %collective-permute-start.7 = (bf16[2,6,1,128,128]{4,3,2,1,0:T(8,128)(2,1)S(1)}, bf16[2,6,1,128,128]{4,3,2,1,0:T(8,128)(2,1)S(1)}, u32[]{:S(2)}, u32[]{:S(2)}) collective-permute-start(bf16[2,6,1,128,128]{4,3,2,1,0:T(8,128)(2,1)S(1)} %pad_maximum_fusion.3), channel_id=1, source_target_pairs={{0,1},{1,2},{2,3},{3,4},{4,5},{5,6},{6,7},{7,8},{8,9},{9,10},{10,1... | collective-permute-start | bytes 1179656 | tf_op jit(solution)/shard_map/ppermute | solution.py:10
  89.9 7.9 %collective-permute-done.7 = bf16[2,6,1,128,128]{4,3,2,1,0:T(8,128)(2,1)S(1)} collective-permute-done((bf16[2,6,1,128,128]{4,3,2,1,0:T(8,128)(2,1)S(1)}, bf16[2,6,1,128,128]{4,3,2,1,0:T(8,128)(2,1)S(1)}, u32[]{:S(2)}, u32[]{:S(2)}) %collective-permute-start.7) | collective-permute-done | bytes 393248 | tf_op jit(solution)/shard_map/ppermute | solution.py:10
  97.8 0.1 maximum_bitcast_fusion.2
  97.9 1.2 %copy.111 = bf16[6,3,2,128,128]{4,2,3,1,0:T(2,128)(2,1)S(1)} copy(bf16[6,3,2,128,128]{4,3,1,0,2:T(8,128)(2,1)S(1)} %maximum_bitcast_fusion.2) | data formatting | bytes 2359296
  99.2 1.0 pad.4.clone
  100.3 1.3 %fusion.10 = bf16[6,3,2,8,20,128]{5,2,4,3,1,0:T(2,128)(2,1)S(1)} fusion(bf16[6,3,2,7,2,128]{5,2,4,3,1,0:T(2,128)(2,1)S(1)} %slice.51, bf16[6,3,2,8,18,128]{5,2,4,3,1,0:T(2,128)(2,1)S(1)} %bitcast.80), kind=kLoop, calls=%fused_computation.17 | loop fusion | flops 4423680 | bytes 2930688 | tf_op jit(solution)/shard_map/conv_general_dilated | solution.py:52
  101.7 0.7 fusion.35
  102.4 0.1 copy.104
  102.7 0.7 copy.105
  (49 shorter events, 1.2 us)
Async XLA Ops:
  0.0 101.7 %copy-start = (bf16[3,3,3,128,256]{4,3,2,1,0:T(8,128)(2,1)S(1)}, bf16[3,3,3,128,256]{4,3,2,1,0:T(8,128)(2,1)}, u32[]{:S(2)}) copy-start(bf16[3,3,3,128,256]{4,3,2,1,0:T(8,128)(2,1)} %param.20) | copy-start | bytes 5308420
  0.0 6.4 %copy-start.6 = (s32[2]{0:T(128)S(1)}, s32[2]{0:T(128)}, u32[]{:S(2)}) copy-start(s32[2]{0:T(128)} %param.12) | copy-start | bytes 28
  3.0 12.0 %collective-permute-start = (bf16[2,2,2,128,128]{4,3,2,1,0:T(8,128)(2,1)S(1)}, bf16[2,2,2,128,128]{4,3,2,1,0:T(8,128)(2,1)S(1)}, u32[]{:S(2)}, u32[]{:S(2)}) collective-permute-start(bf16[2,2,2,128,128]{4,3,2,1,0:T(8,128)(2,1)S(1)} %slice.39), channel_id=1, source_target_pairs={{0,16},{16,32},{32,48},{48,64},{64,80},{80,96},{96,112},{112,128},... | collective-permute-start | bytes 786440 | tf_op jit(solution)/shard_map/ppermute | solution.py:10
  15.8 10.3 %collective-permute-start.1 = (bf16[2,6,1,128,128]{4,3,2,1,0:T(8,128)(2,1)S(1)}, bf16[2,6,1,128,128]{4,3,2,1,0:T(8,128)(2,1)S(1)}, u32[]{:S(2)}, u32[]{:S(2)}) collective-permute-start(bf16[2,6,1,128,128]{4,3,2,1,0:T(8,128)(2,1)S(1)} %get-tuple-element.7), channel_id=1, source_target_pairs={{0,1},{1,2},{2,3},{3,4},{4,5},{5,6},{6,7},{7,8},{8,9},{9,10},{10,1... | collective-permute-start | bytes 1179656 | tf_op jit(solution)/shard_map/ppermute | solution.py:20
  17.8 10.1 %collective-permute-start.2 = (bf16[2,6,1,128,128]{4,3,2,1,0:T(8,128)(2,1)S(1)}, bf16[2,6,1,128,128]{4,3,2,1,0:T(8,128)(2,1)S(1)}, u32[]{:S(2)}, u32[]{:S(2)}) collective-permute-start(bf16[2,6,1,128,128]{4,3,2,1,0:T(8,128)(2,1)S(1)} %get-tuple-element.8), channel_id=1, source_target_pairs={{1,0},{2,1},{3,2},{4,3},{5,4},{6,5},{7,6},{8,7},{9,8},{10,9},{11,1... | collective-permute-start | bytes 1179656 | tf_op jit(solution)/shard_map/ppermute | solution.py:21
  31.1 1.7 %copy-start.3 = (bf16[3,3,3,128,128]{4,3,2,1,0:T(8,128)(2,1)S(1)}, bf16[3,3,3,128,128]{4,3,2,1,0:T(8,128)(2,1)}, u32[]{:S(2)}) copy-start(bf16[3,3,3,128,128]{4,3,2,1,0:T(8,128)(2,1)} %param.15) | copy-start | bytes 2654212
  31.1 1.7 %copy-start.7 = (f32[128]{0:T(128)S(1)}, f32[128]{0:T(128)}, u32[]{:S(2)}) copy-start(f32[128]{0:T(128)} %param.16) | copy-start | bytes 1540
  31.2 1.7 %copy-start.10 = (pred[16,17]{0,1:T(8,128)(4,1)S(1)}, pred[16,17]{0,1:T(8,128)(4,1)}, u32[]{:S(2)}) copy-start(pred[16,17]{0,1:T(8,128)(4,1)} %constant.41) | copy-start | bytes 820
  37.9 0.7 copy-start.2
  38.9 12.3 %collective-permute-start.3 = (bf16[2,2,2,128,128]{4,3,2,1,0:T(8,128)(2,1)S(1)}, bf16[2,2,2,128,128]{4,3,2,1,0:T(8,128)(2,1)S(1)}, u32[]{:S(2)}, u32[]{:S(2)}) collective-permute-start(bf16[2,2,2,128,128]{4,3,2,1,0:T(8,128)(2,1)S(1)} %slice.45), channel_id=1, source_target_pairs={{0,16},{16,32},{32,48},{48,64},{64,80},{80,96},{96,112},{112,128},... | collective-permute-start | bytes 786440 | tf_op jit(solution)/shard_map/ppermute | solution.py:10
  52.0 10.3 %collective-permute-start.4 = (bf16[2,6,1,128,128]{4,3,2,1,0:T(8,128)(2,1)S(1)}, bf16[2,6,1,128,128]{4,3,2,1,0:T(8,128)(2,1)S(1)}, u32[]{:S(2)}, u32[]{:S(2)}) collective-permute-start(bf16[2,6,1,128,128]{4,3,2,1,0:T(8,128)(2,1)S(1)} %get-tuple-element.5), channel_id=1, source_target_pairs={{0,1},{1,2},{2,3},{3,4},{4,5},{5,6},{6,7},{7,8},{8,9},{9,10},{10,1... | collective-permute-start | bytes 1179656 | tf_op jit(solution)/shard_map/ppermute | solution.py:20
  53.9 10.1 %collective-permute-start.5 = (bf16[2,6,1,128,128]{4,3,2,1,0:T(8,128)(2,1)S(1)}, bf16[2,6,1,128,128]{4,3,2,1,0:T(8,128)(2,1)S(1)}, u32[]{:S(2)}, u32[]{:S(2)}) collective-permute-start(bf16[2,6,1,128,128]{4,3,2,1,0:T(8,128)(2,1)S(1)} %get-tuple-element.6), channel_id=1, source_target_pairs={{1,0},{2,1},{3,2},{4,3},{5,4},{6,5},{7,6},{8,7},{9,8},{10,9},{11,1... | collective-permute-start | bytes 1179656 | tf_op jit(solution)/shard_map/ppermute | solution.py:21
  67.3 1.7 %copy-start.4 = (bf16[3,3,3,128,128]{4,3,2,1,0:T(8,128)(2,1)S(1)}, bf16[3,3,3,128,128]{4,3,2,1,0:T(8,128)(2,1)}, u32[]{:S(2)}) copy-start(bf16[3,3,3,128,128]{4,3,2,1,0:T(8,128)(2,1)} %param.18) | copy-start | bytes 2654212
  67.3 1.7 %copy-start.8 = (f32[128]{0:T(128)S(1)}, f32[128]{0:T(128)}, u32[]{:S(2)}) copy-start(f32[128]{0:T(128)} %param.19) | copy-start | bytes 1540
  73.9 1.0 %copy-start.1 = (bf16[2,4,2,128,128]{4,3,2,1,0:T(8,128)(2,1)S(1)}, bf16[2,4,2,128,128]{4,3,2,1,0:T(8,128)(2,1)}, u32[]{:S(2)}) copy-start(bf16[2,4,2,128,128]{4,3,2,1,0:T(8,128)(2,1)} %param.11) | copy-start | bytes 1572868
  75.1 11.6 %collective-permute-start.6 = (bf16[2,2,2,128,128]{4,3,2,1,0:T(8,128)(2,1)S(1)}, bf16[2,2,2,128,128]{4,3,2,1,0:T(8,128)(2,1)S(1)}, u32[]{:S(2)}, u32[]{:S(2)}) collective-permute-start(bf16[2,2,2,128,128]{4,3,2,1,0:T(8,128)(2,1)S(1)} %slice.50), channel_id=1, source_target_pairs={{0,16},{16,32},{32,48},{48,64},{64,80},{80,96},{96,112},{112,128},... | collective-permute-start | bytes 786440 | tf_op jit(solution)/shard_map/ppermute | solution.py:10
  86.8 2.8 %copy-start.9 = (s32[2]{0:T(128)S(1)}, s32[2]{0:T(128)}, u32[]{:S(2)}) copy-start(s32[2]{0:T(128)} %param.13) | copy-start | bytes 28
  87.5 10.3 %collective-permute-start.7 = (bf16[2,6,1,128,128]{4,3,2,1,0:T(8,128)(2,1)S(1)}, bf16[2,6,1,128,128]{4,3,2,1,0:T(8,128)(2,1)S(1)}, u32[]{:S(2)}, u32[]{:S(2)}) collective-permute-start(bf16[2,6,1,128,128]{4,3,2,1,0:T(8,128)(2,1)S(1)} %pad_maximum_fusion.3), channel_id=1, source_target_pairs={{0,1},{1,2},{2,3},{3,4},{4,5},{5,6},{6,7},{7,8},{8,9},{9,10},{10,1... | collective-permute-start | bytes 1179656 | tf_op jit(solution)/shard_map/ppermute | solution.py:10
  100.2 1.5 %copy-start.5 = (f32[256]{0:T(256)S(1)}, f32[256]{0:T(256)}, u32[]{:S(2)}) copy-start(f32[256]{0:T(256)} %param.21) | copy-start | bytes 3076
  100.2 1.5 %copy-start.11 = (pred[16,9]{0,1:T(8,128)(4,1)S(1)}, pred[16,9]{0,1:T(8,128)(4,1)}, u32[]{:S(2)}) copy-start(pred[16,9]{0,1:T(8,128)(4,1)} %constant.40) | copy-start | bytes 436
where the time goes:
time: 104 us; the launch traced here: 103 us
  waiting for transfers between devices  46.9 us (45%)
  starting transfers between devices  23.1 us (22%)
  local copies, waits for them, and re-layouts  12.5 us (12%)
  matrix products  11.1 us (11%)
  other arithmetic  9.13 us (9%)
    ppermute x4, waiting for transfers between devices, shifted(): return lax.ppermute(block, axis, route)  36.6 us
    ppermute x2, starting transfers between devices, padded(): after = lax.ppermute(initial, axis, down)  9.89 us
    conv_general_dilated x3, matrix products, run_conv(): lax.conv_general_dilated(extended, weight, strides, pad, dimension_number...  9.44 us
    ppermute x4, starting transfers between devices, shifted(): return lax.ppermute(block, axis, route)  9.38 us
    ppermute x2, waiting for transfers between devices, padded(): before = lax.ppermute(last, axis, up)  6.85 us
    unnamed x28, local copies, waits for them, and re-layouts  5.92 us
    conv_general_dilated x3, other arithmetic, run_conv(): lax.conv_general_dilated(extended, weight, strides, pad, dimension_number...  4.72 us
    ppermute x2, starting transfers between devices, padded(): before = lax.ppermute(last, axis, up)  3.84 us
  transfers between devices with their start and end apart: 8, of which 8 were waited for; matrix products, arithmetic and copies ran while one was open for 0% of the time, Pallas kernels for 0%

commit v1 on v0

v1 whole, which is shorter than its diff:
```python
import functools

import jax
import jax.numpy as jnp
from jax import lax
from jax.experimental import pallas as pl
from jax.experimental.pallas import tpu as pltpu
from jax.sharding import PartitionSpec as P

F32 = jnp.float32
BF16 = jnp.bfloat16
VMEM_LIMIT = 56 * 2**20


def activate(values, gain):
    values = values.astype(F32)
    mean = jnp.mean(values * values, axis=-1, keepdims=True)
    scaled = values * lax.rsqrt(mean + 1e-06) * gain
    return scaled / (1.0 + jnp.exp(-scaled))


def first_kernel(meta, video, gain, act, tail):
    for slot in range(2):
        for frame in range(4):
            act[slot, frame] = activate(video[slot, frame], gain[...]).astype(BF16)
    last = meta[2]
    tail[...] = act[last]


def pair_weight(weight, wide):
    zero = jnp.zeros((128, 128), BF16)
    for kt in range(3):
        for j in range(4):
            rows = pl.ds((kt * 4 + j) * 128, 128)
            for kw in range(3):
                for r in range(2):
                    kh = j - r
                    inside = 0 <= kh <= 2
                    wide[rows, pl.ds((kw * 2 + r) * 128, 128)] = weight[kt, kh, kw] if inside else zero


def pair_conv(source, wide, frame, count, row):
    m = count * 128
    pieces = [
        source[pl.ds(frame + kt, count), row + j].reshape(m, 128) for kt in range(3) for j in range(4)
    ]
    z = jnp.dot(jnp.concatenate(pieces, axis=1), wide[...], preferred_element_type=F32)
    left = z[:, :256].reshape(count, 128, 256)
    right = z[:, 512:].reshape(count, 128, 256)
    edge = jnp.zeros((count, 1, 256), F32)
    left = jnp.concatenate([edge, left[:, :127]], axis=1)
    right = jnp.concatenate([right[:, 1:], edge], axis=1)
    return left.reshape(m, 256) + z[:, 256:512] + right.reshape(m, 256)


def main_kernel(
    meta, own, pin, cross, pown, ppin, pcross, video, w_one, bias_one, gain_two, w_two, bias_two, w_down, bias_down,
    out, below, sent,
    ux, u2, wide, ys, total, lower,
):
    has_a, has_b, last, parity, top, bottom = (meta[i] for i in range(6))
    keep_a, keep_b = has_a > 0, has_b > 0

    def assemble(near_above, near_below, p_above, p_below):
        for k, src in ((0, p_above), (2, pown), (4, p_below)):
            for f in range(4):
                v = src[f]
                ux[f, k : k + 2] = jnp.where(keep_a, v, jnp.zeros_like(v))
        for k, src in ((0, near_above), (2, own), (4, near_below)):
            ux[4:8, k : k + 2] = src[0]
            ux[10:14, k : k + 2] = src[1]
            for f in range(2):
                v = src[0, 2 + f]
                ux[8 + f, k : k + 2] = jnp.where(keep_b, v, jnp.zeros_like(v))

    @pl.when(parity == 0)
    def _():
        assemble(cross, pin, pcross, ppin)

    @pl.when(parity != 0)
    def _():
        assemble(pin, cross, ppin, pcross)

    pair_weight(w_one, wide)
    for source, count, target in ((0, 2, 0), (2, 2, 2), (4, 2, 4), (8, 2, 8), (10, 2, 10)):
        for row in (0, 2):
            h = pair_conv(ux, wide, source, count, row)
            for r in range(2):
                v = activate(h[:, r * 128 : r * 128 + 128] + bias_one[...], gain_two[...])
                local = row + r
                if local == 0:
                    v = jnp.where(top > 0, jnp.zeros_like(v), v)
                if local == 3:
                    v = jnp.where(bottom > 0, jnp.zeros_like(v), v)
                if target == 0:
                    v = jnp.where(keep_a, v, jnp.zeros_like(v))
                v = v.astype(BF16).reshape(count, 128, 128)
                u2[target : target + 2, local] = v
                if target == 4:
                    u2[6:8, local] = jnp.where(keep_b, v, jnp.zeros_like(v))
    pair_weight(w_two, wide)
    ys[:, :, :8] = jnp.zeros((8, 2, 8, 128), F32)
    for slot in range(2):
        for half in range(2):
            h = pair_conv(u2, wide, 6 * slot + 2 * half, 2, 0)
            for r in range(2):
                v = h[:, r * 128 : r * 128 + 128] + bias_two[...]
                y = video[slot, 2 * half : 2 * half + 2, r].reshape(256, 128).astype(F32) + v
                y = y.astype(BF16).astype(F32).reshape(2, 128, 128)
                ys[4 * slot + 2 * half : 4 * slot + 2 * half + 2, r, 8:] = y

    def columns(slot, frame, r):
        at = 4 * slot + frame
        return jnp.concatenate(
            [ys[at, r, pl.ds(7 + kw, 64, stride=2)].astype(BF16) for kw in range(3)], axis=1
        )

    def gather(frames, r):
        return jnp.concatenate([columns(slot, f, r) for slot in range(2) for f in frames], axis=0)

    sums = {}
    for kt, frames, goes in ((0, (0, 2), (1, 2)), (1, (1, 3), (1, 2)), (2, (0, 2), (0, 1))):
        upper, under = gather(frames, 0), gather(frames, 1)
        here = jnp.dot(
            jnp.concatenate([upper, under], axis=1), w_down[kt, 384:], preferred_element_type=F32
        )
        next_band = jnp.dot(under, w_down[kt, :384], preferred_element_type=F32)
        for slot in range(2):
            for i, t in enumerate(goes):
                part = slice((slot * 2 + i) * 64, (slot * 2 + i) * 64 + 64)
                for name, value in (("here", here), ("next", next_band)):
                    key = (name, slot, t)
                    sums[key] = sums[key] + value[part] if key in sums else value[part]
    zero = jnp.zeros((64, 256), F32)
    sums["here", 1, 0] += jnp.where(keep_b, sums["here", 0, 2], zero)
    sums["next", 1, 0] += jnp.where(keep_b, sums["next", 0, 2], zero)
    for slot in range(2):
        for t in range(2):
            out[slot, t] = sums["here", slot, t] + bias_down[...]
            below[slot, t] = sums["next", slot, t].astype(BF16)
    sent[0] = jnp.where(last > 0, sums["here", 1, 2], sums["here", 0, 2]).astype(BF16)
    sent[1] = jnp.where(last > 0, sums["next", 1, 2], sums["next", 0, 2]).astype(BF16)


def call(kernel, outs, scratch, n_in, flops):
    vmem = pl.BlockSpec(memory_space=pltpu.VMEM)
    return pl.pallas_call(
        kernel,
        out_shape=[jax.ShapeDtypeStruct(shape, dtype) for shape, dtype in outs],
        in_specs=[pl.BlockSpec(memory_space=pltpu.SMEM)] + [vmem] * n_in,
        out_specs=[vmem] * len(outs),
        scratch_shapes=scratch,
        compiler_params=pltpu.CompilerParams(vmem_limit_bytes=VMEM_LIMIT),
        cost_estimate=pl.CostEstimate(flops=flops, bytes_accessed=2**20, transcendentals=0),
    )


def local(
    video, pred_slot, frames, gain_one, conv_one, bias_one, gain_two, conv_two, bias_two, down_weight, down_bias
):
    n_block, n_space = lax.axis_size("block"), lax.axis_size("space")
    space = lax.axis_index("space")
    has = (pred_slot >= 0).astype(jnp.int32)
    last = (frames[1] > 0).astype(jnp.int32)
    meta = jnp.stack(
        [has[0], has[1], last, space % 2, (space == 0).astype(jnp.int32), (space == n_space - 1).astype(jnp.int32)]
    )
    band = video.shape
    act, tail = call(first_kernel, [(band, BF16), (band[1:], BF16)], [], 2, 10**6)(
        meta, video, gain_one.reshape(1, 128)
    )
    inner = [(i, i ^ 1) for i in range(n_space)]
    outer = [(i, j) for i in range(n_space) if 0 <= (j := i + 1 if i % 2 else i - 1) < n_space]
    onward = [(b, b + 1) for b in range(n_block - 1)]
    corner = [(b * n_space + i, (b + 1) * n_space + j) for b in range(n_block - 1) for i, j in outer]
    pin = lax.ppermute(act, "space", inner)
    cross = lax.ppermute(act, "space", outer)
    pown = lax.ppermute(tail, "block", onward)
    pcross = lax.ppermute(tail, ("block", "space"), corner)
    ppin = lax.ppermute(pown, "space", inner)
    out, below, sent = call(
        main_kernel,
        [((2, 2, 64, 256), F32), ((2, 2, 64, 256), BF16), ((2, 64, 256), BF16)],
        [
            pltpu.VMEM((14, 6, 128, 128), BF16),
            pltpu.VMEM((12, 4, 128, 128), BF16),
            pltpu.VMEM((1536, 768), BF16),
            pltpu.VMEM((8, 2, 136, 128), F32),
            pltpu.VMEM((8, 128), F32),
            pltpu.VMEM((8, 128), F32),
        ],
        14,
        10**10,
    )(
        meta, act, pin, cross, pown, ppin, pcross, video,
        conv_one, bias_one.reshape(1, 128), gain_two.reshape(1, 128), conv_two, bias_two.reshape(1, 128),
        down_weight.reshape(3, 1152, 256), down_bias.reshape(1, 256),
    )
    got = lax.ppermute(sent, "block", onward)
    got = jnp.where(has[0] > 0, got.astype(F32), 0.0)
    first = jnp.pad(got[:, None, None], ((0, 0), (0, 1), (0, 1), (0, 0), (0, 0)))
    below = (below.astype(F32) + first[1]).astype(BF16)
    above = lax.ppermute(below, "space", [(i, i + 1) for i in range(n_space - 1)])
    down = out + above.astype(F32) + first[0]
    keep = (2 * jnp.arange(2, dtype=jnp.int32))[None, :] < frames[:, None]
    down = jnp.where(keep[:, :, None, None], down, 0.0)
    return down.astype(BF16)[:, :, None]


def solution(mesh):
    return jax.shard_map(
        local,
        mesh=mesh,
        in_specs=(P("block", None, "space", None, None), P("block"), P("block")) + (P(),) * 8,
        out_specs=P("block", None, "space", None, None),
        check_vma=False,
    )
```

time: 104 us -> 61.9 us (0.60)
  waiting for transfers between devices: 46.9 us -> 23.2 us
  Pallas kernels: 0 us -> 16.3 us
  matrix products: 11.1 us -> 0 us
  local copies, waits for them, and re-layouts: 12.5 us -> 2.96 us
  starting transfers between devices: 23.1 us -> 15 us
  other arithmetic: 9.13 us -> 3.36 us
    ppermute x8 -> x7, waiting for transfers between devices: 46.9 us -> 23.2 us  [the longest x1 10.1 us: local(): pcross = lax.ppermute(tail, ('block', 'space'), corner)]
    pallas_call x0 -> x2, Pallas kernels: none -> 16.3 us  [the longest x1 13.8 us: local(): call(main_kernel, [((2, 2, 64, 256), F32), ((2, 2, 64, 256), BF16), ((2,...]
    conv_general_dilated x3 -> x0, matrix products: 9.44 us -> none  [run_conv(): lax.conv_general_dilated(extended, weight, strides, pad, dimension_number...]
    ppermute x8 -> x7, starting transfers between devices: 23.1 us -> 15 us  [the longest x1 5.59 us: local(): pcross = lax.ppermute(tail, ('block', 'space'), corner)]
    unnamed x28 -> x12, local copies, waits for them, and re-layouts: 5.92 us -> 1.13 us
    conv_general_dilated x3 -> x0, other arithmetic: 4.72 us -> none  [run_conv(): lax.conv_general_dilated(extended, weight, strides, pad, dimension_number...]
    concatenate x3 -> x0, local copies, waits for them, and re-layouts: 3.58 us -> none  [the longest x2 2.56 us: padded(): x = jnp.concatenate([before, x, after], axis=dim)]
    broadcast_in_dim x0 -> x2, other arithmetic: none -> 1.7 us  [the longest x1 1.69 us: local(): return down.astype(BF16)[:, :, None]]
  transfers between devices with their start and end apart: 8 -> 7, of which waited for: 8 -> 4; matrix products, arithmetic and copies ran while one was open for 0% -> 0% of each run, Pallas kernels for 0% -> 0%
where the time goes in v1:
time: 61.9 us; the launch traced here: 61.6 us
  waiting for transfers between devices  23.2 us (37%)
  Pallas kernels  16.3 us (26%)
  starting transfers between devices  15 us (24%)
  other arithmetic  3.36 us (5%)
  local copies, waits for them, and re-layouts  2.96 us (5%)
  between operations  0.82 us (1%)
    pallas_call x1, Pallas kernels, local(): call(main_kernel, [((2, 2, 64, 256), F32), ((2, 2, 64, 256), BF16), ((2,...  13.8 us
    ppermute x1, waiting for transfers between devices, local(): pcross = lax.ppermute(tail, ('block', 'space'), corner)  10.1 us
    ppermute x1, waiting for transfers between devices, local(): got = lax.ppermute(sent, 'block', onward)  6.54 us
    ppermute x1, starting transfers between devices, local(): pcross = lax.ppermute(tail, ('block', 'space'), corner)  5.59 us
    ppermute x1, waiting for transfers between devices, local(): lax.ppermute(below, 'space', [(i, i + 1) for i in range(n_space - 1)])  5.48 us
    ppermute x1, starting transfers between devices, local(): pown = lax.ppermute(tail, 'block', onward)  3.39 us
    pallas_call x1, Pallas kernels, local(): call(first_kernel, [(band, BF16), (band[1:], BF16)], [], 2, 10 ** 6)  2.5 us
    ppermute x1, starting transfers between devices, local(): cross = lax.ppermute(act, 'space', outer)  2.11 us
  transfers between devices with their start and end apart: 7, of which 4 were waited for; matrix products, arithmetic and copies ran while one was open for 0% of the time, Pallas kernels for 0%

profile of v1, /device:TPU:136, one launch (start us, length us, event | category | flops | bytes accessed | tf_op | source)
XLA Modules:
  0.0 61.6 jit_solution(10422302976733875292)
XLA Ops:
  0.0 0.7 %compare_convert_fusion = s32[2]{0:T(128)S(1)} fusion(s32[2]{0:T(128)} %param.12), kind=kLoop, calls=%fused_computation.11 | loop fusion | flops 4 | bytes 16 | tf_op jit(solution)/shard_map/convert_element_type | solution.py:163
  0.7 1.2 %slice.15 = s32[1]{0:T(128)} slice(s32[2]{0:T(128)} %param.13), slice={[1:2]} | slice | bytes 8 | tf_op jit(solution)/shard_map/slice | solution.py:164
  2.6 0.6 stack.24.meta
  3.1 2.5 %shard_map.109 = (bf16[2,4,2,128,128]{4,3,2,1,0:T(8,128)(2,1)}, bf16[4,2,128,128]{3,2,1,0:T(8,128)(2,1)}) custom-call(s32[6]{0:T(128)} %stack.24.meta, bf16[2,4,2,128,128]{4,3,2,1,0:T(8,128)(2,1)} %video.3, f32[1,128]{1,0:T(1,128)} %bitcast.36), custom_call_target="tpu_custom_call" | custom-call | flops 1000000 | bytes 1048576 | tf_op jit(solution)/shard_map/pallas_call | solution.py:169
  5.6 3.4 %collective-permute-start.2 = (bf16[4,2,128,128]{3,2,1,0:T(8,128)(2,1)}, bf16[4,2,128,128]{3,2,1,0:T(8,128)(2,1)S(1)}, u32[]{:S(2)}, u32[]{:S(2)}) collective-permute-start(bf16[4,2,128,128]{3,2,1,0:T(8,128)(2,1)} %get-tuple-element.11), channel_id=1, source_target_pairs={{0,16},{16,32},{32,48},{48,64},{64,80},{80,96},{96,112},{112,128},... | collective-permute-start | bytes 786440 | tf_op jit(solution)/shard_map/ppermute | solution.py:178
  9.0 0.1 collective-permute-start
  9.1 2.1 %collective-permute-start.1 = (bf16[2,4,2,128,128]{4,3,2,1,0:T(8,128)(2,1)}, bf16[2,4,2,128,128]{4,3,2,1,0:T(8,128)(2,1)S(1)}, u32[]{:S(2)}, u32[]{:S(2)}) collective-permute-start(bf16[2,4,2,128,128]{4,3,2,1,0:T(8,128)(2,1)} %get-tuple-element.10.own), channel_id=1, source_target_pairs={{1,2},{2,1},{3,4},{4,3},{5,6},{6,5},{7,8},{8,7},{9,10},{10,9},{11,... | collective-permute-start | bytes 1572872 | tf_op jit(solution)/shard_map/ppermute | solution.py:177
  11.3 5.6 %collective-permute-start.4 = (bf16[4,2,128,128]{3,2,1,0:T(8,128)(2,1)}, bf16[4,2,128,128]{3,2,1,0:T(8,128)(2,1)S(1)}, u32[]{:S(2)}, u32[]{:S(2)}) collective-permute-start(bf16[4,2,128,128]{3,2,1,0:T(8,128)(2,1)} %get-tuple-element.11), channel_id=1, source_target_pairs={{1,18},{2,17},{3,20},{4,19},{5,22},{6,21},{7,24},{8,23},{9,26},{10... | collective-permute-start | bytes 786440 | tf_op jit(solution)/shard_map/ppermute | solution.py:179
  16.9 1.0 %collective-permute-done.2.pown = bf16[4,2,128,128]{3,2,1,0:T(8,128)(2,1)S(1)} collective-permute-done((bf16[4,2,128,128]{3,2,1,0:T(8,128)(2,1)}, bf16[4,2,128,128]{3,2,1,0:T(8,128)(2,1)S(1)}, u32[]{:S(2)}, u32[]{:S(2)}) %collective-permute-start.2) | collective-permute-done | bytes 262176 | tf_op jit(solution)/shard_map/ppermute | solution.py:178
  17.9 0.0 copy-start.2
  17.9 0.0 collective-permute-start.3
  17.9 10.1 %collective-permute-done.4.pcross = bf16[4,2,128,128]{3,2,1,0:T(8,128)(2,1)S(1)} collective-permute-done((bf16[4,2,128,128]{3,2,1,0:T(8,128)(2,1)}, bf16[4,2,128,128]{3,2,1,0:T(8,128)(2,1)S(1)}, u32[]{:S(2)}, u32[]{:S(2)}) %collective-permute-start.4) | collective-permute-done | bytes 262176 | tf_op jit(solution)/shard_map/ppermute | solution.py:179
  28.1 0.0 copy-start.3
  28.1 0.0 collective-permute-done.3.ppin
  28.1 0.0 copy-start.4
  28.1 0.0 collective-permute-done.pin
  28.1 0.0 copy-start
  28.1 0.0 collective-permute-done.1.cross
  28.1 0.0 copy-start.1
  28.1 0.0 copy-done.2
  28.1 0.7 %copy-done.3 = bf16[4,2,128,128]{3,2,1,0:T(8,128)(2,1)} copy-done((bf16[4,2,128,128]{3,2,1,0:T(8,128)(2,1)}, bf16[4,2,128,128]{3,2,1,0:T(8,128)(2,1)S(1)}, u32[]{:S(2)}) %copy-start.3) | copy-done | bytes 262168
  28.8 0.1 copy-done.4
  28.9 0.2 copy-done
  29.1 0.2 copy-done.1
  29.2 0.0 copy-start.5
  29.2 13.8 %shard_map.110 = (f32[2,2,64,256]{3,2,1,0:T(8,128)}, bf16[2,2,64,256]{3,2,1,0:T(8,128)(2,1)}, bf16[2,64,256]{2,1,0:T(8,128)(2,1)}) custom-call(s32[6]{0:T(128)} %stack.24.meta, bf16[2,4,2,128,128]{4,3,2,1,0:T(8,128)(2,1)} %get-tuple-element.10.own, bf16[2,4,2,128,128]{4,3,2,1,0:T(8,128)(2,1)} %copy-done, bf16[2,4,2,128,128]{4,3,2,1,0:T(8,128)(2,1)} %copy-done.1, ...), custom_call_target="tpu_custom_call" | custom-call | flops 10000000000 | bytes 1048576 | tf_op jit(solution)/shard_map/pallas_call | solution.py:181
  43.0 1.9 %collective-permute-start.5 = (bf16[2,64,256]{2,1,0:T(8,128)(2,1)}, bf16[2,64,256]{2,1,0:T(8,128)(2,1)S(1)}, u32[]{:S(2)}, u32[]{:S(2)}) collective-permute-start(bf16[2,64,256]{2,1,0:T(8,128)(2,1)} %get-tuple-element.14), channel_id=1, source_target_pairs={{0,16},{16,32},{32,48},{48,64},{64,80},{80,96},{96,112},{112,128},... | collective-permute-start | bytes 196616 | tf_op jit(solution)/shard_map/ppermute | solution.py:199
  44.9 6.5 %collective-permute-done.5 = bf16[2,64,256]{2,1,0:T(8,128)(2,1)S(1)} collective-permute-done((bf16[2,64,256]{2,1,0:T(8,128)(2,1)}, bf16[2,64,256]{2,1,0:T(8,128)(2,1)S(1)}, u32[]{:S(2)}, u32[]{:S(2)}) %collective-permute-start.5) | collective-permute-done | bytes 65568 | tf_op jit(solution)/shard_map/ppermute | solution.py:199
  51.5 0.9 %fusion.2 = bf16[2,2,64,256]{3,2,1,0:T(8,128)(2,1)S(1)} fusion(f32[2,1,1,64,256]{4,3,0,2,1:T(8,128)S(1)} %select_bitcast_fusion, bf16[2,2,64,256]{3,2,1,0:T(8,128)(2,1)} %get-tuple-element.13), kind=kLoop, calls=%fused_computation.4 | loop fusion | flops 196608 | bytes 393216 | tf_op jit(solution)/shard_map/convert_element_type | solution.py:202
  52.4 1.9 %collective-permute-start.6 = (bf16[2,2,64,256]{3,2,1,0:T(8,128)(2,1)S(1)}, bf16[2,2,64,256]{3,2,1,0:T(8,128)(2,1)S(1)}, u32[]{:S(2)}, u32[]{:S(2)}) collective-permute-start(bf16[2,2,64,256]{3,2,1,0:T(8,128)(2,1)S(1)} %fusion.2), channel_id=1, source_target_pairs={{0,1},{1,2},{2,3},{3,4},{4,5},{5,6},{6,7},{7,8},{8,9},{9,10},{10,1... | collective-permute-start | bytes 393224 | tf_op jit(solution)/shard_map/ppermute | solution.py:203
  54.3 0.0 copy-done.5
  54.4 0.1 broadcast_compare_fusion
  54.4 5.5 %collective-permute-done.6 = bf16[2,2,64,256]{3,2,1,0:T(8,128)(2,1)S(1)} collective-permute-done((bf16[2,2,64,256]{3,2,1,0:T(8,128)(2,1)S(1)}, bf16[2,2,64,256]{3,2,1,0:T(8,128)(2,1)S(1)}, u32[]{:S(2)}, u32[]{:S(2)}) %collective-permute-start.6) | collective-permute-done | bytes 131104 | tf_op jit(solution)/shard_map/ppermute | solution.py:203
  59.9 1.7 %fusion.7 = bf16[2,2,1,64,256]{4,3,2,1,0:T(8,128)(2,1)} fusion(f32[2,1,1,64,256]{4,3,0,2,1:T(8,128)S(1)} %select_bitcast_fusion, f32[2,2,64,256]{3,2,1,0:T(8,128)} %get-tuple-element.12, bf16[2,2,64,256]{3,2,1,0:T(8,128)(2,1)S(1)} %collective-permute-done.6, pred[2,2]{1,0:T(4,128)(4,1)S(1)} %broadcast_compare_fusion), kind=kLoop, calls=%fused_computation.9 | loop fusion | flops 327680 | bytes 655364 | tf_op jit(solution)/shard_map/broadcast_in_dim | solution.py:207
  (2 shorter events, 0.0 us)
Async XLA Ops:
  5.6 12.2 %collective-permute-start.2 = (bf16[4,2,128,128]{3,2,1,0:T(8,128)(2,1)}, bf16[4,2,128,128]{3,2,1,0:T(8,128)(2,1)S(1)}, u32[]{:S(2)}, u32[]{:S(2)}) collective-permute-start(bf16[4,2,128,128]{3,2,1,0:T(8,128)(2,1)} %get-tuple-element.11), channel_id=1, source_target_pairs={{0,16},{16,32},{32,48},{48,64},{64,80},{80,96},{96,112},{112,128},... | collective-permute-start | bytes 786440 | tf_op jit(solution)/shard_map/ppermute | solution.py:178
  9.0 19.0 %collective-permute-start = (bf16[2,4,2,128,128]{4,3,2,1,0:T(8,128)(2,1)}, bf16[2,4,2,128,128]{4,3,2,1,0:T(8,128)(2,1)S(1)}, u32[]{:S(2)}, u32[]{:S(2)}) collective-permute-start(bf16[2,4,2,128,128]{4,3,2,1,0:T(8,128)(2,1)} %get-tuple-element.10.own), channel_id=1, source_target_pairs={{0,1},{1,0},{2,3},{3,2},{4,5},{5,4},{6,7},{7,6},{8,9},{9,8},{10,11... | collective-permute-start | bytes 1572872 | tf_op jit(solution)/shard_map/ppermute | solution.py:176
  9.1 19.0 %collective-permute-start.1 = (bf16[2,4,2,128,128]{4,3,2,1,0:T(8,128)(2,1)}, bf16[2,4,2,128,128]{4,3,2,1,0:T(8,128)(2,1)S(1)}, u32[]{:S(2)}, u32[]{:S(2)}) collective-permute-start(bf16[2,4,2,128,128]{4,3,2,1,0:T(8,128)(2,1)} %get-tuple-element.10.own), channel_id=1, source_target_pairs={{1,2},{2,1},{3,4},{4,3},{5,6},{6,5},{7,8},{8,7},{9,10},{10,9},{11,... | collective-permute-start | bytes 1572872 | tf_op jit(solution)/shard_map/ppermute | solution.py:177
  11.3 16.8 %collective-permute-start.4 = (bf16[4,2,128,128]{3,2,1,0:T(8,128)(2,1)}, bf16[4,2,128,128]{3,2,1,0:T(8,128)(2,1)S(1)}, u32[]{:S(2)}, u32[]{:S(2)}) collective-permute-start(bf16[4,2,128,128]{3,2,1,0:T(8,128)(2,1)} %get-tuple-element.11), channel_id=1, source_target_pairs={{1,18},{2,17},{3,20},{4,19},{5,22},{6,21},{7,24},{8,23},{9,26},{10... | collective-permute-start | bytes 786440 | tf_op jit(solution)/shard_map/ppermute | solution.py:179
  17.9 10.2 %copy-start.2 = (bf16[4,2,128,128]{3,2,1,0:T(8,128)(2,1)}, bf16[4,2,128,128]{3,2,1,0:T(8,128)(2,1)S(1)}, u32[]{:S(2)}) copy-start(bf16[4,2,128,128]{3,2,1,0:T(8,128)(2,1)S(1)} %collective-permute-done.2.pown) | copy-start | bytes 786436
  17.9 10.2 %collective-permute-start.3 = (bf16[4,2,128,128]{3,2,1,0:T(8,128)(2,1)S(1)}, bf16[4,2,128,128]{3,2,1,0:T(8,128)(2,1)S(1)}, u32[]{:S(2)}, u32[]{:S(2)}) collective-permute-start(bf16[4,2,128,128]{3,2,1,0:T(8,128)(2,1)S(1)} %collective-permute-done.2.pown), channel_id=1, source_target_pairs={{0,1},{1,0},{2,3},{3,2},{4,5},{5,4},{6,7},{7,6},{8,9},{9,8},{10,11... | collective-permute-start | bytes 786440 | tf_op jit(solution)/shard_map/ppermute | solution.py:180
  28.1 0.7 %copy-start.3 = (bf16[4,2,128,128]{3,2,1,0:T(8,128)(2,1)}, bf16[4,2,128,128]{3,2,1,0:T(8,128)(2,1)S(1)}, u32[]{:S(2)}) copy-start(bf16[4,2,128,128]{3,2,1,0:T(8,128)(2,1)S(1)} %collective-permute-done.4.pcross) | copy-start | bytes 786436
  28.1 0.8 %copy-start.4 = (bf16[4,2,128,128]{3,2,1,0:T(8,128)(2,1)}, bf16[4,2,128,128]{3,2,1,0:T(8,128)(2,1)S(1)}, u32[]{:S(2)}) copy-start(bf16[4,2,128,128]{3,2,1,0:T(8,128)(2,1)S(1)} %collective-permute-done.3.ppin) | copy-start | bytes 786436
  28.1 1.0 %copy-start = (bf16[2,4,2,128,128]{4,3,2,1,0:T(8,128)(2,1)}, bf16[2,4,2,128,128]{4,3,2,1,0:T(8,128)(2,1)S(1)}, u32[]{:S(2)}) copy-start(bf16[2,4,2,128,128]{4,3,2,1,0:T(8,128)(2,1)S(1)} %collective-permute-done.pin) | copy-start | bytes 1572868
  28.1 1.1 %copy-start.1 = (bf16[2,4,2,128,128]{4,3,2,1,0:T(8,128)(2,1)}, bf16[2,4,2,128,128]{4,3,2,1,0:T(8,128)(2,1)S(1)}, u32[]{:S(2)}) copy-start(bf16[2,4,2,128,128]{4,3,2,1,0:T(8,128)(2,1)S(1)} %collective-permute-done.1.cross) | copy-start | bytes 1572868
  29.2 25.1 %copy-start.5 = (s32[2]{0:T(128)S(1)}, s32[2]{0:T(128)}, u32[]{:S(2)}) copy-start(s32[2]{0:T(128)} %param.13) | copy-start | bytes 28
  43.0 8.5 %collective-permute-start.5 = (bf16[2,64,256]{2,1,0:T(8,128)(2,1)}, bf16[2,64,256]{2,1,0:T(8,128)(2,1)S(1)}, u32[]{:S(2)}, u32[]{:S(2)}) collective-permute-start(bf16[2,64,256]{2,1,0:T(8,128)(2,1)} %get-tuple-element.14), channel_id=1, source_target_pairs={{0,16},{16,32},{32,48},{48,64},{64,80},{80,96},{96,112},{112,128},... | collective-permute-start | bytes 196616 | tf_op jit(solution)/shard_map/ppermute | solution.py:199
  52.4 7.5 %collective-permute-start.6 = (bf16[2,2,64,256]{3,2,1,0:T(8,128)(2,1)S(1)}, bf16[2,2,64,256]{3,2,1,0:T(8,128)(2,1)S(1)}, u32[]{:S(2)}, u32[]{:S(2)}) collective-permute-start(bf16[2,2,64,256]{3,2,1,0:T(8,128)(2,1)S(1)} %fusion.2), channel_id=1, source_target_pairs={{0,1},{1,2},{2,3},{3,4},{4,5},{5,6},{6,7},{7,8},{8,9},{9,10},{10,1... | collective-permute-start | bytes 393224 | tf_op jit(solution)/shard_map/ppermute | solution.py:203

commit v2 on v1

v2 whole, which is shorter than its diff:
```python
import jax
import jax.numpy as jnp
from jax import lax
from jax.experimental import pallas as pl
from jax.experimental.pallas import tpu as pltpu
from jax.sharding import PartitionSpec as P

F32 = jnp.float32
BF16 = jnp.bfloat16
VMEM_LIMIT = 26 * 2**20
OWN = 10**9
SECOND = 10**9


def activate(values, gain):
    values = values.astype(F32)
    mean = jnp.mean(values * values, axis=-1, keepdims=True)
    scaled = values * lax.rsqrt(mean + 1e-06) * gain
    return scaled / (1.0 + jnp.exp(-scaled))


def masked(keep, value):
    return jnp.where(keep, value, jnp.zeros_like(value))


def first_kernel(frames, video, gain, act, tail):
    for slot in range(2):
        for frame in range(4):
            act[slot, frame] = activate(video[slot, frame], gain[...]).astype(BF16)
    tail[...] = act[jnp.where(frames[1] > 0, 1, 0)]


def pair_weight(weight, wide):
    zero = jnp.zeros((128, 128), BF16)
    for kt in range(3):
        for j in range(4):
            rows = pl.ds((kt * 4 + j) * 128, 128)
            for kw in range(3):
                for r in range(2):
                    kh = j - r
                    inside = 0 <= kh <= 2
                    wide[rows, pl.ds((kw * 2 + r) * 128, 128)] = weight[kt, kh, kw] if inside else zero


def weight_kernel(w_one, w_two, wide, wide_two):
    pair_weight(w_one, wide)
    pair_weight(w_two, wide_two)


def pair_conv(source, wide, frame, count, row):
    m = count * 128
    pieces = [
        source[pl.ds(frame + kt, count), row + j].reshape(m, 128) for kt in range(3) for j in range(4)
    ]
    z = jnp.dot(jnp.concatenate(pieces, axis=1), wide[...], preferred_element_type=F32)
    left = z[:, :256].reshape(count, 128, 256)
    right = z[:, 512:].reshape(count, 128, 256)
    edge = jnp.zeros((count, 1, 256), F32)
    left = jnp.concatenate([edge, left[:, :127]], axis=1)
    right = jnp.concatenate([right[:, 1:], edge], axis=1)
    return left.reshape(m, 256) + z[:, 256:512] + right.reshape(m, 256)


def hidden_rows(ux, wide, bias, gain, frame, row):
    space = lax.axis_index("space")
    h = pair_conv(ux, wide, frame, 2, row)
    for r in range(2):
        v = activate(h[:, r * 128 : r * 128 + 128] + bias[...], gain[...])
        if row + r == 0:
            v = masked(space > 0, v)
        if row + r == 3:
            v = masked(space < lax.axis_size("space") - 1, v)
        yield row + r, v.astype(BF16).reshape(2, 128, 128)


def summed_rows(u2, wide, bias, frame, video, slot, first, ys, at):
    h = pair_conv(u2, wide, frame, 2, 0)
    for r in range(2):
        v = h[:, r * 128 : r * 128 + 128] + bias[...]
        y = video[slot, first : first + 2, r].reshape(256, 128).astype(F32) + v
        ys[at : at + 2, r, 8:] = y.astype(BF16).astype(F32).reshape(2, 128, 128)


def strided(ys, w_down):
    def gather(frames, r):
        return jnp.concatenate(
            [
                jnp.concatenate([ys[f, r, pl.ds(7 + kw, 64, stride=2)].astype(BF16) for kw in range(3)], axis=1)
                for f in frames
            ],
            axis=0,
        )

    here, below = {}, {}
    for kt, frames, goes in ((0, (0, 2), (1, 2)), (1, (1, 3), (1, 2)), (2, (0, 2), (0, 1))):
        upper, under = gather(frames, 0), gather(frames, 1)
        parts = (
            (here, jnp.dot(jnp.concatenate([upper, under], axis=1), w_down[kt, 384:], preferred_element_type=F32)),
            (below, jnp.dot(under, w_down[kt, :384], preferred_element_type=F32)),
        )
        for i, t in enumerate(goes):
            for sums, value in parts:
                part = value[i * 64 : i * 64 + 64]
                sums[t] = sums[t] + part if t in sums else part
    return here, below


def fill(ux, first, count, own, above, below, take):
    for k, src in ((0, above), (2, own), (4, below)):
        for f in range(count):
            ux[first + f, k : k + 2] = take(src, f)


def by_parity(body, pin, cross):
    parity = lax.rem(lax.axis_index("space"), 2)

    @pl.when(parity == 0)
    def _():
        body(cross, pin)

    @pl.when(parity != 0)
    def _():
        body(pin, cross)


def own_kernel(pred, own, pin, cross, wide, bias_one, gain_two, u2a, u2b, ux):
    keep = pred[1] >= 0

    def assemble(above, below):
        fill(ux, 0, 4, own, above, below, lambda src, f: src[0, f])
        fill(ux, 4, 2, own, above, below, lambda src, f: masked(keep, src[0, 2 + f]))
        fill(ux, 6, 4, own, above, below, lambda src, f: src[1, f])

    by_parity(assemble, pin, cross)
    for frame, target in ((0, 0), (4, 2), (6, 4)):
        for row in (0, 2):
            for at, v in hidden_rows(ux, wide, bias_one, gain_two, frame, row):
                if target == 0:
                    u2a[:, at] = v
                    v = masked(keep, v)
                u2b[target : target + 2, at] = v


def second_kernel(u2, video, wide_two, bias_two, w_down, bias_down, here_b, below_b, sent_b, ys):
    ys[:, :, :8] = jnp.zeros((4, 2, 8, 128), F32)
    for half in range(2):
        summed_rows(u2, wide_two, bias_two, 2 * half, video, 1, 2 * half, ys, 2 * half)
    here, below = strided(ys, w_down)
    for t in range(2):
        here_b[t] = here[t] + bias_down[...]
        below_b[t] = below[t]
    sent_b[0] = here[2]
    sent_b[1] = below[2]


def rest_kernel(
    pred, frames, own, pin, cross, pown, ppin, pcross, u2a, here_b, below_b, sent_b, video,
    wide, bias_one, gain_two, wide_two, bias_two, w_down, bias_down,
    out, below_out, sent,
    ux, u2, ys,
):
    keep_a, keep_b = pred[0] >= 0, pred[1] >= 0

    def assemble_own(above, below):
        fill(ux, 4, 2, own, above, below, lambda src, f: src[0, f])

    def assemble_before(above, below):
        fill(ux, 0, 4, pown, above, below, lambda src, f: masked(keep_a, src[f]))

    by_parity(assemble_own, pin, cross)
    by_parity(assemble_before, ppin, pcross)
    ys[:, :, :8] = jnp.zeros((4, 2, 8, 128), F32)
    u2[4:6] = u2a[...]
    for frame, target in ((0, 0), (2, 2)):
        for row in (0, 2):
            for at, v in hidden_rows(ux, wide, bias_one, gain_two, frame, row):
                u2[target : target + 2, at] = masked(keep_a, v) if target == 0 else v
    for half in (1, 0):
        summed_rows(u2, wide_two, bias_two, 2 * half, video, 0, 2 * half, ys, 2 * half)
    here, below = strided(ys, w_down)
    for t in range(2):
        out[0, t] = here[t] + bias_down[...]
        below_out[0, t] = below[t]
    out[1, 0] = here_b[0] + masked(keep_b, here[2])
    out[1, 1] = here_b[1]
    below_out[1, 0] = below_b[0] + masked(keep_b, below[2])
    below_out[1, 1] = below_b[1]
    second = frames[1] > 0
    sent[0] = jnp.where(second, sent_b[0], here[2]).astype(BF16)
    sent[1] = jnp.where(second, sent_b[1], below[2]).astype(BF16)


def relay_kernel(pred, got, below, below_out):
    below_out[...] = below[...].astype(BF16)
    below_out[0, 0] = (below[0, 0] + masked(pred[0] >= 0, got[1].astype(F32))).astype(BF16)


def last_kernel(pred, frames, here, got, above, out):
    for slot in range(2):
        for t in range(2):
            v = here[slot, t] + above[slot, t].astype(F32)
            if slot == 0 and t == 0:
                v = v + masked(pred[0] >= 0, got[0].astype(F32))
            out[slot, t, 0] = masked(2 * t < frames[slot], v).astype(BF16)


VMEM = pl.BlockSpec(memory_space=pltpu.VMEM)
SMEM = pl.BlockSpec(memory_space=pltpu.SMEM)


def call(kernel, outs, scratch, scalars, arrays, flops, limit=VMEM_LIMIT):
    return pl.pallas_call(
        kernel,
        out_shape=[jax.ShapeDtypeStruct(shape, dtype) for shape, dtype in outs],
        in_specs=[SMEM] * len(scalars) + [VMEM] * len(arrays),
        out_specs=[VMEM] * len(outs),
        scratch_shapes=scratch,
        compiler_params=pltpu.CompilerParams(vmem_limit_bytes=limit),
        cost_estimate=pl.CostEstimate(flops=flops, bytes_accessed=2**18, transcendentals=0),
    )(*scalars, *arrays)


def local(
    video, pred_slot, frames, gain_one, conv_one, bias_one, gain_two, conv_two, bias_two, down_weight, down_bias
):
    n_block, n_space = lax.axis_size("block"), lax.axis_size("space")
    band = video.shape
    act, tail = call(
        first_kernel, [(band, BF16), (band[1:], BF16)], [], (frames,), (video, gain_one.reshape(1, 128)), 10**9,
        60 * 2**20,
    )
    inner = [(i, i ^ 1) for i in range(n_space)]
    outer = [(i, j) for i in range(n_space) if 0 <= (j := i + 1 if i % 2 else i - 1) < n_space]
    onward = [(b, b + 1) for b in range(n_block - 1)]
    corner = [(b * n_space + i, (b + 1) * n_space + j) for b in range(n_block - 1) for i, j in outer]
    pown = lax.ppermute(tail, "block", onward)
    pin = lax.ppermute(act, "space", inner)
    cross = lax.ppermute(act, "space", outer)
    pcross = lax.ppermute(tail, ("block", "space"), corner)
    wide = ((1536, 768), BF16)
    conv_one, pown = lax.optimization_barrier((conv_one, pown))
    wide_one, wide_two = call(weight_kernel, [wide, wide], [], (), (conv_one, conv_two), 10**10)
    norm = (wide_one, bias_one.reshape(1, 128), gain_two.reshape(1, 128))
    stride = (wide_two, bias_two.reshape(1, 128), down_weight.reshape(3, 1152, 256), down_bias.reshape(1, 256))
    ys = pltpu.VMEM((4, 2, 136, 128), F32)
    one = ((2, 64, 256), F32)
    both = ((2, 2, 64, 256), F32)
    u2a, u2b = call(
        own_kernel, [((2, 4, 128, 128), BF16), ((6, 4, 128, 128), BF16)], [pltpu.VMEM((10, 6, 128, 128), BF16)],
        (pred_slot,), (act, pin, cross, *norm), OWN,
    )
    ppin = lax.ppermute(pown, "space", inner)
    here_b, below_b, sent_b = call(second_kernel, [one, one, one], [ys], (), (u2b, video, *stride), SECOND)
    out, below, sent = call(
        rest_kernel, [both, both, ((2, 64, 256), BF16)],
        [pltpu.VMEM((6, 6, 128, 128), BF16), pltpu.VMEM((6, 4, 128, 128), BF16), ys], (pred_slot, frames),
        (act, pin, cross, pown, ppin, pcross, u2a, here_b, below_b, sent_b, video, *norm, *stride), 5 * 10**9,
    )
    got = lax.ppermute(sent, "block", onward)
    [below] = call(relay_kernel, [(both[0], BF16)], [], (pred_slot,), (got, below), 10**6)
    above = lax.ppermute(below, "space", [(i, i + 1) for i in range(n_space - 1)])
    [down] = call(last_kernel, [((2, 2, 1, 64, 256), BF16)], [], (pred_slot, frames), (out, got, above), 10**6)
    return down


def solution(mesh):
    return jax.shard_map(
        local,
        mesh=mesh,
        in_specs=(P("block", None, "space", None, None), P("block"), P("block")) + (P(),) * 8,
        out_specs=P("block", None, "space", None, None),
        check_vma=False,
    )
```

time: 61.9 us -> 49 us (0.79)
  waiting for transfers between devices: 23.2 us -> 14.1 us
  other arithmetic: 3.36 us -> 0 us
  local copies, waits for them, and re-layouts: 2.96 us -> 0.06 us
  starting transfers between devices: 15 us -> 16.6 us
  Pallas kernels: 16.3 us -> 17.8 us
    ppermute x1, waiting for transfers between devices: 10.1 us -> 0.08 us  [local(): pcross = lax.ppermute(tail, ('block', 'space'), corner)]
    ppermute x1, waiting for transfers between devices: 0.01 us -> 2.62 us  [local(): cross = lax.ppermute(act, 'space', outer)]
    broadcast_in_dim x2 -> x0, other arithmetic: 1.7 us -> none  [the longest x1 1.69 us: local(): return down.astype(BF16)[:, :, None]]
    ppermute x1, waiting for transfers between devices: 6.54 us -> 4.91 us  [local(): got = lax.ppermute(sent, 'block', onward)]
    convert_element_type x2 -> x0, other arithmetic: 1.58 us -> none  [the longest x1 0.92 us: local(): below = (below.astype(F32) + first[1]).astype(BF16)]
    pallas_call x2 -> x7, Pallas kernels: 16.3 us -> 17.8 us  [call(): pl.pallas_call(kernel, out_shape=[jax.ShapeDtypeStruct(shape, dtype) for...]
    ppermute x1, starting transfers between devices: 1.91 us -> 3.36 us  [local(): got = lax.ppermute(sent, 'block', onward)]
    slice x1 -> x0, local copies, waits for them, and re-layouts: 1.24 us -> none  [local(): last = (frames[1] > 0).astype(jnp.int32)]
  transfers between devices with their start and end apart: 7 -> 7, of which waited for: 4 -> 5; matrix products, arithmetic and copies ran while one was open for 0% -> 0% of each run, Pallas kernels for 0% -> 15%
where the time goes in v2:
time: 49 us; the launch traced here: 48.7 us
  Pallas kernels  17.8 us (36%)
  starting transfers between devices  16.6 us (34%)
  waiting for transfers between devices  14.1 us (29%)
    pallas_call x7, Pallas kernels, call(): pl.pallas_call(kernel, out_shape=[jax.ShapeDtypeStruct(shape, dtype) for...  17.8 us
    ppermute x1, starting transfers between devices, local(): pcross = lax.ppermute(tail, ('block', 'space'), corner)  5.73 us
    ppermute x1, waiting for transfers between devices, local(): lax.ppermute(below, 'space', [(i, i + 1) for i in range(n_space - 1)])  5.57 us
    ppermute x1, waiting for transfers between devices, local(): got = lax.ppermute(sent, 'block', onward)  4.91 us
    ppermute x1, starting transfers between devices, local(): got = lax.ppermute(sent, 'block', onward)  3.36 us
    ppermute x1, starting transfers between devices, local(): pown = lax.ppermute(tail, 'block', onward)  3.35 us
    ppermute x1, waiting for transfers between devices, local(): cross = lax.ppermute(act, 'space', outer)  2.62 us
    ppermute x1, starting transfers between devices, local(): cross = lax.ppermute(act, 'space', outer)  2.11 us
  transfers between devices with their start and end apart: 7, of which 5 were waited for; matrix products, arithmetic and copies ran while one was open for 0% of the time, Pallas kernels for 15%

profile of v2, /device:TPU:136, one launch (start us, length us, event | category | flops | bytes accessed | tf_op | source)
XLA Modules:
  0.0 48.7 jit_solution(1581677800123091667)
XLA Ops:
  0.0 0.0 copy-start.9
  0.0 0.0 copy-start.10
  0.0 2.7 %shard_map.109 = (bf16[2,4,2,128,128]{4,3,2,1,0:T(8,128)(2,1)}, bf16[4,2,128,128]{3,2,1,0:T(8,128)(2,1)}) custom-call(s32[2]{0:T(128)} %frames.5, bf16[2,4,2,128,128]{4,3,2,1,0:T(8,128)(2,1)} %video.5, f32[1,128]{1,0:T(1,128)} %bitcast.16), custom_call_target="tpu_custom_call" | custom-call | flops 1000000000 | bytes 262144 | tf_op jit(solution)/shard_map/pallas_call | solution.py:212
  2.7 3.4 %collective-permute-start.2 = (bf16[4,2,128,128]{3,2,1,0:T(8,128)(2,1)}, bf16[4,2,128,128]{3,2,1,0:T(8,128)(2,1)S(1)}, u32[]{:S(2)}, u32[]{:S(2)}) collective-permute-start(bf16[4,2,128,128]{3,2,1,0:T(8,128)(2,1)} %get-tuple-element.20), channel_id=1, source_target_pairs={{0,16},{16,32},{32,48},{48,64},{64,80},{80,96},{96,112},{112,128},... | collective-permute-start | bytes 786440 | tf_op jit(solution)/shard_map/ppermute | solution.py:236
  6.0 0.0 copy-start.2
  6.0 0.0 copy-start.3
  6.1 0.0 copy-start.5
  6.1 0.0 copy-start.6
  6.1 0.1 collective-permute-start
  6.2 2.1 %collective-permute-start.1 = (bf16[2,4,2,128,128]{4,3,2,1,0:T(8,128)(2,1)}, bf16[2,4,2,128,128]{4,3,2,1,0:T(8,128)(2,1)S(1)}, u32[]{:S(2)}, u32[]{:S(2)}) collective-permute-start(bf16[2,4,2,128,128]{4,3,2,1,0:T(8,128)(2,1)} %get-tuple-element.19.own), channel_id=1, source_target_pairs={{1,2},{2,1},{3,4},{4,3},{5,6},{6,5},{7,8},{8,7},{9,10},{10,9},{11,... | collective-permute-start | bytes 1572872 | tf_op jit(solution)/shard_map/ppermute | solution.py:238
  8.3 5.7 %collective-permute-start.4 = (bf16[4,2,128,128]{3,2,1,0:T(8,128)(2,1)}, bf16[4,2,128,128]{3,2,1,0:T(8,128)(2,1)S(1)}, u32[]{:S(2)}, u32[]{:S(2)}) collective-permute-start(bf16[4,2,128,128]{3,2,1,0:T(8,128)(2,1)} %get-tuple-element.20), channel_id=1, source_target_pairs={{1,18},{2,17},{3,20},{4,19},{5,22},{6,21},{7,24},{8,23},{9,26},{10... | collective-permute-start | bytes 786440 | tf_op jit(solution)/shard_map/ppermute | solution.py:239
  14.0 0.9 %collective-permute-done.2.pown = bf16[4,2,128,128]{3,2,1,0:T(8,128)(2,1)S(1)} collective-permute-done((bf16[4,2,128,128]{3,2,1,0:T(8,128)(2,1)}, bf16[4,2,128,128]{3,2,1,0:T(8,128)(2,1)S(1)}, u32[]{:S(2)}, u32[]{:S(2)}) %collective-permute-start.2) | collective-permute-done | bytes 262176 | tf_op jit(solution)/shard_map/ppermute | solution.py:236
  14.9 0.0 collective-permute-start.3
  14.9 0.0 copy-done.9
  14.9 0.0 copy-done.10
  14.9 0.6 %shard_map.110 = (bf16[1536,768]{1,0:T(8,128)(2,1)S(1)}, bf16[1536,768]{1,0:T(8,128)(2,1)S(1)}) custom-call(bf16[3,3,3,128,128]{4,3,2,1,0:T(8,128)(2,1)S(1)} %copy-done.9, bf16[3,3,3,128,128]{4,3,2,1,0:T(8,128)(2,1)S(1)} %copy-done.10), custom_call_target="tpu_custom_call" | custom-call | flops 10000000000 | bytes 262144 | tf_op jit(solution)/shard_map/pallas_call | solution.py:212
  15.5 0.0 copy-start
  15.6 0.0 copy-start.1
  15.6 0.0 copy-start.4
  15.6 0.0 copy-start.7
  15.6 0.0 collective-permute-done.pin
  15.6 2.6 %collective-permute-done.1.cross = bf16[2,4,2,128,128]{4,3,2,1,0:T(8,128)(2,1)S(1)} collective-permute-done((bf16[2,4,2,128,128]{4,3,2,1,0:T(8,128)(2,1)}, bf16[2,4,2,128,128]{4,3,2,1,0:T(8,128)(2,1)S(1)}, u32[]{:S(2)}, u32[]{:S(2)}) %collective-permute-start.1) | collective-permute-done | bytes 524320 | tf_op jit(solution)/shard_map/ppermute | solution.py:238
  18.2 0.0 copy-done.2
  18.2 0.0 copy-done.3
  18.2 0.0 copy-done.5
  18.2 0.0 copy-done.6
  18.3 4.9 %shard_map.111 = (bf16[2,4,128,128]{3,2,1,0:T(8,128)(2,1)S(1)}, bf16[6,4,128,128]{3,2,1,0:T(8,128)(2,1)S(1)}) custom-call(s32[2]{0:T(128)S(1)} %copy-done.3, bf16[2,4,2,128,128]{4,3,2,1,0:T(8,128)(2,1)S(1)} %copy-done.2, bf16[2,4,2,128,128]{4,3,2,1,0:T(8,128)(2,1)S(1)} %collective-permute-done.pin, ...), custom_call_target="tpu_custom_call" | custom-call | flops 1000000000 | bytes 262144 | tf_op jit(solution)/shard_map/pallas_call | solution.py:212
  23.2 0.0 copy-done
  23.2 0.0 copy-done.1
  23.2 0.0 copy-done.4
  23.2 0.0 copy-done.7
  23.2 0.0 copy-start.8
  23.3 1.9 %shard_map.112 = (f32[2,64,256]{2,1,0:T(8,128)S(1)}, f32[2,64,256]{2,1,0:T(8,128)S(1)}, f32[2,64,256]{2,1,0:T(8,128)S(1)}) custom-call(bf16[6,4,128,128]{3,2,1,0:T(8,128)(2,1)S(1)} %get-tuple-element.25.u2, bf16[2,4,2,128,128]{4,3,2,1,0:T(8,128)(2,1)S(1)} %copy-done.1, bf16[1536,768]{1,0:T(8,128)(2,1)S(1)} %get-tuple-element.26.wide_two, ...), custom_call_target="tpu_custom_call" | custom-call | flops 1000000000 | bytes 262144 | tf_op jit(solution)/shard_map/pallas_call | solution.py:212
  25.2 0.1 collective-permute-done.4.pcross
  25.3 0.0 collective-permute-done.3.ppin
  25.3 0.0 copy-done.8
  25.3 5.9 %shard_map.113 = (f32[2,2,64,256]{3,2,1,0:T(8,128)S(1)}, f32[2,2,64,256]{3,2,1,0:T(8,128)S(1)}, bf16[2,64,256]{2,1,0:T(8,128)(2,1)S(1)}) custom-call(s32[2]{0:T(128)S(1)} %copy-done.3, s32[2]{0:T(128)S(1)} %copy-done.8, bf16[2,4,2,128,128]{4,3,2,1,0:T(8,128)(2,1)S(1)} %copy-done.2, bf16[2,4,2,128,128]{4,3,2,1,0:T(8,128)(2,1)S(1)} %collective-permute-done.pin, ...), custom_call_target="tpu_custom_call" | custom-call | flops 5000000000 | bytes 262144 | tf_op jit(solution)/shard_map/pallas_call | solution.py:212
  31.2 3.4 %collective-permute-start.5 = (bf16[2,64,256]{2,1,0:T(8,128)(2,1)S(1)}, bf16[2,64,256]{2,1,0:T(8,128)(2,1)S(1)}, u32[]{:S(2)}, u32[]{:S(2)}) collective-permute-start(bf16[2,64,256]{2,1,0:T(8,128)(2,1)S(1)} %get-tuple-element.31), channel_id=1, source_target_pairs={{0,16},{16,32},{32,48},{48,64},{64,80},{80,96},{96,112},{112,128},... | collective-permute-start | bytes 196616 | tf_op jit(solution)/shard_map/ppermute | solution.py:259
  34.5 4.9 %collective-permute-done.5.got = bf16[2,64,256]{2,1,0:T(8,128)(2,1)S(1)} collective-permute-done((bf16[2,64,256]{2,1,0:T(8,128)(2,1)S(1)}, bf16[2,64,256]{2,1,0:T(8,128)(2,1)S(1)}, u32[]{:S(2)}, u32[]{:S(2)}) %collective-permute-start.5) | collective-permute-done | bytes 65568 | tf_op jit(solution)/shard_map/ppermute | solution.py:259
  39.4 0.6 %shard_map.114 = bf16[2,2,64,256]{3,2,1,0:T(8,128)(2,1)S(1)} custom-call(s32[2]{0:T(128)S(1)} %copy-done.3, bf16[2,64,256]{2,1,0:T(8,128)(2,1)S(1)} %collective-permute-done.5.got, f32[2,2,64,256]{3,2,1,0:T(8,128)S(1)} %get-tuple-element.32.below), custom_call_target="tpu_custom_call" | custom-call | flops 1000000 | bytes 262144 | tf_op jit(solution)/shard_map/pallas_call | solution.py:212
  40.0 1.9 %collective-permute-start.6 = (bf16[2,2,64,256]{3,2,1,0:T(8,128)(2,1)S(1)}, bf16[2,2,64,256]{3,2,1,0:T(8,128)(2,1)S(1)}, u32[]{:S(2)}, u32[]{:S(2)}) collective-permute-start(bf16[2,2,64,256]{3,2,1,0:T(8,128)(2,1)S(1)} %shard_map.114), channel_id=1, source_target_pairs={{0,1},{1,2},{2,3},{3,4},{4,5},{5,6},{6,7},{7,8},{8,9},{9,10},{10,1... | collective-permute-start | bytes 393224 | tf_op jit(solution)/shard_map/ppermute | solution.py:261
  41.9 5.6 %collective-permute-done.6.above = bf16[2,2,64,256]{3,2,1,0:T(8,128)(2,1)S(1)} collective-permute-done((bf16[2,2,64,256]{3,2,1,0:T(8,128)(2,1)S(1)}, bf16[2,2,64,256]{3,2,1,0:T(8,128)(2,1)S(1)}, u32[]{:S(2)}, u32[]{:S(2)}) %collective-permute-start.6) | collective-permute-done | bytes 131104 | tf_op jit(solution)/shard_map/ppermute | solution.py:261
  47.5 1.2 %shard_map.115 = bf16[2,2,1,64,256]{4,3,2,1,0:T(8,128)(2,1)} custom-call(s32[2]{0:T(128)S(1)} %copy-done.3, s32[2]{0:T(128)S(1)} %copy-done.8, f32[2,2,64,256]{3,2,1,0:T(8,128)S(1)} %get-tuple-element.30.here, bf16[2,64,256]{2,1,0:T(8,128)(2,1)S(1)} %collective-permute-done.5.got, bf16[2,2,64,256]{3,2,1,0:T(8,128)(2,1)S(1)} %collective-permute-done.6.above), custom_call_target="tpu_custom_call" | custom-call | flops 1000000 | bytes 262144 | tf_op jit(solution)/shard_map/pallas_call | solution.py:212
Async XLA Ops:
  0.0 14.9 %copy-start.9 = (bf16[3,3,3,128,128]{4,3,2,1,0:T(8,128)(2,1)S(1)}, bf16[3,3,3,128,128]{4,3,2,1,0:T(8,128)(2,1)}, u32[]{:S(2)}) copy-start(bf16[3,3,3,128,128]{4,3,2,1,0:T(8,128)(2,1)} %w_one) | copy-start | bytes 2654212
  0.0 14.9 %copy-start.10 = (bf16[3,3,3,128,128]{4,3,2,1,0:T(8,128)(2,1)S(1)}, bf16[3,3,3,128,128]{4,3,2,1,0:T(8,128)(2,1)}, u32[]{:S(2)}) copy-start(bf16[3,3,3,128,128]{4,3,2,1,0:T(8,128)(2,1)} %w_two.1) | copy-start | bytes 2654212
  2.7 12.2 %collective-permute-start.2 = (bf16[4,2,128,128]{3,2,1,0:T(8,128)(2,1)}, bf16[4,2,128,128]{3,2,1,0:T(8,128)(2,1)S(1)}, u32[]{:S(2)}, u32[]{:S(2)}) collective-permute-start(bf16[4,2,128,128]{3,2,1,0:T(8,128)(2,1)} %get-tuple-element.20), channel_id=1, source_target_pairs={{0,16},{16,32},{32,48},{48,64},{64,80},{80,96},{96,112},{112,128},... | collective-permute-start | bytes 786440 | tf_op jit(solution)/shard_map/ppermute | solution.py:236
  6.0 12.2 %copy-start.2 = (bf16[2,4,2,128,128]{4,3,2,1,0:T(8,128)(2,1)S(1)}, bf16[2,4,2,128,128]{4,3,2,1,0:T(8,128)(2,1)}, u32[]{:S(2)}) copy-start(bf16[2,4,2,128,128]{4,3,2,1,0:T(8,128)(2,1)} %get-tuple-element.19.own) | copy-start | bytes 1572868
  6.0 12.2 %copy-start.3 = (s32[2]{0:T(128)S(1)}, s32[2]{0:T(128)}, u32[]{:S(2)}) copy-start(s32[2]{0:T(128)} %pred_.7) | copy-start | bytes 28
  6.1 12.2 %copy-start.5 = (f32[128]{0:T(128)S(1)}, f32[128]{0:T(128)}, u32[]{:S(2)}) copy-start(f32[128]{0:T(128)} %param.16) | copy-start | bytes 1540
  6.1 12.2 %copy-start.6 = (f32[128]{0:T(128)S(1)}, f32[128]{0:T(128)}, u32[]{:S(2)}) copy-start(f32[128]{0:T(128)} %param.17) | copy-start | bytes 1540
  6.1 9.5 %collective-permute-start = (bf16[2,4,2,128,128]{4,3,2,1,0:T(8,128)(2,1)}, bf16[2,4,2,128,128]{4,3,2,1,0:T(8,128)(2,1)S(1)}, u32[]{:S(2)}, u32[]{:S(2)}) collective-permute-start(bf16[2,4,2,128,128]{4,3,2,1,0:T(8,128)(2,1)} %get-tuple-element.19.own), channel_id=1, source_target_pairs={{0,1},{1,0},{2,3},{3,2},{4,5},{5,4},{6,7},{7,6},{8,9},{9,8},{10,11... | collective-permute-start | bytes 1572872 | tf_op jit(solution)/shard_map/ppermute | solution.py:237
  6.2 12.1 %collective-permute-start.1 = (bf16[2,4,2,128,128]{4,3,2,1,0:T(8,128)(2,1)}, bf16[2,4,2,128,128]{4,3,2,1,0:T(8,128)(2,1)S(1)}, u32[]{:S(2)}, u32[]{:S(2)}) collective-permute-start(bf16[2,4,2,128,128]{4,3,2,1,0:T(8,128)(2,1)} %get-tuple-element.19.own), channel_id=1, source_target_pairs={{1,2},{2,1},{3,4},{4,3},{5,6},{6,5},{7,8},{8,7},{9,10},{10,9},{11,... | collective-permute-start | bytes 1572872 | tf_op jit(solution)/shard_map/ppermute | solution.py:238
  8.3 17.0 %collective-permute-start.4 = (bf16[4,2,128,128]{3,2,1,0:T(8,128)(2,1)}, bf16[4,2,128,128]{3,2,1,0:T(8,128)(2,1)S(1)}, u32[]{:S(2)}, u32[]{:S(2)}) collective-permute-start(bf16[4,2,128,128]{3,2,1,0:T(8,128)(2,1)} %get-tuple-element.20), channel_id=1, source_target_pairs={{1,18},{2,17},{3,20},{4,19},{5,22},{6,21},{7,24},{8,23},{9,26},{10... | collective-permute-start | bytes 786440 | tf_op jit(solution)/shard_map/ppermute | solution.py:239
  14.9 10.4 %collective-permute-start.3 = (bf16[4,2,128,128]{3,2,1,0:T(8,128)(2,1)S(1)}, bf16[4,2,128,128]{3,2,1,0:T(8,128)(2,1)S(1)}, u32[]{:S(2)}, u32[]{:S(2)}) collective-permute-start(bf16[4,2,128,128]{3,2,1,0:T(8,128)(2,1)S(1)} %collective-permute-done.2.pown), channel_id=1, source_target_pairs={{0,1},{1,0},{2,3},{3,2},{4,5},{5,4},{6,7},{7,6},{8,9},{9,8},{10,11... | collective-permute-start | bytes 786440 | tf_op jit(solution)/shard_map/ppermute | solution.py:252
  15.5 7.7 %copy-start = (bf16[3,3,3,128,256]{4,3,2,1,0:T(8,128)(2,1)S(1)}, bf16[3,3,3,128,256]{4,3,2,1,0:T(8,128)(2,1)}, u32[]{:S(2)}) copy-start(bf16[3,3,3,128,256]{4,3,2,1,0:T(8,128)(2,1)} %param.20) | copy-start | bytes 5308420
  15.6 7.7 %copy-start.1 = (bf16[2,4,2,128,128]{4,3,2,1,0:T(8,128)(2,1)S(1)}, bf16[2,4,2,128,128]{4,3,2,1,0:T(8,128)(2,1)}, u32[]{:S(2)}) copy-start(bf16[2,4,2,128,128]{4,3,2,1,0:T(8,128)(2,1)} %video.5) | copy-start | bytes 1572868
  15.6 7.7 %copy-start.4 = (f32[256]{0:T(256)S(1)}, f32[256]{0:T(256)}, u32[]{:S(2)}) copy-start(f32[256]{0:T(256)} %param.21) | copy-start | bytes 3076
  15.6 7.7 %copy-start.7 = (f32[128]{0:T(128)S(1)}, f32[128]{0:T(128)}, u32[]{:S(2)}) copy-start(f32[128]{0:T(128)} %param.19) | copy-start | bytes 1540
  23.2 2.0 %copy-start.8 = (s32[2]{0:T(128)S(1)}, s32[2]{0:T(128)}, u32[]{:S(2)}) copy-start(s32[2]{0:T(128)} %frames.5) | copy-start | bytes 28
  31.2 8.3 %collective-permute-start.5 = (bf16[2,64,256]{2,1,0:T(8,128)(2,1)S(1)}, bf16[2,64,256]{2,1,0:T(8,128)(2,1)S(1)}, u32[]{:S(2)}, u32[]{:S(2)}) collective-permute-start(bf16[2,64,256]{2,1,0:T(8,128)(2,1)S(1)} %get-tuple-element.31), channel_id=1, source_target_pairs={{0,16},{16,32},{32,48},{48,64},{64,80},{80,96},{96,112},{112,128},... | collective-permute-start | bytes 196616 | tf_op jit(solution)/shard_map/ppermute | solution.py:259
  40.0 7.5 %collective-permute-start.6 = (bf16[2,2,64,256]{3,2,1,0:T(8,128)(2,1)S(1)}, bf16[2,2,64,256]{3,2,1,0:T(8,128)(2,1)S(1)}, u32[]{:S(2)}, u32[]{:S(2)}) collective-permute-start(bf16[2,2,64,256]{3,2,1,0:T(8,128)(2,1)S(1)} %shard_map.114), channel_id=1, source_target_pairs={{0,1},{1,2},{2,3},{3,4},{4,5},{5,6},{6,7},{7,8},{8,9},{9,10},{10,1... | collective-permute-start | bytes 393224 | tf_op jit(solution)/shard_map/ppermute | solution.py:261

commit v3 on v2

v3 whole, which is shorter than its diff:
```python
import jax
import jax.numpy as jnp
from jax import lax
from jax.experimental import pallas as pl
from jax.experimental.pallas import tpu as pltpu
from jax.sharding import PartitionSpec as P

F32 = jnp.float32
BF16 = jnp.bfloat16
VMEM_LIMIT = 26 * 2**20
WEIGHT = 3 * 10**9
MID = 2 * 10**9
OUTER = 2 * 10**10
SECOND = 2 * 10**9


def activate(values, gain):
    values = values.astype(F32)
    mean = jnp.mean(values * values, axis=-1, keepdims=True)
    scaled = values * lax.rsqrt(mean + 1e-06) * gain
    return scaled / (1.0 + jnp.exp(-scaled))


def masked(keep, value):
    return jnp.where(keep, value, jnp.zeros_like(value))


def pair_weight(weight, wide):
    zero = jnp.zeros((128, 128), BF16)
    for kt in range(3):
        for j in range(4):
            rows = pl.ds((kt * 4 + j) * 128, 128)
            for kw in range(3):
                for r in range(2):
                    kh = j - r
                    inside = 0 <= kh <= 2
                    wide[rows, pl.ds((kw * 2 + r) * 128, 128)] = weight[kt, kh, kw] if inside else zero


def weight_kernel(w_one, w_two, wide, wide_two):
    pair_weight(w_one, wide)
    pair_weight(w_two, wide_two)


def pair_conv(source, wide, frame, count, row):
    m = count * 128
    pieces = [
        source[pl.ds(frame + kt, count), row + j].reshape(m, 128) for kt in range(3) for j in range(4)
    ]
    z = jnp.dot(jnp.concatenate(pieces, axis=1), wide[...], preferred_element_type=F32)
    left = z[:, :256].reshape(count, 128, 256)
    right = z[:, 512:].reshape(count, 128, 256)
    edge = jnp.zeros((count, 1, 256), F32)
    left = jnp.concatenate([edge, left[:, :127]], axis=1)
    right = jnp.concatenate([right[:, 1:], edge], axis=1)
    return left.reshape(m, 256) + z[:, 256:512] + right.reshape(m, 256)


def first_kernel(frames, video, gain, act, tail):
    for slot in range(2):
        for frame in range(4):
            act[slot, frame] = activate(video[slot, frame], gain[...]).astype(BF16)
    tail[...] = act[jnp.where(frames[1] > 0, 1, 0)]


def hidden_rows(source, wide, bias, gain, frame, row):
    h = pair_conv(source, wide, frame, 2, row)
    for r in range(2):
        v = activate(h[:, r * 128 : r * 128 + 128] + bias[...], gain[...])
        yield r, v.reshape(2, 128, 128)


def inside(value, top, bottom):
    space = lax.axis_index("space")
    if top:
        value = masked(space > 0, value)
    if bottom:
        value = masked(space < lax.axis_size("space") - 1, value)
    return value


def summed_rows(u2, wide, bias, frame, video, slot, first, ys, at):
    h = pair_conv(u2, wide, frame, 2, 0)
    for r in range(2):
        v = h[:, r * 128 : r * 128 + 128] + bias[...]
        y = video[slot, first : first + 2, r].reshape(256, 128).astype(F32) + v
        ys[pl.ds(at, 2), r, 8:] = y.astype(BF16).astype(F32).reshape(2, 128, 128)


def columns(ys, frame, r):
    return jnp.concatenate([ys[frame, r, pl.ds(7 + kw, 64, stride=2)].astype(BF16) for kw in range(3)], axis=1)


def mid_kernel(pred, own, pin, wide, bias_one, gain_two, near, mid):
    keep = pred[1] >= 0
    parity = lax.rem(lax.axis_index("space"), 2)
    for src, at in ((own, 2 * parity), (pin, 2 - 2 * parity)):
        for slot in range(2):
            for f in range(4):
                v = src[slot, f]
                near[6 * slot + f, pl.ds(at, 2)] = v
                if slot == 0 and f >= 2:
                    near[2 + f, pl.ds(at, 2)] = masked(keep, v)
    for frame, target in ((0, 0), (4, 2), (6, 4)):
        for r, v in hidden_rows(near, wide, bias_one, gain_two, frame, 0):
            mid[target : target + 2, r] = v.astype(BF16)


def outer_kernel(pred, near, mid, cross, wide, bias_one, gain_two, u2a, u2b, ux):
    keep = pred[1] >= 0
    parity = lax.rem(lax.axis_index("space"), 2)
    at, other = 2 * parity, 2 - 2 * parity
    ux[:, pl.ds(other, 2)] = near[:, pl.ds(at, 2)]
    for slot in range(2):
        for f in range(4):
            v = cross[slot, f]
            ux[6 * slot + f, pl.ds(at, 2)] = v
            if slot == 0 and f >= 2:
                ux[2 + f, pl.ds(at, 2)] = masked(keep, v)
    for frame, target in ((0, 0), (4, 2), (6, 4)):
        for r, v in hidden_rows(ux, wide, bias_one, gain_two, frame, 0):
            v = inside(v, r == 0, r == 1).astype(BF16)
            if target == 0:
                u2a[:, at + r] = v
                v = masked(keep, v)
            u2b[target : target + 2, at + r] = v
    u2a[:, pl.ds(other, 2)] = mid[0:2]
    u2b[0:2, pl.ds(other, 2)] = masked(keep, mid[0:2])
    u2b[2:6, pl.ds(other, 2)] = mid[2:6]


def before(refs, frame, keep, ux, at):
    parity = lax.rem(lax.axis_index("space"), 2)
    for src, row in zip(refs, (2, 4 - 4 * parity, 4 * parity)):
        ux[at, pl.ds(row, 2)] = masked(keep, src[frame])


def strided(ys, w_down):
    rows = {(f, r): columns(ys, f, r) for f in range(4) for r in range(2)}
    here, below = {}, {}
    for kt, read, goes in ((0, (0, 2), (1, 2)), (1, (1, 3), (1, 2)), (2, (0, 2), (0, 1))):
        upper, under = (jnp.concatenate([rows[f, r] for f in read], axis=0) for r in range(2))
        parts = (
            (here, jnp.dot(jnp.concatenate([upper, under], axis=1), w_down[kt, 384:], preferred_element_type=F32)),
            (below, jnp.dot(under, w_down[kt, :384], preferred_element_type=F32)),
        )
        for i, t in enumerate(goes):
            for sums, value in parts:
                part = value[i * 64 : i * 64 + 64]
                sums[t] = sums[t] + part if t in sums else part
    return here, below


def second_kernel(u2, video, wide_two, bias_two, w_down, bias_down, here_b, below_b, sent_b, ys):
    ys[:, :, :8] = jnp.zeros((4, 2, 8, 128), F32)
    for half in range(2):
        summed_rows(u2, wide_two, bias_two, 2 * half, video, 1, 2 * half, ys, 2 * half)
    here, below = strided(ys, w_down)
    for t in range(2):
        here_b[t] = here[t] + bias_down[...]
        below_b[t] = below[t]
    sent_b[0] = here[2]
    sent_b[1] = below[2]


def context_kernel(
    pred, frames, near, cross, pown, ppin, pcross, u2a, sent_b, video,
    wide, bias_one, gain_two, wide_two, bias_two, w_down,
    u2c, ya, sent,
    ux, us, ys,
):
    keep = pred[0] >= 0
    parity = lax.rem(lax.axis_index("space"), 2)
    for f in range(2):
        before((pown, ppin, pcross), 2 + f, keep, ux, f)
    ux[2:4, pl.ds(2 - 2 * parity, 4)] = near[0:2]
    ux[2:4, pl.ds(4 * parity, 2)] = cross[0, 0:2]
    us[2:4] = u2a[...]
    ys[:, :, :8] = jnp.zeros((2, 2, 8, 128), F32)
    for row in (0, 2):
        for r, v in hidden_rows(ux, wide, bias_one, gain_two, 0, row):
            us[0:2, row + r] = inside(v, row + r == 0, row + r == 3).astype(BF16)
    u2c[...] = us[0:2]
    summed_rows(us, wide_two, bias_two, 0, video, 0, 2, ys, 0)
    ya[...] = ys[...]
    here, below = 0.0, 0.0
    for kt in range(2):
        upper, under = columns(ys, kt, 0), columns(ys, kt, 1)
        both = jnp.concatenate([upper, under], axis=1)
        here = here + jnp.dot(both, w_down[kt, 384:], preferred_element_type=F32)
        below = below + jnp.dot(under, w_down[kt, :384], preferred_element_type=F32)
    second = frames[1] > 0
    sent[0] = jnp.where(second, sent_b[0], here).astype(BF16)
    sent[1] = jnp.where(second, sent_b[1], below).astype(BF16)


def rest_kernel(
    pred, pown, ppin, pcross, u2c, u2a, ya, here_b, below_b, video,
    wide, bias_one, gain_two, wide_two, bias_two, w_down, bias_down,
    out, below_out,
    ux, ua, ys,
):
    keep_a, keep_b = pred[0] >= 0, pred[1] >= 0
    for f in range(4):
        before((pown, ppin, pcross), f, keep_a, ux, f)
    ua[2:4] = u2c[...]
    ys[0:2, :, :8] = jnp.zeros((2, 2, 8, 128), F32)
    ys[2:4] = ya[...]
    for row in (0, 2):
        for r, v in hidden_rows(ux, wide, bias_one, gain_two, 0, row):
            ua[0:2, row + r] = masked(keep_a, inside(v, row + r == 0, row + r == 3)).astype(BF16)
    summed_rows(ua, wide_two, bias_two, 0, video, 0, 0, ys, 0)
    here, below = strided(ys, w_down)
    for t in range(2):
        out[0, t] = here[t] + bias_down[...]
        below_out[0, t] = below[t]
    out[1, 0] = here_b[0] + masked(keep_b, here[2])
    out[1, 1] = here_b[1]
    below_out[1, 0] = below_b[0] + masked(keep_b, below[2])
    below_out[1, 1] = below_b[1]


def relay_kernel(pred, got, below, below_out):
    below_out[...] = below[...].astype(BF16)
    below_out[0, 0] = (below[0, 0] + masked(pred[0] >= 0, got[1].astype(F32))).astype(BF16)


def last_kernel(pred, frames, here, got, above, out):
    for slot in range(2):
        for t in range(2):
            v = here[slot, t] + above[slot, t].astype(F32)
            if slot == 0 and t == 0:
                v = v + masked(pred[0] >= 0, got[0].astype(F32))
            out[slot, t, 0] = masked(2 * t < frames[slot], v).astype(BF16)


VMEM = pl.BlockSpec(memory_space=pltpu.VMEM)
SMEM = pl.BlockSpec(memory_space=pltpu.SMEM)


def call(kernel, outs, scratch, scalars, arrays, flops, limit=VMEM_LIMIT):
    return pl.pallas_call(
        kernel,
        out_shape=[jax.ShapeDtypeStruct(shape, dtype) for shape, dtype in outs],
        in_specs=[SMEM] * len(scalars) + [VMEM] * len(arrays),
        out_specs=[VMEM] * len(outs),
        scratch_shapes=scratch,
        compiler_params=pltpu.CompilerParams(vmem_limit_bytes=limit),
        cost_estimate=pl.CostEstimate(flops=flops, bytes_accessed=2**18, transcendentals=0),
    )(*scalars, *arrays)


def local(
    video, pred_slot, frames, gain_one, conv_one, bias_one, gain_two, conv_two, bias_two, down_weight, down_bias
):
    n_block, n_space = lax.axis_size("block"), lax.axis_size("space")
    inner = [(i, i ^ 1) for i in range(n_space)]
    outer = [(i, j) for i in range(n_space) if 0 <= (j := i + 1 if i % 2 else i - 1) < n_space]
    onward = [(b, b + 1) for b in range(n_block - 1)]
    corner = [(b * n_space + i, (b + 1) * n_space + j) for b in range(n_block - 1) for i, j in outer]
    band = video.shape
    act, tail = call(
        first_kernel, [(band, BF16), (band[1:], BF16)], [], (frames,), (video, gain_one.reshape(1, 128)), 10**9,
        60 * 2**20,
    )
    pown = lax.ppermute(tail, "block", onward)
    pin = lax.ppermute(act, "space", inner)
    cross = lax.ppermute(act, "space", outer)
    pcross = lax.ppermute(tail, ("block", "space"), corner)
    wide = ((1536, 768), BF16)
    conv_one, pown = lax.optimization_barrier((conv_one, pown))
    wide_one, wide_two = call(weight_kernel, [wide, wide], [], (), (conv_one, conv_two), WEIGHT)
    ppin = lax.ppermute(pown, "space", inner)
    norm = (wide_one, bias_one.reshape(1, 128), gain_two.reshape(1, 128))
    stride = (wide_two, bias_two.reshape(1, 128), down_weight.reshape(3, 1152, 256))

    def hidden(count, rows=4):
        return ((count, rows, 128, 128), BF16)

    def vmem(shape):
        return pltpu.VMEM(*shape)

    both = ((2, 2, 64, 256), F32)
    near, mid = call(mid_kernel, [hidden(10), hidden(6, 2)], [], (pred_slot,), (act, pin, *norm), MID)
    u2a, u2b = call(
        outer_kernel, [hidden(2), hidden(6)], [vmem(hidden(10))], (pred_slot,),
        (near, mid, cross, *norm), OUTER,
    )
    before_refs = (pown, ppin, pcross)
    bias = down_bias.reshape(1, 256)
    one = ((2, 64, 256), F32)
    ys = ((4, 2, 136, 128), F32)
    here_b, below_b, sent_b = call(
        second_kernel, [one, one, one], [vmem(ys)], (), (u2b, video, *stride, bias), SECOND
    )
    ya = ((2,) + ys[0][1:], F32)
    u2c, ya, sent = call(
        context_kernel, [hidden(2), ya, ((2, 64, 256), BF16)], [vmem(hidden(4, 6)), vmem(hidden(4)), vmem(ya)],
        (pred_slot, frames), (near, cross, *before_refs, u2a, sent_b, video, *norm, *stride), 10**9,
    )
    out, below = call(
        rest_kernel, [both, both], [vmem(hidden(4, 6)), vmem(hidden(4)), vmem(ys)], (pred_slot,),
        (*before_refs, u2c, u2a, ya, here_b, below_b, video, *norm, *stride, bias), 4 * 10**9,
    )
    got = lax.ppermute(sent, "block", onward)
    [below] = call(relay_kernel, [(both[0], BF16)], [], (pred_slot,), (got, below), 10**6)
    above = lax.ppermute(below, "space", [(i, i + 1) for i in range(n_space - 1)])
    [down] = call(last_kernel, [((2, 2, 1, 64, 256), BF16)], [], (pred_slot, frames), (out, got, above), 10**6)
    return down


def solution(mesh):
    return jax.shard_map(
        local,
        mesh=mesh,
        in_specs=(P("block", None, "space", None, None), P("block"), P("block")) + (P(),) * 8,
        out_specs=P("block", None, "space", None, None),
        check_vma=False,
    )
```

time: 49 us -> 46.6 us (0.951)
  waiting for transfers between devices: 14.1 us -> 10.7 us
  Pallas kernels: 17.8 us -> 20 us
  starting transfers between devices: 16.6 us -> 15.3 us
    ppermute x1, waiting for transfers between devices: 2.62 us -> 0.01 us  [local(): cross = lax.ppermute(act, 'space', outer)]
    ppermute x1, waiting for transfers between devices: 4.91 us -> 2.32 us  [local(): got = lax.ppermute(sent, 'block', onward)]
    pallas_call x7 -> x9, Pallas kernels: 17.8 us -> 20 us  [call(): pl.pallas_call(kernel, out_shape=[jax.ShapeDtypeStruct(shape, dtype) for...]
    ppermute x1, waiting for transfers between devices: 0.08 us -> 1.87 us  [local(): pcross = lax.ppermute(tail, ('block', 'space'), corner)]
    ppermute x1, starting transfers between devices: 3.36 us -> 2.1 us  [local(): got = lax.ppermute(sent, 'block', onward)]
  transfers between devices with their start and end apart: 7 -> 7, of which waited for: 5 -> 4; matrix products, arithmetic and copies ran while one was open for 0% -> 0% of each run, Pallas kernels for 15% -> 26%
where the time goes in v3:
time: 46.6 us; the launch traced here: 46.3 us
  Pallas kernels  20 us (43%)
  starting transfers between devices  15.3 us (33%)
  waiting for transfers between devices  10.7 us (23%)
    pallas_call x9, Pallas kernels, call(): pl.pallas_call(kernel, out_shape=[jax.ShapeDtypeStruct(shape, dtype) for...  20 us
    ppermute x1, starting transfers between devices, local(): pcross = lax.ppermute(tail, ('block', 'space'), corner)  5.73 us
    ppermute x1, waiting for transfers between devices, local(): lax.ppermute(below, 'space', [(i, i + 1) for i in range(n_space - 1)])  5.57 us
    ppermute x1, starting transfers between devices, local(): pown = lax.ppermute(tail, 'block', onward)  3.35 us
    ppermute x1, waiting for transfers between devices, local(): got = lax.ppermute(sent, 'block', onward)  2.32 us
    ppermute x1, starting transfers between devices, local(): cross = lax.ppermute(act, 'space', outer)  2.11 us
    ppermute x1, starting transfers between devices, local(): got = lax.ppermute(sent, 'block', onward)  2.1 us
    ppermute x1, starting transfers between devices, local(): lax.ppermute(below, 'space', [(i, i + 1) for i in range(n_space - 1)])  1.92 us
  transfers between devices with their start and end apart: 7, of which 4 were waited for; matrix products, arithmetic and copies ran while one was open for 0% of the time, Pallas kernels for 26%

profile of v3, /device:TPU:136, one launch (start us, length us, event | category | flops | bytes accessed | tf_op | source)
XLA Modules:
  0.0 46.3 jit_solution(10030818328222322229)
XLA Ops:
  0.0 0.0 copy-start.7
  0.0 0.0 copy-start.8
  0.0 2.7 %shard_map.109 = (bf16[2,4,2,128,128]{4,3,2,1,0:T(8,128)(2,1)}, bf16[4,2,128,128]{3,2,1,0:T(8,128)(2,1)}) custom-call(s32[2]{0:T(128)} %frames.5, bf16[2,4,2,128,128]{4,3,2,1,0:T(8,128)(2,1)} %video.7, f32[1,128]{1,0:T(1,128)} %bitcast.22), custom_call_target="tpu_custom_call" | custom-call | flops 1000000000 | bytes 262144 | tf_op jit(solution)/shard_map/pallas_call | solution.py:242
  2.7 3.4 %collective-permute-start = (bf16[4,2,128,128]{3,2,1,0:T(8,128)(2,1)}, bf16[4,2,128,128]{3,2,1,0:T(8,128)(2,1)S(1)}, u32[]{:S(2)}, u32[]{:S(2)}) collective-permute-start(bf16[4,2,128,128]{3,2,1,0:T(8,128)(2,1)} %get-tuple-element.23), channel_id=1, source_target_pairs={{0,16},{16,32},{32,48},{48,64},{64,80},{80,96},{96,112},{112,128},... | collective-permute-start | bytes 786440 | tf_op jit(solution)/shard_map/ppermute | solution.py:266
  6.0 0.0 copy-start.2
  6.0 0.0 copy-start.4
  6.0 0.0 copy-start.5
  6.1 0.0 copy-start.9
  6.1 0.1 collective-permute-start.3
  6.2 2.1 %collective-permute-start.4 = (bf16[2,4,2,128,128]{4,3,2,1,0:T(8,128)(2,1)}, bf16[2,4,2,128,128]{4,3,2,1,0:T(8,128)(2,1)S(1)}, u32[]{:S(2)}, u32[]{:S(2)}) collective-permute-start(bf16[2,4,2,128,128]{4,3,2,1,0:T(8,128)(2,1)} %get-tuple-element.25.own), channel_id=1, source_target_pairs={{1,2},{2,1},{3,4},{4,3},{5,6},{6,5},{7,8},{8,7},{9,10},{10,9},{11,... | collective-permute-start | bytes 1572872 | tf_op jit(solution)/shard_map/ppermute | solution.py:268
  8.3 5.7 %collective-permute-start.2 = (bf16[4,2,128,128]{3,2,1,0:T(8,128)(2,1)}, bf16[4,2,128,128]{3,2,1,0:T(8,128)(2,1)S(1)}, u32[]{:S(2)}, u32[]{:S(2)}) collective-permute-start(bf16[4,2,128,128]{3,2,1,0:T(8,128)(2,1)} %get-tuple-element.23), channel_id=1, source_target_pairs={{1,18},{2,17},{3,20},{4,19},{5,22},{6,21},{7,24},{8,23},{9,26},{10... | collective-permute-start | bytes 786440 | tf_op jit(solution)/shard_map/ppermute | solution.py:269
  14.0 0.9 %collective-permute-done.pown = bf16[4,2,128,128]{3,2,1,0:T(8,128)(2,1)S(1)} collective-permute-done((bf16[4,2,128,128]{3,2,1,0:T(8,128)(2,1)}, bf16[4,2,128,128]{3,2,1,0:T(8,128)(2,1)S(1)}, u32[]{:S(2)}, u32[]{:S(2)}) %collective-permute-start) | collective-permute-done | bytes 262176 | tf_op jit(solution)/shard_map/ppermute | solution.py:266
  14.9 0.0 collective-permute-start.1
  14.9 0.0 copy-done.7
  14.9 0.0 copy-done.8
  14.9 0.6 %shard_map.110 = (bf16[1536,768]{1,0:T(8,128)(2,1)S(1)}, bf16[1536,768]{1,0:T(8,128)(2,1)S(1)}) custom-call(bf16[3,3,3,128,128]{4,3,2,1,0:T(8,128)(2,1)S(1)} %copy-done.7, bf16[3,3,3,128,128]{4,3,2,1,0:T(8,128)(2,1)S(1)} %copy-done.8), custom_call_target="tpu_custom_call" | custom-call | flops 3000000000 | bytes 262144 | tf_op jit(solution)/shard_map/pallas_call | solution.py:242
  15.5 0.0 collective-permute-done.3.pin
  15.5 0.0 copy-done.2
  15.6 0.0 copy-done.4
  15.6 0.0 copy-done.5
  15.6 0.0 copy-done.9
  15.6 2.9 %shard_map.111 = (bf16[10,4,128,128]{3,2,1,0:T(8,128)(2,1)S(1)}, bf16[6,2,128,128]{3,2,1,0:T(8,128)(2,1)S(1)}) custom-call(s32[2]{0:T(128)S(1)} %copy-done.2, bf16[2,4,2,128,128]{4,3,2,1,0:T(8,128)(2,1)S(1)} %copy-done.9, bf16[2,4,2,128,128]{4,3,2,1,0:T(8,128)(2,1)S(1)} %collective-permute-done.3.pin, bf16[1536,768]{1,0:T(8,128)(2,1)S(1)} %get-tuple-element.27.wide, ...), custom_call_target="tpu_custom_call" | custom-call | flops 2000000000 | bytes 262144 | tf_op jit(solution)/shard_map/pallas_call | solution.py:242
  18.5 0.0 collective-permute-done.4.cross
  18.5 0.0 copy-start
  18.5 0.0 copy-start.1
  18.5 0.0 copy-start.6
  18.5 0.0 copy-start.10
  18.5 2.9 %shard_map.112 = (bf16[2,4,128,128]{3,2,1,0:T(8,128)(2,1)S(1)}, bf16[6,4,128,128]{3,2,1,0:T(8,128)(2,1)S(1)}) custom-call(s32[2]{0:T(128)S(1)} %copy-done.2, bf16[10,4,128,128]{3,2,1,0:T(8,128)(2,1)S(1)} %get-tuple-element.28.near, bf16[6,2,128,128]{3,2,1,0:T(8,128)(2,1)S(1)} %get-tuple-element.29.mid, ...), custom_call_target="tpu_custom_call" | custom-call | flops 20000000000 | bytes 262144 | tf_op jit(solution)/shard_map/pallas_call | solution.py:242
  21.4 0.0 copy-done
  21.4 0.0 copy-done.1
  21.4 0.0 copy-done.6
  21.4 0.0 copy-done.10
  21.5 0.0 copy-start.3
  21.5 1.9 %shard_map.113 = (f32[2,64,256]{2,1,0:T(8,128)S(1)}, f32[2,64,256]{2,1,0:T(8,128)S(1)}, f32[2,64,256]{2,1,0:T(8,128)S(1)}) custom-call(bf16[6,4,128,128]{3,2,1,0:T(8,128)(2,1)S(1)} %get-tuple-element.31.u2, bf16[2,4,2,128,128]{4,3,2,1,0:T(8,128)(2,1)S(1)} %copy-done.1, bf16[1536,768]{1,0:T(8,128)(2,1)S(1)} %get-tuple-element.32.wide_two, ...), custom_call_target="tpu_custom_call" | custom-call | flops 2000000000 | bytes 262144 | tf_op jit(solution)/shard_map/pallas_call | solution.py:242
  23.4 1.9 %collective-permute-done.2.pcross = bf16[4,2,128,128]{3,2,1,0:T(8,128)(2,1)S(1)} collective-permute-done((bf16[4,2,128,128]{3,2,1,0:T(8,128)(2,1)}, bf16[4,2,128,128]{3,2,1,0:T(8,128)(2,1)S(1)}, u32[]{:S(2)}, u32[]{:S(2)}) %collective-permute-start.2) | collective-permute-done | bytes 262176 | tf_op jit(solution)/shard_map/ppermute | solution.py:269
  25.3 0.0 collective-permute-done.1.ppin
  25.3 0.0 copy-done.3
  25.3 3.5 %shard_map.114 = (bf16[2,4,128,128]{3,2,1,0:T(8,128)(2,1)S(1)}, f32[2,2,136,128]{3,2,1,0:T(8,128)S(1)}, bf16[2,64,256]{2,1,0:T(8,128)(2,1)S(1)}) custom-call(s32[2]{0:T(128)S(1)} %copy-done.2, s32[2]{0:T(128)S(1)} %copy-done.3, bf16[10,4,128,128]{3,2,1,0:T(8,128)(2,1)S(1)} %get-tuple-element.28.near, ...), custom_call_target="tpu_custom_call" | custom-call | flops 1000000000 | bytes 262144 | tf_op jit(solution)/shard_map/pallas_call | solution.py:242
  28.7 2.1 %collective-permute-start.5 = (bf16[2,64,256]{2,1,0:T(8,128)(2,1)S(1)}, bf16[2,64,256]{2,1,0:T(8,128)(2,1)S(1)}, u32[]{:S(2)}, u32[]{:S(2)}) collective-permute-start(bf16[2,64,256]{2,1,0:T(8,128)(2,1)S(1)} %get-tuple-element.39), channel_id=1, source_target_pairs={{0,16},{16,32},{32,48},{48,64},{64,80},{80,96},{96,112},{112,128},... | collective-permute-start | bytes 196616 | tf_op jit(solution)/shard_map/ppermute | solution.py:305
  30.9 3.8 %shard_map.115 = (f32[2,2,64,256]{3,2,1,0:T(8,128)S(1)}, f32[2,2,64,256]{3,2,1,0:T(8,128)S(1)}) custom-call(s32[2]{0:T(128)S(1)} %copy-done.2, bf16[4,2,128,128]{3,2,1,0:T(8,128)(2,1)S(1)} %collective-permute-done.pown, bf16[4,2,128,128]{3,2,1,0:T(8,128)(2,1)S(1)} %collective-permute-done.1.ppin, bf16[4,2,128,128]{3,2,1,0:T(8,128)(2,1)S(1)} %collective-permute-done.2.pcross, ...), custom_call_target="tpu_custom_call" | custom-call | flops 4000000000 | bytes 262144 | tf_op jit(solution)/shard_map/pallas_call | solution.py:242
  34.7 2.3 %collective-permute-done.5.got = bf16[2,64,256]{2,1,0:T(8,128)(2,1)S(1)} collective-permute-done((bf16[2,64,256]{2,1,0:T(8,128)(2,1)S(1)}, bf16[2,64,256]{2,1,0:T(8,128)(2,1)S(1)}, u32[]{:S(2)}, u32[]{:S(2)}) %collective-permute-start.5) | collective-permute-done | bytes 65568 | tf_op jit(solution)/shard_map/ppermute | solution.py:305
  37.0 0.6 %shard_map.116 = bf16[2,2,64,256]{3,2,1,0:T(8,128)(2,1)S(1)} custom-call(s32[2]{0:T(128)S(1)} %copy-done.2, bf16[2,64,256]{2,1,0:T(8,128)(2,1)S(1)} %collective-permute-done.5.got, f32[2,2,64,256]{3,2,1,0:T(8,128)S(1)} %get-tuple-element.40.below), custom_call_target="tpu_custom_call" | custom-call | flops 1000000 | bytes 262144 | tf_op jit(solution)/shard_map/pallas_call | solution.py:242
  37.6 1.9 %collective-permute-start.6 = (bf16[2,2,64,256]{3,2,1,0:T(8,128)(2,1)S(1)}, bf16[2,2,64,256]{3,2,1,0:T(8,128)(2,1)S(1)}, u32[]{:S(2)}, u32[]{:S(2)}) collective-permute-start(bf16[2,2,64,256]{3,2,1,0:T(8,128)(2,1)S(1)} %shard_map.116), channel_id=1, source_target_pairs={{0,1},{1,2},{2,3},{3,4},{4,5},{5,6},{6,7},{7,8},{8,9},{9,10},{10,1... | collective-permute-start | bytes 393224 | tf_op jit(solution)/shard_map/ppermute | solution.py:307
  39.5 5.6 %collective-permute-done.6.above = bf16[2,2,64,256]{3,2,1,0:T(8,128)(2,1)S(1)} collective-permute-done((bf16[2,2,64,256]{3,2,1,0:T(8,128)(2,1)S(1)}, bf16[2,2,64,256]{3,2,1,0:T(8,128)(2,1)S(1)}, u32[]{:S(2)}, u32[]{:S(2)}) %collective-permute-start.6) | collective-permute-done | bytes 131104 | tf_op jit(solution)/shard_map/ppermute | solution.py:307
  45.1 1.2 %shard_map.117 = bf16[2,2,1,64,256]{4,3,2,1,0:T(8,128)(2,1)} custom-call(s32[2]{0:T(128)S(1)} %copy-done.2, s32[2]{0:T(128)S(1)} %copy-done.3, f32[2,2,64,256]{3,2,1,0:T(8,128)S(1)} %get-tuple-element.38.here, bf16[2,64,256]{2,1,0:T(8,128)(2,1)S(1)} %collective-permute-done.5.got, bf16[2,2,64,256]{3,2,1,0:T(8,128)(2,1)S(1)} %collective-permute-done.6.above), custom_call_target="tpu_custom_call" | custom-call | flops 1000000 | bytes 262144 | tf_op jit(solution)/shard_map/pallas_call | solution.py:242
Async XLA Ops:
  0.0 14.9 %copy-start.7 = (bf16[3,3,3,128,128]{4,3,2,1,0:T(8,128)(2,1)S(1)}, bf16[3,3,3,128,128]{4,3,2,1,0:T(8,128)(2,1)}, u32[]{:S(2)}) copy-start(bf16[3,3,3,128,128]{4,3,2,1,0:T(8,128)(2,1)} %w_one) | copy-start | bytes 2654212
  0.0 14.9 %copy-start.8 = (bf16[3,3,3,128,128]{4,3,2,1,0:T(8,128)(2,1)S(1)}, bf16[3,3,3,128,128]{4,3,2,1,0:T(8,128)(2,1)}, u32[]{:S(2)}) copy-start(bf16[3,3,3,128,128]{4,3,2,1,0:T(8,128)(2,1)} %w_two.1) | copy-start | bytes 2654212
  2.7 12.2 %collective-permute-start = (bf16[4,2,128,128]{3,2,1,0:T(8,128)(2,1)}, bf16[4,2,128,128]{3,2,1,0:T(8,128)(2,1)S(1)}, u32[]{:S(2)}, u32[]{:S(2)}) collective-permute-start(bf16[4,2,128,128]{3,2,1,0:T(8,128)(2,1)} %get-tuple-element.23), channel_id=1, source_target_pairs={{0,16},{16,32},{32,48},{48,64},{64,80},{80,96},{96,112},{112,128},... | collective-permute-start | bytes 786440 | tf_op jit(solution)/shard_map/ppermute | solution.py:266
  6.0 9.5 %copy-start.2 = (s32[2]{0:T(128)S(1)}, s32[2]{0:T(128)}, u32[]{:S(2)}) copy-start(s32[2]{0:T(128)} %pred_.11) | copy-start | bytes 28
  6.0 9.5 %copy-start.4 = (f32[128]{0:T(128)S(1)}, f32[128]{0:T(128)}, u32[]{:S(2)}) copy-start(f32[128]{0:T(128)} %param.16) | copy-start | bytes 1540
  6.0 9.5 %copy-start.5 = (f32[128]{0:T(128)S(1)}, f32[128]{0:T(128)}, u32[]{:S(2)}) copy-start(f32[128]{0:T(128)} %param.17) | copy-start | bytes 1540
  6.1 9.5 %copy-start.9 = (bf16[2,4,2,128,128]{4,3,2,1,0:T(8,128)(2,1)S(1)}, bf16[2,4,2,128,128]{4,3,2,1,0:T(8,128)(2,1)}, u32[]{:S(2)}) copy-start(bf16[2,4,2,128,128]{4,3,2,1,0:T(8,128)(2,1)} %get-tuple-element.25.own) | copy-start | bytes 1572868
  6.1 9.5 %collective-permute-start.3 = (bf16[2,4,2,128,128]{4,3,2,1,0:T(8,128)(2,1)}, bf16[2,4,2,128,128]{4,3,2,1,0:T(8,128)(2,1)S(1)}, u32[]{:S(2)}, u32[]{:S(2)}) collective-permute-start(bf16[2,4,2,128,128]{4,3,2,1,0:T(8,128)(2,1)} %get-tuple-element.25.own), channel_id=1, source_target_pairs={{0,1},{1,0},{2,3},{3,2},{4,5},{5,4},{6,7},{7,6},{8,9},{9,8},{10,11... | collective-permute-start | bytes 1572872 | tf_op jit(solution)/shard_map/ppermute | solution.py:267
  6.2 12.3 %collective-permute-start.4 = (bf16[2,4,2,128,128]{4,3,2,1,0:T(8,128)(2,1)}, bf16[2,4,2,128,128]{4,3,2,1,0:T(8,128)(2,1)S(1)}, u32[]{:S(2)}, u32[]{:S(2)}) collective-permute-start(bf16[2,4,2,128,128]{4,3,2,1,0:T(8,128)(2,1)} %get-tuple-element.25.own), channel_id=1, source_target_pairs={{1,2},{2,1},{3,4},{4,3},{5,6},{6,5},{7,8},{8,7},{9,10},{10,9},{11,... | collective-permute-start | bytes 1572872 | tf_op jit(solution)/shard_map/ppermute | solution.py:268
  8.3 17.0 %collective-permute-start.2 = (bf16[4,2,128,128]{3,2,1,0:T(8,128)(2,1)}, bf16[4,2,128,128]{3,2,1,0:T(8,128)(2,1)S(1)}, u32[]{:S(2)}, u32[]{:S(2)}) collective-permute-start(bf16[4,2,128,128]{3,2,1,0:T(8,128)(2,1)} %get-tuple-element.23), channel_id=1, source_target_pairs={{1,18},{2,17},{3,20},{4,19},{5,22},{6,21},{7,24},{8,23},{9,26},{10... | collective-permute-start | bytes 786440 | tf_op jit(solution)/shard_map/ppermute | solution.py:269
  14.9 10.4 %collective-permute-start.1 = (bf16[4,2,128,128]{3,2,1,0:T(8,128)(2,1)S(1)}, bf16[4,2,128,128]{3,2,1,0:T(8,128)(2,1)S(1)}, u32[]{:S(2)}, u32[]{:S(2)}) collective-permute-start(bf16[4,2,128,128]{3,2,1,0:T(8,128)(2,1)S(1)} %collective-permute-done.pown), channel_id=1, source_target_pairs={{0,1},{1,0},{2,3},{3,2},{4,5},{5,4},{6,7},{7,6},{8,9},{9,8},{10,11... | collective-permute-start | bytes 786440 | tf_op jit(solution)/shard_map/ppermute | solution.py:273
  18.5 3.0 %copy-start = (bf16[3,3,3,128,256]{4,3,2,1,0:T(8,128)(2,1)S(1)}, bf16[3,3,3,128,256]{4,3,2,1,0:T(8,128)(2,1)}, u32[]{:S(2)}) copy-start(bf16[3,3,3,128,256]{4,3,2,1,0:T(8,128)(2,1)} %param.20) | copy-start | bytes 5308420
  18.5 2.9 %copy-start.1 = (bf16[2,4,2,128,128]{4,3,2,1,0:T(8,128)(2,1)S(1)}, bf16[2,4,2,128,128]{4,3,2,1,0:T(8,128)(2,1)}, u32[]{:S(2)}) copy-start(bf16[2,4,2,128,128]{4,3,2,1,0:T(8,128)(2,1)} %video.7) | copy-start | bytes 1572868
  18.5 2.9 %copy-start.6 = (f32[128]{0:T(128)S(1)}, f32[128]{0:T(128)}, u32[]{:S(2)}) copy-start(f32[128]{0:T(128)} %param.19) | copy-start | bytes 1540
  18.5 2.9 %copy-start.10 = (f32[256]{0:T(256)S(1)}, f32[256]{0:T(256)}, u32[]{:S(2)}) copy-start(f32[256]{0:T(256)} %param.21) | copy-start | bytes 3076
  21.5 3.8 %copy-start.3 = (s32[2]{0:T(128)S(1)}, s32[2]{0:T(128)}, u32[]{:S(2)}) copy-start(s32[2]{0:T(128)} %frames.5) | copy-start | bytes 28
  28.7 8.3 %collective-permute-start.5 = (bf16[2,64,256]{2,1,0:T(8,128)(2,1)S(1)}, bf16[2,64,256]{2,1,0:T(8,128)(2,1)S(1)}, u32[]{:S(2)}, u32[]{:S(2)}) collective-permute-start(bf16[2,64,256]{2,1,0:T(8,128)(2,1)S(1)} %get-tuple-element.39), channel_id=1, source_target_pairs={{0,16},{16,32},{32,48},{48,64},{64,80},{80,96},{96,112},{112,128},... | collective-permute-start | bytes 196616 | tf_op jit(solution)/shard_map/ppermute | solution.py:305
  37.6 7.5 %collective-permute-start.6 = (bf16[2,2,64,256]{3,2,1,0:T(8,128)(2,1)S(1)}, bf16[2,2,64,256]{3,2,1,0:T(8,128)(2,1)S(1)}, u32[]{:S(2)}, u32[]{:S(2)}) collective-permute-start(bf16[2,2,64,256]{3,2,1,0:T(8,128)(2,1)S(1)} %shard_map.116), channel_id=1, source_target_pairs={{0,1},{1,2},{2,3},{3,4},{4,5},{5,6},{6,7},{7,8},{8,9},{9,10},{10,1... | collective-permute-start | bytes 393224 | tf_op jit(solution)/shard_map/ppermute | solution.py:307

commit v4 on v3

--- a/solution.py
+++ b/solution.py
@@ -9,37 +9,34 @@
 BF16 = jnp.bfloat16
 VMEM_LIMIT = 26 * 2**20
 WEIGHT = 3 * 10**9
-MID = 2 * 10**9
-OUTER = 2 * 10**10
-SECOND = 2 * 10**9
+MID = 10**10
+OUTER = 10**9
+SECOND = 10**9
 
 
 def activate(values, gain):
     values = values.astype(F32)
     mean = jnp.mean(values * values, axis=-1, keepdims=True)
-    scaled = values * lax.rsqrt(mean + 1e-06) * gain
-    return scaled / (1.0 + jnp.exp(-scaled))
+    half = values * lax.rsqrt(mean + 1e-06) * (0.5 * gain)
+    return half + half * jnp.tanh(half)
 
 
 def masked(keep, value):
     return jnp.where(keep, value, jnp.zeros_like(value))
 
 
-def pair_weight(weight, wide):
+def pair_weight(weight):
     zero = jnp.zeros((128, 128), BF16)
-    for kt in range(3):
-        for j in range(4):
-            rows = pl.ds((kt * 4 + j) * 128, 128)
-            for kw in range(3):
-                for r in range(2):
-                    kh = j - r
-                    inside = 0 <= kh <= 2
-                    wide[rows, pl.ds((kw * 2 + r) * 128, 128)] = weight[kt, kh, kw] if inside else zero
-
-
-def weight_kernel(w_one, w_two, wide, wide_two):
-    pair_weight(w_one, wide)
-    pair_weight(w_two, wide_two)
+    return jnp.concatenate(
+        [
+            jnp.concatenate(
+                [weight[kt, j - r, kw] if 0 <= j - r <= 2 else zero for kw in range(3) for r in range(2)], axis=1
+            )
+            for kt in range(3)
+            for j in range(4)
+        ],
+        axis=0,
+    )
 
 
 def pair_conv(source, wide, frame, count, row):
@@ -47,7 +44,7 @@
     pieces = [
         source[pl.ds(frame + kt, count), row + j].reshape(m, 128) for kt in range(3) for j in range(4)
     ]
-    z = jnp.dot(jnp.concatenate(pieces, axis=1), wide[...], preferred_element_type=F32)
+    z = jnp.dot(jnp.concatenate(pieces, axis=1), pair_weight(wide), preferred_element_type=F32)
     left = z[:, :256].reshape(count, 128, 256)
     right = z[:, 512:].reshape(count, 128, 256)
     edge = jnp.zeros((count, 1, 256), F32)
@@ -257,7 +254,6 @@
     inner = [(i, i ^ 1) for i in range(n_space)]
     outer = [(i, j) for i in range(n_space) if 0 <= (j := i + 1 if i % 2 else i - 1) < n_space]
     onward = [(b, b + 1) for b in range(n_block - 1)]
-    corner = [(b * n_space + i, (b + 1) * n_space + j) for b in range(n_block - 1) for i, j in outer]
     band = video.shape
     act, tail = call(
         first_kernel, [(band, BF16), (band[1:], BF16)], [], (frames,), (video, gain_one.reshape(1, 128)), 10**9,
@@ -265,14 +261,10 @@
     )
     pown = lax.ppermute(tail, "block", onward)
     pin = lax.ppermute(act, "space", inner)
-    cross = lax.ppermute(act, "space", outer)
-    pcross = lax.ppermute(tail, ("block", "space"), corner)
-    wide = ((1536, 768), BF16)
-    conv_one, pown = lax.optimization_barrier((conv_one, pown))
-    wide_one, wide_two = call(weight_kernel, [wide, wide], [], (), (conv_one, conv_two), WEIGHT)
-    ppin = lax.ppermute(pown, "space", inner)
-    norm = (wide_one, bias_one.reshape(1, 128), gain_two.reshape(1, 128))
-    stride = (wide_two, bias_two.reshape(1, 128), down_weight.reshape(3, 1152, 256))
+    sent_act, pin = lax.optimization_barrier((act, pin))
+    cross = lax.ppermute(sent_act, "space", outer)
+    norm = (conv_one, bias_one.reshape(1, 128), gain_two.reshape(1, 128))
+    stride = (conv_two, bias_two.reshape(1, 128), down_weight.reshape(3, 1152, 256))
 
     def hidden(count, rows=4):
         return ((count, rows, 128, 128), BF16)
@@ -282,6 +274,9 @@
 
     both = ((2, 2, 64, 256), F32)
     near, mid = call(mid_kernel, [hidden(10), hidden(6, 2)], [], (pred_slot,), (act, pin, *norm), MID)
+    pown, mid = lax.optimization_barrier((pown, mid))
+    ppin = lax.ppermute(pown, "space", inner)
+    pcross = lax.ppermute(pown, "space", outer)
     u2a, u2b = call(
         outer_kernel, [hidden(2), hidden(6)], [vmem(hidden(10))], (pred_slot,),
         (near, mid, cross, *norm), OUTER,

time: 46.6 us -> 45.6 us (0.979)
  starting transfers between devices: 15.3 us -> 11.3 us
  waiting for transfers between devices: 10.7 us -> 13.8 us
  Pallas kernels: 20 us -> 18.9 us
  local copies, waits for them, and re-layouts: 0.06 us -> 1.09 us
    ppermute x2, starting transfers between devices: 7.83 us -> 4.04 us  [the longest x1 2.12 us: local(): pcross = lax.ppermute(pown, 'space', outer)]
    ppermute x1, waiting for transfers between devices: 0.89 us -> 3.66 us  [local(): pown = lax.ppermute(tail, 'block', onward)]
    pallas_call x9 -> x8, Pallas kernels: 20 us -> 18.9 us  [call(): pl.pallas_call(kernel, out_shape=[jax.ShapeDtypeStruct(shape, dtype) for...]
    unnamed x22, local copies, waits for them, and re-layouts: 0.06 us -> 1.09 us
  transfers between devices with their start and end apart: 7 -> 7, of which waited for: 4 -> 5; matrix products, arithmetic and copies ran while one was open for 0% -> 0% of each run, Pallas kernels for 26% -> 25%
where the time goes in v4:
time: 45.6 us; the launch traced here: 45.3 us
  Pallas kernels  18.9 us (41%)
  waiting for transfers between devices  13.8 us (30%)
  starting transfers between devices  11.3 us (25%)
  local copies, waits for them, and re-layouts  1.09 us (2%)
    pallas_call x8, Pallas kernels, call(): pl.pallas_call(kernel, out_shape=[jax.ShapeDtypeStruct(shape, dtype) for...  18.9 us
    ppermute x1, waiting for transfers between devices, local(): lax.ppermute(below, 'space', [(i, i + 1) for i in range(n_space - 1)])  5.57 us
    ppermute x1, waiting for transfers between devices, local(): pown = lax.ppermute(tail, 'block', onward)  3.66 us
    ppermute x1, starting transfers between devices, local(): pown = lax.ppermute(tail, 'block', onward)  3.39 us
    ppermute x1, waiting for transfers between devices, local(): got = lax.ppermute(sent, 'block', onward)  2.62 us
    ppermute x1, starting transfers between devices, local(): pcross = lax.ppermute(pown, 'space', outer)  2.12 us
    ppermute x1, starting transfers between devices, local(): lax.ppermute(below, 'space', [(i, i + 1) for i in range(n_space - 1)])  1.92 us
    ppermute x1, starting transfers between devices, local(): got = lax.ppermute(sent, 'block', onward)  1.92 us
  transfers between devices with their start and end apart: 7, of which 5 were waited for; matrix products, arithmetic and copies ran while one was open for 0% of the time, Pallas kernels for 25%

profile of v4, /device:TPU:136, one launch (start us, length us, event | category | flops | bytes accessed | tf_op | source)
XLA Modules:
  0.0 45.3 jit_solution(15685911421073549365)
XLA Ops:
  0.0 0.0 copy-start.3
  0.0 0.0 copy-start.4
  0.0 0.0 copy-start.8
  0.0 0.0 copy-start.9
  0.0 2.5 %shard_map.109 = (bf16[2,4,2,128,128]{4,3,2,1,0:T(8,128)(2,1)}, bf16[4,2,128,128]{3,2,1,0:T(8,128)(2,1)}) custom-call(s32[2]{0:T(128)} %frames.5, bf16[2,4,2,128,128]{4,3,2,1,0:T(8,128)(2,1)} %video.7, f32[1,128]{1,0:T(1,128)} %bitcast.22), custom_call_target="tpu_custom_call" | custom-call | flops 1000000000 | bytes 262144 | tf_op jit(solution)/shard_map/pallas_call | solution.py:239
  2.5 0.0 collective-permute-start.1
  2.5 3.4 %collective-permute-start = (bf16[4,2,128,128]{3,2,1,0:T(8,128)(2,1)}, bf16[4,2,128,128]{3,2,1,0:T(8,128)(2,1)S(1)}, u32[]{:S(2)}, u32[]{:S(2)}) collective-permute-start(bf16[4,2,128,128]{3,2,1,0:T(8,128)(2,1)} %get-tuple-element.23), channel_id=1, source_target_pairs={{0,16},{16,32},{32,48},{48,64},{64,80},{80,96},{96,112},{112,128},... | collective-permute-start | bytes 786440 | tf_op jit(solution)/shard_map/ppermute | solution.py:262
  5.9 0.0 collective-permute-done.1.pin
  5.9 1.9 %collective-permute-start.4 = (bf16[2,4,2,128,128]{4,3,2,1,0:T(8,128)(2,1)}, bf16[2,4,2,128,128]{4,3,2,1,0:T(8,128)(2,1)S(1)}, u32[]{:S(2)}, u32[]{:S(2)}) collective-permute-start(bf16[2,4,2,128,128]{4,3,2,1,0:T(8,128)(2,1)} %get-tuple-element.29.own), channel_id=1, source_target_pairs={{1,2},{2,1},{3,4},{4,3},{5,6},{6,5},{7,8},{8,7},{9,10},{10,9},{11,... | collective-permute-start | bytes 1572872 | tf_op jit(solution)/shard_map/ppermute | solution.py:265
  7.9 0.0 copy-done.3
  7.9 0.0 copy-done.4
  7.9 0.0 copy-done.8
  7.9 0.0 copy-done.9
  7.9 0.0 copy-start.10
  7.9 1.0 %copy-done.10 = bf16[2,4,2,128,128]{4,3,2,1,0:T(8,128)(2,1)S(1)} copy-done((bf16[2,4,2,128,128]{4,3,2,1,0:T(8,128)(2,1)S(1)}, bf16[2,4,2,128,128]{4,3,2,1,0:T(8,128)(2,1)}, u32[]{:S(2)}) %copy-start.10) | copy-done | bytes 524312
  9.0 2.8 %shard_map.110 = (bf16[10,4,128,128]{3,2,1,0:T(8,128)(2,1)S(1)}, bf16[6,2,128,128]{3,2,1,0:T(8,128)(2,1)S(1)}) custom-call(s32[2]{0:T(128)S(1)} %copy-done.4, bf16[2,4,2,128,128]{4,3,2,1,0:T(8,128)(2,1)S(1)} %copy-done.10, bf16[2,4,2,128,128]{4,3,2,1,0:T(8,128)(2,1)S(1)} %collective-permute-done.1.pin, bf16[3,3,3,128,128]{4,3,2,1,0:T(8,128)(2,1)S(1)} %copy-done.3, ...), custom_call_target="tpu_custom_call" | custom-call | flops 10000000000 | bytes 262144 | tf_op jit(solution)/shard_map/pallas_call | solution.py:239
  11.8 3.7 %collective-permute-done.pown = bf16[4,2,128,128]{3,2,1,0:T(8,128)(2,1)S(1)} collective-permute-done((bf16[4,2,128,128]{3,2,1,0:T(8,128)(2,1)}, bf16[4,2,128,128]{3,2,1,0:T(8,128)(2,1)S(1)}, u32[]{:S(2)}, u32[]{:S(2)}) %collective-permute-start) | collective-permute-done | bytes 262176 | tf_op jit(solution)/shard_map/ppermute | solution.py:262
  15.4 0.0 collective-permute-start.2
  15.5 2.1 %collective-permute-start.3 = (bf16[4,2,128,128]{3,2,1,0:T(8,128)(2,1)S(1)}, bf16[4,2,128,128]{3,2,1,0:T(8,128)(2,1)S(1)}, u32[]{:S(2)}, u32[]{:S(2)}) collective-permute-start(bf16[4,2,128,128]{3,2,1,0:T(8,128)(2,1)S(1)} %collective-permute-done.pown), channel_id=1, source_target_pairs={{1,2},{2,1},{3,4},{4,3},{5,6},{6,5},{7,8},{8,7},{9,10},{10,9},{11,... | collective-permute-start | bytes 786440 | tf_op jit(solution)/shard_map/ppermute | solution.py:279
  17.6 0.3 collective-permute-done.4.cross
  17.9 0.0 copy-start
  17.9 0.0 copy-start.1
  17.9 0.0 copy-start.2
  17.9 0.0 copy-start.5
  17.9 0.0 copy-start.7
  17.9 2.8 %shard_map.111 = (bf16[2,4,128,128]{3,2,1,0:T(8,128)(2,1)S(1)}, bf16[6,4,128,128]{3,2,1,0:T(8,128)(2,1)S(1)}) custom-call(s32[2]{0:T(128)S(1)} %copy-done.4, bf16[10,4,128,128]{3,2,1,0:T(8,128)(2,1)S(1)} %get-tuple-element.28.near, bf16[6,2,128,128]{3,2,1,0:T(8,128)(2,1)S(1)} %get-tuple-element.30.mid, ...), custom_call_target="tpu_custom_call" | custom-call | flops 1000000000 | bytes 262144 | tf_op jit(solution)/shard_map/pallas_call | solution.py:239
  20.7 0.0 copy-done
  20.7 0.0 copy-done.1
  20.7 0.0 copy-done.2
  20.7 0.0 copy-done.5
  20.7 0.0 copy-done.7
  20.7 0.0 copy-start.6
  20.7 1.9 %shard_map.112 = (f32[2,64,256]{2,1,0:T(8,128)S(1)}, f32[2,64,256]{2,1,0:T(8,128)S(1)}, f32[2,64,256]{2,1,0:T(8,128)S(1)}) custom-call(bf16[6,4,128,128]{3,2,1,0:T(8,128)(2,1)S(1)} %get-tuple-element.32.u2, bf16[2,4,2,128,128]{4,3,2,1,0:T(8,128)(2,1)S(1)} %copy-done.2, bf16[3,3,3,128,128]{4,3,2,1,0:T(8,128)(2,1)S(1)} %copy-done.1, f32[1,128]{1,0:T(1,128)S(1)} %bitcast.9, ...), custom_call_target="tpu_custom_call" | custom-call | flops 1000000000 | bytes 262144 | tf_op jit(solution)/shard_map/pallas_call | solution.py:239
  22.6 0.0 collective-permute-done.2.ppin
  22.6 1.7 %collective-permute-done.3.pcross = bf16[4,2,128,128]{3,2,1,0:T(8,128)(2,1)S(1)} collective-permute-done((bf16[4,2,128,128]{3,2,1,0:T(8,128)(2,1)S(1)}, bf16[4,2,128,128]{3,2,1,0:T(8,128)(2,1)S(1)}, u32[]{:S(2)}, u32[]{:S(2)}) %collective-permute-start.3) | collective-permute-done | bytes 262176 | tf_op jit(solution)/shard_map/ppermute | solution.py:279
  24.3 0.0 copy-done.6
  24.3 3.4 %shard_map.113 = (bf16[2,4,128,128]{3,2,1,0:T(8,128)(2,1)S(1)}, f32[2,2,136,128]{3,2,1,0:T(8,128)S(1)}, bf16[2,64,256]{2,1,0:T(8,128)(2,1)S(1)}) custom-call(s32[2]{0:T(128)S(1)} %copy-done.4, s32[2]{0:T(128)S(1)} %copy-done.6, bf16[10,4,128,128]{3,2,1,0:T(8,128)(2,1)S(1)} %get-tuple-element.28.near, ...), custom_call_target="tpu_custom_call" | custom-call | flops 1000000000 | bytes 262144 | tf_op jit(solution)/shard_map/pallas_call | solution.py:239
  27.7 1.9 %collective-permute-start.5 = (bf16[2,64,256]{2,1,0:T(8,128)(2,1)S(1)}, bf16[2,64,256]{2,1,0:T(8,128)(2,1)S(1)}, u32[]{:S(2)}, u32[]{:S(2)}) collective-permute-start(bf16[2,64,256]{2,1,0:T(8,128)(2,1)S(1)} %get-tuple-element.39), channel_id=1, source_target_pairs={{0,16},{16,32},{32,48},{48,64},{64,80},{80,96},{96,112},{112,128},... | collective-permute-start | bytes 196616 | tf_op jit(solution)/shard_map/ppermute | solution.py:300
  29.7 3.7 %shard_map.114 = (f32[2,2,64,256]{3,2,1,0:T(8,128)S(1)}, f32[2,2,64,256]{3,2,1,0:T(8,128)S(1)}) custom-call(s32[2]{0:T(128)S(1)} %copy-done.4, bf16[4,2,128,128]{3,2,1,0:T(8,128)(2,1)S(1)} %collective-permute-done.pown, bf16[4,2,128,128]{3,2,1,0:T(8,128)(2,1)S(1)} %collective-permute-done.2.ppin, bf16[4,2,128,128]{3,2,1,0:T(8,128)(2,1)S(1)} %collective-permute-done.3.pcross, ...), custom_call_target="tpu_custom_call" | custom-call | flops 4000000000 | bytes 262144 | tf_op jit(solution)/shard_map/pallas_call | solution.py:239
  33.4 2.6 %collective-permute-done.5.got = bf16[2,64,256]{2,1,0:T(8,128)(2,1)S(1)} collective-permute-done((bf16[2,64,256]{2,1,0:T(8,128)(2,1)S(1)}, bf16[2,64,256]{2,1,0:T(8,128)(2,1)S(1)}, u32[]{:S(2)}, u32[]{:S(2)}) %collective-permute-start.5) | collective-permute-done | bytes 65568 | tf_op jit(solution)/shard_map/ppermute | solution.py:300
  36.0 0.6 %shard_map.115 = bf16[2,2,64,256]{3,2,1,0:T(8,128)(2,1)S(1)} custom-call(s32[2]{0:T(128)S(1)} %copy-done.4, bf16[2,64,256]{2,1,0:T(8,128)(2,1)S(1)} %collective-permute-done.5.got, f32[2,2,64,256]{3,2,1,0:T(8,128)S(1)} %get-tuple-element.40.below), custom_call_target="tpu_custom_call" | custom-call | flops 1000000 | bytes 262144 | tf_op jit(solution)/shard_map/pallas_call | solution.py:239
  36.6 1.9 %collective-permute-start.6 = (bf16[2,2,64,256]{3,2,1,0:T(8,128)(2,1)S(1)}, bf16[2,2,64,256]{3,2,1,0:T(8,128)(2,1)S(1)}, u32[]{:S(2)}, u32[]{:S(2)}) collective-permute-start(bf16[2,2,64,256]{3,2,1,0:T(8,128)(2,1)S(1)} %shard_map.115), channel_id=1, source_target_pairs={{0,1},{1,2},{2,3},{3,4},{4,5},{5,6},{6,7},{7,8},{8,9},{9,10},{10,1... | collective-permute-start | bytes 393224 | tf_op jit(solution)/shard_map/ppermute | solution.py:302
  38.5 5.6 %collective-permute-done.6.above = bf16[2,2,64,256]{3,2,1,0:T(8,128)(2,1)S(1)} collective-permute-done((bf16[2,2,64,256]{3,2,1,0:T(8,128)(2,1)S(1)}, bf16[2,2,64,256]{3,2,1,0:T(8,128)(2,1)S(1)}, u32[]{:S(2)}, u32[]{:S(2)}) %collective-permute-start.6) | collective-permute-done | bytes 131104 | tf_op jit(solution)/shard_map/ppermute | solution.py:302
  44.1 1.2 %shard_map.116 = bf16[2,2,1,64,256]{4,3,2,1,0:T(8,128)(2,1)} custom-call(s32[2]{0:T(128)S(1)} %copy-done.4, s32[2]{0:T(128)S(1)} %copy-done.6, f32[2,2,64,256]{3,2,1,0:T(8,128)S(1)} %get-tuple-element.38.here, bf16[2,64,256]{2,1,0:T(8,128)(2,1)S(1)} %collective-permute-done.5.got, bf16[2,2,64,256]{3,2,1,0:T(8,128)(2,1)S(1)} %collective-permute-done.6.above), custom_call_target="tpu_custom_call" | custom-call | flops 1000000 | bytes 262144 | tf_op jit(solution)/shard_map/pallas_call | solution.py:239
Async XLA Ops:
  0.0 7.9 %copy-start.3 = (bf16[3,3,3,128,128]{4,3,2,1,0:T(8,128)(2,1)S(1)}, bf16[3,3,3,128,128]{4,3,2,1,0:T(8,128)(2,1)}, u32[]{:S(2)}) copy-start(bf16[3,3,3,128,128]{4,3,2,1,0:T(8,128)(2,1)} %wide.7) | copy-start | bytes 2654212
  0.0 7.9 %copy-start.4 = (s32[2]{0:T(128)S(1)}, s32[2]{0:T(128)}, u32[]{:S(2)}) copy-start(s32[2]{0:T(128)} %pred_.11) | copy-start | bytes 28
  0.0 7.9 %copy-start.8 = (f32[128]{0:T(128)S(1)}, f32[128]{0:T(128)}, u32[]{:S(2)}) copy-start(f32[128]{0:T(128)} %param.16) | copy-start | bytes 1540
  0.0 7.9 %copy-start.9 = (f32[128]{0:T(128)S(1)}, f32[128]{0:T(128)}, u32[]{:S(2)}) copy-start(f32[128]{0:T(128)} %param.17) | copy-start | bytes 1540
  2.5 3.4 %collective-permute-start.1 = (bf16[2,4,2,128,128]{4,3,2,1,0:T(8,128)(2,1)}, bf16[2,4,2,128,128]{4,3,2,1,0:T(8,128)(2,1)S(1)}, u32[]{:S(2)}, u32[]{:S(2)}) collective-permute-start(bf16[2,4,2,128,128]{4,3,2,1,0:T(8,128)(2,1)} %get-tuple-element.29.own), channel_id=1, source_target_pairs={{0,1},{1,0},{2,3},{3,2},{4,5},{5,4},{6,7},{7,6},{8,9},{9,8},{10,11... | collective-permute-start | bytes 1572872 | tf_op jit(solution)/shard_map/ppermute | solution.py:263
  2.5 12.9 %collective-permute-start = (bf16[4,2,128,128]{3,2,1,0:T(8,128)(2,1)}, bf16[4,2,128,128]{3,2,1,0:T(8,128)(2,1)S(1)}, u32[]{:S(2)}, u32[]{:S(2)}) collective-permute-start(bf16[4,2,128,128]{3,2,1,0:T(8,128)(2,1)} %get-tuple-element.23), channel_id=1, source_target_pairs={{0,16},{16,32},{32,48},{48,64},{64,80},{80,96},{96,112},{112,128},... | collective-permute-start | bytes 786440 | tf_op jit(solution)/shard_map/ppermute | solution.py:262
  5.9 11.9 %collective-permute-start.4 = (bf16[2,4,2,128,128]{4,3,2,1,0:T(8,128)(2,1)}, bf16[2,4,2,128,128]{4,3,2,1,0:T(8,128)(2,1)S(1)}, u32[]{:S(2)}, u32[]{:S(2)}) collective-permute-start(bf16[2,4,2,128,128]{4,3,2,1,0:T(8,128)(2,1)} %get-tuple-element.29.own), channel_id=1, source_target_pairs={{1,2},{2,1},{3,4},{4,3},{5,6},{6,5},{7,8},{8,7},{9,10},{10,9},{11,... | collective-permute-start | bytes 1572872 | tf_op jit(solution)/shard_map/ppermute | solution.py:265
  7.9 1.1 %copy-start.10 = (bf16[2,4,2,128,128]{4,3,2,1,0:T(8,128)(2,1)S(1)}, bf16[2,4,2,128,128]{4,3,2,1,0:T(8,128)(2,1)}, u32[]{:S(2)}) copy-start(bf16[2,4,2,128,128]{4,3,2,1,0:T(8,128)(2,1)} %get-tuple-element.29.own) | copy-start | bytes 1572868
  15.4 7.2 %collective-permute-start.2 = (bf16[4,2,128,128]{3,2,1,0:T(8,128)(2,1)S(1)}, bf16[4,2,128,128]{3,2,1,0:T(8,128)(2,1)S(1)}, u32[]{:S(2)}, u32[]{:S(2)}) collective-permute-start(bf16[4,2,128,128]{3,2,1,0:T(8,128)(2,1)S(1)} %collective-permute-done.pown), channel_id=1, source_target_pairs={{0,1},{1,0},{2,3},{3,2},{4,5},{5,4},{6,7},{7,6},{8,9},{9,8},{10,11... | collective-permute-start | bytes 786440 | tf_op jit(solution)/shard_map/ppermute | solution.py:278
  15.5 8.9 %collective-permute-start.3 = (bf16[4,2,128,128]{3,2,1,0:T(8,128)(2,1)S(1)}, bf16[4,2,128,128]{3,2,1,0:T(8,128)(2,1)S(1)}, u32[]{:S(2)}, u32[]{:S(2)}) collective-permute-start(bf16[4,2,128,128]{3,2,1,0:T(8,128)(2,1)S(1)} %collective-permute-done.pown), channel_id=1, source_target_pairs={{1,2},{2,1},{3,4},{4,3},{5,6},{6,5},{7,8},{8,7},{9,10},{10,9},{11,... | collective-permute-start | bytes 786440 | tf_op jit(solution)/shard_map/ppermute | solution.py:279
  17.9 2.8 %copy-start = (bf16[3,3,3,128,256]{4,3,2,1,0:T(8,128)(2,1)S(1)}, bf16[3,3,3,128,256]{4,3,2,1,0:T(8,128)(2,1)}, u32[]{:S(2)}) copy-start(bf16[3,3,3,128,256]{4,3,2,1,0:T(8,128)(2,1)} %param.20) | copy-start | bytes 5308420
  17.9 2.8 %copy-start.1 = (bf16[3,3,3,128,128]{4,3,2,1,0:T(8,128)(2,1)S(1)}, bf16[3,3,3,128,128]{4,3,2,1,0:T(8,128)(2,1)}, u32[]{:S(2)}) copy-start(bf16[3,3,3,128,128]{4,3,2,1,0:T(8,128)(2,1)} %wide_two.5) | copy-start | bytes 2654212
  17.9 2.8 %copy-start.2 = (bf16[2,4,2,128,128]{4,3,2,1,0:T(8,128)(2,1)S(1)}, bf16[2,4,2,128,128]{4,3,2,1,0:T(8,128)(2,1)}, u32[]{:S(2)}) copy-start(bf16[2,4,2,128,128]{4,3,2,1,0:T(8,128)(2,1)} %video.7) | copy-start | bytes 1572868
  17.9 2.8 %copy-start.5 = (f32[128]{0:T(128)S(1)}, f32[128]{0:T(128)}, u32[]{:S(2)}) copy-start(f32[128]{0:T(128)} %param.19) | copy-start | bytes 1540
  17.9 2.9 %copy-start.7 = (f32[256]{0:T(256)S(1)}, f32[256]{0:T(256)}, u32[]{:S(2)}) copy-start(f32[256]{0:T(256)} %param.21) | copy-start | bytes 3076
  20.7 3.6 %copy-start.6 = (s32[2]{0:T(128)S(1)}, s32[2]{0:T(128)}, u32[]{:S(2)}) copy-start(s32[2]{0:T(128)} %frames.5) | copy-start | bytes 28
  27.7 8.3 %collective-permute-start.5 = (bf16[2,64,256]{2,1,0:T(8,128)(2,1)S(1)}, bf16[2,64,256]{2,1,0:T(8,128)(2,1)S(1)}, u32[]{:S(2)}, u32[]{:S(2)}) collective-permute-start(bf16[2,64,256]{2,1,0:T(8,128)(2,1)S(1)} %get-tuple-element.39), channel_id=1, source_target_pairs={{0,16},{16,32},{32,48},{48,64},{64,80},{80,96},{96,112},{112,128},... | collective-permute-start | bytes 196616 | tf_op jit(solution)/shard_map/ppermute | solution.py:300
  36.6 7.5 %collective-permute-start.6 = (bf16[2,2,64,256]{3,2,1,0:T(8,128)(2,1)S(1)}, bf16[2,2,64,256]{3,2,1,0:T(8,128)(2,1)S(1)}, u32[]{:S(2)}, u32[]{:S(2)}) collective-permute-start(bf16[2,2,64,256]{3,2,1,0:T(8,128)(2,1)S(1)} %shard_map.115), channel_id=1, source_target_pairs={{0,1},{1,2},{2,3},{3,4},{4,5},{5,6},{6,7},{7,8},{8,9},{9,10},{10,1... | collective-permute-start | bytes 393224 | tf_op jit(solution)/shard_map/ppermute | solution.py:302

commit v5 on v4

--- a/solution.py
+++ b/solution.py
@@ -25,32 +25,41 @@
     return jnp.where(keep, value, jnp.zeros_like(value))
 
 
-def pair_weight(weight):
+def blocks(rows):
+    return jnp.concatenate([jnp.concatenate(row, axis=1) for row in rows], axis=0)
+
+
+def shared_weight(weight):
+    return blocks(
+        [[weight[kt, j - r, kw] for kw in range(3) for r in range(2)] for kt in range(3) for j in (1, 2)]
+    )
+
+
+def single_weight(weight, kh):
     zero = jnp.zeros((128, 128), BF16)
-    return jnp.concatenate(
+    return blocks(
         [
-            jnp.concatenate(
-                [weight[kt, j - r, kw] if 0 <= j - r <= 2 else zero for kw in range(3) for r in range(2)], axis=1
-            )
-            for kt in range(3)
-            for j in range(4)
-        ],
-        axis=0,
-    )
-
-
-def pair_conv(source, wide, frame, count, row):
-    m = count * 128
-    pieces = [
-        source[pl.ds(frame + kt, count), row + j].reshape(m, 128) for kt in range(3) for j in range(4)
-    ]
-    z = jnp.dot(jnp.concatenate(pieces, axis=1), pair_weight(wide), preferred_element_type=F32)
-    left = z[:, :256].reshape(count, 128, 256)
-    right = z[:, 512:].reshape(count, 128, 256)
-    edge = jnp.zeros((count, 1, 256), F32)
-    left = jnp.concatenate([edge, left[:, :127]], axis=1)
-    right = jnp.concatenate([right[:, 1:], edge], axis=1)
-    return left.reshape(m, 256) + z[:, 256:512] + right.reshape(m, 256)
+            [weight[f - t, kh, kw] if 0 <= f - t <= 2 else zero for kw in range(3) for t in range(2)]
+            for f in range(4)
+        ]
+    )
+
+
+def pair_conv(source, weight, frame, row):
+    shared = [source[pl.ds(frame + kt, 2), row + j].reshape(256, 128) for kt in range(3) for j in (1, 2)]
+    z = jnp.dot(jnp.concatenate(shared, axis=1), shared_weight(weight), preferred_element_type=F32)
+    ends = []
+    for at, kh in ((row, 0), (row + 3, 2)):
+        pieces = jnp.concatenate([source[frame + f, at] for f in range(4)], axis=1)
+        ends.append(jnp.dot(pieces, single_weight(weight, kh), preferred_element_type=F32))
+    taps = []
+    for kw in range(3):
+        end = blocks([[e[:, (kw * 2 + t) * 128 : (kw * 2 + t) * 128 + 128] for e in ends] for t in range(2)])
+        taps.append(z[:, kw * 256 : kw * 256 + 256] + end)
+    edge = jnp.zeros((2, 1, 256), F32)
+    left = jnp.concatenate([edge, taps[0].reshape(2, 128, 256)[:, :127]], axis=1)
+    right = jnp.concatenate([taps[2].reshape(2, 128, 256)[:, 1:], edge], axis=1)
+    return left.reshape(256, 256) + taps[1] + right.reshape(256, 256)
 
 
 def first_kernel(frames, video, gain, act, tail):
@@ -60,8 +69,8 @@
     tail[...] = act[jnp.where(frames[1] > 0, 1, 0)]
 
 
-def hidden_rows(source, wide, bias, gain, frame, row):
-    h = pair_conv(source, wide, frame, 2, row)
+def hidden_rows(source, weight, bias, gain, frame, row):
+    h = pair_conv(source, weight, frame, row)
     for r in range(2):
         v = activate(h[:, r * 128 : r * 128 + 128] + bias[...], gain[...])
         yield r, v.reshape(2, 128, 128)
@@ -76,8 +85,8 @@
     return value
 
 
-def summed_rows(u2, wide, bias, frame, video, slot, first, ys, at):
-    h = pair_conv(u2, wide, frame, 2, 0)
+def summed_rows(u2, weight, bias, frame, video, slot, first, ys, at):
+    h = pair_conv(u2, weight, frame, 0)
     for r in range(2):
         v = h[:, r * 128 : r * 128 + 128] + bias[...]
         y = video[slot, first : first + 2, r].reshape(256, 128).astype(F32) + v
@@ -88,7 +97,7 @@
     return jnp.concatenate([ys[frame, r, pl.ds(7 + kw, 64, stride=2)].astype(BF16) for kw in range(3)], axis=1)
 
 
-def mid_kernel(pred, own, pin, wide, bias_one, gain_two, near, mid):
+def mid_kernel(pred, own, pin, w_one, bias_one, gain_two, near, mid):
     keep = pred[1] >= 0
     parity = lax.rem(lax.axis_index("space"), 2)
     for src, at in ((own, 2 * parity), (pin, 2 - 2 * parity)):
@@ -99,11 +108,11 @@
                 if slot == 0 and f >= 2:
                     near[2 + f, pl.ds(at, 2)] = masked(keep, v)
     for frame, target in ((0, 0), (4, 2), (6, 4)):
-        for r, v in hidden_rows(near, wide, bias_one, gain_two, frame, 0):
+        for r, v in hidden_rows(near, w_one, bias_one, gain_two, frame, 0):
             mid[target : target + 2, r] = v.astype(BF16)
 
 
-def outer_kernel(pred, near, mid, cross, wide, bias_one, gain_two, u2a, u2b, ux):
+def outer_kernel(pred, near, mid, cross, w_one, bias_one, gain_two, u2a, u2b, ux):
     keep = pred[1] >= 0
     parity = lax.rem(lax.axis_index("space"), 2)
     at, other = 2 * parity, 2 - 2 * parity
@@ -115,7 +124,7 @@
             if slot == 0 and f >= 2:
                 ux[2 + f, pl.ds(at, 2)] = masked(keep, v)
     for frame, target in ((0, 0), (4, 2), (6, 4)):
-        for r, v in hidden_rows(ux, wide, bias_one, gain_two, frame, 0):
+        for r, v in hidden_rows(ux, w_one, bias_one, gain_two, frame, 0):
             v = inside(v, r == 0, r == 1).astype(BF16)
             if target == 0:
                 u2a[:, at + r] = v
@@ -148,10 +157,10 @@
     return here, below
 
 
-def second_kernel(u2, video, wide_two, bias_two, w_down, bias_down, here_b, below_b, sent_b, ys):
+def second_kernel(u2, video, w_two, bias_two, w_down, bias_down, here_b, below_b, sent_b, ys):
     ys[:, :, :8] = jnp.zeros((4, 2, 8, 128), F32)
     for half in range(2):
-        summed_rows(u2, wide_two, bias_two, 2 * half, video, 1, 2 * half, ys, 2 * half)
+        summed_rows(u2, w_two, bias_two, 2 * half, video, 1, 2 * half, ys, 2 * half)
     here, below = strided(ys, w_down)
     for t in range(2):
         here_b[t] = here[t] + bias_down[...]
@@ -162,7 +171,7 @@
 
 def context_kernel(
     pred, frames, near, cross, pown, ppin, pcross, u2a, sent_b, video,
-    wide, bias_one, gain_two, wide_two, bias_two, w_down,
+    w_one, bias_one, gain_two, w_two, bias_two, w_down,
     u2c, ya, sent,
     ux, us, ys,
 ):
@@ -175,10 +184,10 @@
     us[2:4] = u2a[...]
     ys[:, :, :8] = jnp.zeros((2, 2, 8, 128), F32)
     for row in (0, 2):
-        for r, v in hidden_rows(ux, wide, bias_one, gain_two, 0, row):
+        for r, v in hidden_rows(ux, w_one, bias_one, gain_two, 0, row):
             us[0:2, row + r] = inside(v, row + r == 0, row + r == 3).astype(BF16)
     u2c[...] = us[0:2]
-    summed_rows(us, wide_two, bias_two, 0, video, 0, 2, ys, 0)
+    summed_rows(us, w_two, bias_two, 0, video, 0, 2, ys, 0)
     ya[...] = ys[...]
     here, below = 0.0, 0.0
     for kt in range(2):
@@ -193,7 +202,7 @@
 
 def rest_kernel(
     pred, pown, ppin, pcross, u2c, u2a, ya, here_b, below_b, video,
-    wide, bias_one, gain_two, wide_two, bias_two, w_down, bias_down,
+    w_one, bias_one, gain_two, w_two, bias_two, w_down, bias_down,
     out, below_out,
     ux, ua, ys,
 ):
@@ -204,9 +213,9 @@
     ys[0:2, :, :8] = jnp.zeros((2, 2, 8, 128), F32)
     ys[2:4] = ya[...]
     for row in (0, 2):
-        for r, v in hidden_rows(ux, wide, bias_one, gain_two, 0, row):
+        for r, v in hidden_rows(ux, w_one, bias_one, gain_two, 0, row):
             ua[0:2, row + r] = masked(keep_a, inside(v, row + r == 0, row + r == 3)).astype(BF16)
-    summed_rows(ua, wide_two, bias_two, 0, video, 0, 0, ys, 0)
+    summed_rows(ua, w_two, bias_two, 0, video, 0, 0, ys, 0)
     here, below = strided(ys, w_down)
     for t in range(2):
         out[0, t] = here[t] + bias_down[...]

time: 45.6 us -> 45.1 us (0.989)
  Pallas kernels: 18.9 us -> 17 us
  waiting for transfers between devices: 13.8 us -> 15.3 us
    pallas_call x8, Pallas kernels: 18.9 us -> 17 us  [call(): pl.pallas_call(kernel, out_shape=[jax.ShapeDtypeStruct(shape, dtype) for...]
    ppermute x1, waiting for transfers between devices: 2.62 us -> 3.3 us  [local(): got = lax.ppermute(sent, 'block', onward)]
  transfers between devices with their start and end apart: 7 -> 7, of which waited for: 5 -> 5; matrix products, arithmetic and copies ran while one was open for 0% -> 0% of each run, Pallas kernels for 25% -> 22%
where the time goes in v5:
time: 45.1 us; the launch traced here: 44.8 us
  Pallas kernels  17 us (38%)
  waiting for transfers between devices  15.3 us (34%)
  starting transfers between devices  11.2 us (25%)
  local copies, waits for them, and re-layouts  1.09 us (2%)
    pallas_call x8, Pallas kernels, call(): pl.pallas_call(kernel, out_shape=[jax.ShapeDtypeStruct(shape, dtype) for...  17 us
    ppermute x1, waiting for transfers between devices, local(): lax.ppermute(below, 'space', [(i, i + 1) for i in range(n_space - 1)])  5.57 us
    ppermute x1, waiting for transfers between devices, local(): pown = lax.ppermute(tail, 'block', onward)  4.01 us
    ppermute x1, starting transfers between devices, local(): pown = lax.ppermute(tail, 'block', onward)  3.35 us
    ppermute x1, waiting for transfers between devices, local(): got = lax.ppermute(sent, 'block', onward)  3.3 us
    ppermute x1, waiting for transfers between devices, local(): pcross = lax.ppermute(pown, 'space', outer)  2.13 us
    ppermute x1, starting transfers between devices, local(): pcross = lax.ppermute(pown, 'space', outer)  2.12 us
    ppermute x1, starting transfers between devices, local(): got = lax.ppermute(sent, 'block', onward)  1.92 us
  transfers between devices with their start and end apart: 7, of which 5 were waited for; matrix products, arithmetic and copies ran while one was open for 0% of the time, Pallas kernels for 22%

profile of v5, /device:TPU:136, one launch (start us, length us, event | category | flops | bytes accessed | tf_op | source)
XLA Modules:
  0.0 44.8 jit_solution(17826811479354204103)
XLA Ops:
  0.0 0.0 copy-start.3
  0.0 0.0 copy-start.4
  0.0 0.0 copy-start.8
  0.0 0.0 copy-start.9
  0.0 2.5 %shard_map.109 = (bf16[2,4,2,128,128]{4,3,2,1,0:T(8,128)(2,1)}, bf16[4,2,128,128]{3,2,1,0:T(8,128)(2,1)}) custom-call(s32[2]{0:T(128)} %frames.5, bf16[2,4,2,128,128]{4,3,2,1,0:T(8,128)(2,1)} %video.7, f32[1,128]{1,0:T(1,128)} %bitcast.22), custom_call_target="tpu_custom_call" | custom-call | flops 1000000000 | bytes 262144 | tf_op jit(solution)/shard_map/pallas_call | solution.py:248
  2.5 0.0 collective-permute-start.1
  2.5 3.3 %collective-permute-start = (bf16[4,2,128,128]{3,2,1,0:T(8,128)(2,1)}, bf16[4,2,128,128]{3,2,1,0:T(8,128)(2,1)S(1)}, u32[]{:S(2)}, u32[]{:S(2)}) collective-permute-start(bf16[4,2,128,128]{3,2,1,0:T(8,128)(2,1)} %get-tuple-element.23), channel_id=1, source_target_pairs={{0,16},{16,32},{32,48},{48,64},{64,80},{80,96},{96,112},{112,128},... | collective-permute-start | bytes 786440 | tf_op jit(solution)/shard_map/ppermute | solution.py:271
  5.9 0.0 collective-permute-done.1.pin
  5.9 1.9 %collective-permute-start.4 = (bf16[2,4,2,128,128]{4,3,2,1,0:T(8,128)(2,1)}, bf16[2,4,2,128,128]{4,3,2,1,0:T(8,128)(2,1)S(1)}, u32[]{:S(2)}, u32[]{:S(2)}) collective-permute-start(bf16[2,4,2,128,128]{4,3,2,1,0:T(8,128)(2,1)} %get-tuple-element.29.own), channel_id=1, source_target_pairs={{1,2},{2,1},{3,4},{4,3},{5,6},{6,5},{7,8},{8,7},{9,10},{10,9},{11,... | collective-permute-start | bytes 1572872 | tf_op jit(solution)/shard_map/ppermute | solution.py:274
  7.8 0.0 copy-done.3
  7.8 0.0 copy-done.4
  7.8 0.0 copy-done.8
  7.9 0.0 copy-done.9
  7.9 0.0 copy-start.10
  7.9 1.0 %copy-done.10 = bf16[2,4,2,128,128]{4,3,2,1,0:T(8,128)(2,1)S(1)} copy-done((bf16[2,4,2,128,128]{4,3,2,1,0:T(8,128)(2,1)S(1)}, bf16[2,4,2,128,128]{4,3,2,1,0:T(8,128)(2,1)}, u32[]{:S(2)}) %copy-start.10) | copy-done | bytes 524312
  8.9 2.5 %shard_map.110 = (bf16[10,4,128,128]{3,2,1,0:T(8,128)(2,1)S(1)}, bf16[6,2,128,128]{3,2,1,0:T(8,128)(2,1)S(1)}) custom-call(s32[2]{0:T(128)S(1)} %copy-done.4, bf16[2,4,2,128,128]{4,3,2,1,0:T(8,128)(2,1)S(1)} %copy-done.10, bf16[2,4,2,128,128]{4,3,2,1,0:T(8,128)(2,1)S(1)} %collective-permute-done.1.pin, bf16[3,3,3,128,128]{4,3,2,1,0:T(8,128)(2,1)S(1)} %copy-done.3, ...), custom_call_target="tpu_custom_call" | custom-call | flops 10000000000 | bytes 262144 | tf_op jit(solution)/shard_map/pallas_call | solution.py:248
  11.4 4.0 %collective-permute-done.pown = bf16[4,2,128,128]{3,2,1,0:T(8,128)(2,1)S(1)} collective-permute-done((bf16[4,2,128,128]{3,2,1,0:T(8,128)(2,1)}, bf16[4,2,128,128]{3,2,1,0:T(8,128)(2,1)S(1)}, u32[]{:S(2)}, u32[]{:S(2)}) %collective-permute-start) | collective-permute-done | bytes 262176 | tf_op jit(solution)/shard_map/ppermute | solution.py:271
  15.4 0.0 collective-permute-start.2
  15.5 2.1 %collective-permute-start.3 = (bf16[4,2,128,128]{3,2,1,0:T(8,128)(2,1)S(1)}, bf16[4,2,128,128]{3,2,1,0:T(8,128)(2,1)S(1)}, u32[]{:S(2)}, u32[]{:S(2)}) collective-permute-start(bf16[4,2,128,128]{3,2,1,0:T(8,128)(2,1)S(1)} %collective-permute-done.pown), channel_id=1, source_target_pairs={{1,2},{2,1},{3,4},{4,3},{5,6},{6,5},{7,8},{8,7},{9,10},{10,9},{11,... | collective-permute-start | bytes 786440 | tf_op jit(solution)/shard_map/ppermute | solution.py:288
  17.6 0.2 collective-permute-done.4.cross
  17.8 0.0 copy-start
  17.8 0.0 copy-start.1
  17.8 0.0 copy-start.2
  17.8 0.0 copy-start.5
  17.8 0.0 copy-start.7
  17.8 2.5 %shard_map.111 = (bf16[2,4,128,128]{3,2,1,0:T(8,128)(2,1)S(1)}, bf16[6,4,128,128]{3,2,1,0:T(8,128)(2,1)S(1)}) custom-call(s32[2]{0:T(128)S(1)} %copy-done.4, bf16[10,4,128,128]{3,2,1,0:T(8,128)(2,1)S(1)} %get-tuple-element.28.near, bf16[6,2,128,128]{3,2,1,0:T(8,128)(2,1)S(1)} %get-tuple-element.30.mid, ...), custom_call_target="tpu_custom_call" | custom-call | flops 1000000000 | bytes 262144 | tf_op jit(solution)/shard_map/pallas_call | solution.py:248
  20.4 0.0 copy-done
  20.4 0.0 copy-done.1
  20.4 0.0 copy-done.2
  20.4 0.0 copy-done.5
  20.4 0.0 copy-done.7
  20.4 0.0 copy-start.6
  20.4 1.7 %shard_map.112 = (f32[2,64,256]{2,1,0:T(8,128)S(1)}, f32[2,64,256]{2,1,0:T(8,128)S(1)}, f32[2,64,256]{2,1,0:T(8,128)S(1)}) custom-call(bf16[6,4,128,128]{3,2,1,0:T(8,128)(2,1)S(1)} %get-tuple-element.32.u2, bf16[2,4,2,128,128]{4,3,2,1,0:T(8,128)(2,1)S(1)} %copy-done.2, bf16[3,3,3,128,128]{4,3,2,1,0:T(8,128)(2,1)S(1)} %copy-done.1, f32[1,128]{1,0:T(1,128)S(1)} %bitcast.9, ...), custom_call_target="tpu_custom_call" | custom-call | flops 1000000000 | bytes 262144 | tf_op jit(solution)/shard_map/pallas_call | solution.py:248
  22.2 0.0 collective-permute-done.2.ppin
  22.2 2.1 %collective-permute-done.3.pcross = bf16[4,2,128,128]{3,2,1,0:T(8,128)(2,1)S(1)} collective-permute-done((bf16[4,2,128,128]{3,2,1,0:T(8,128)(2,1)S(1)}, bf16[4,2,128,128]{3,2,1,0:T(8,128)(2,1)S(1)}, u32[]{:S(2)}, u32[]{:S(2)}) %collective-permute-start.3) | collective-permute-done | bytes 262176 | tf_op jit(solution)/shard_map/ppermute | solution.py:288
  24.3 0.0 copy-done.6
  24.3 2.9 %shard_map.113 = (bf16[2,4,128,128]{3,2,1,0:T(8,128)(2,1)S(1)}, f32[2,2,136,128]{3,2,1,0:T(8,128)S(1)}, bf16[2,64,256]{2,1,0:T(8,128)(2,1)S(1)}) custom-call(s32[2]{0:T(128)S(1)} %copy-done.4, s32[2]{0:T(128)S(1)} %copy-done.6, bf16[10,4,128,128]{3,2,1,0:T(8,128)(2,1)S(1)} %get-tuple-element.28.near, ...), custom_call_target="tpu_custom_call" | custom-call | flops 1000000000 | bytes 262144 | tf_op jit(solution)/shard_map/pallas_call | solution.py:248
  27.2 1.9 %collective-permute-start.5 = (bf16[2,64,256]{2,1,0:T(8,128)(2,1)S(1)}, bf16[2,64,256]{2,1,0:T(8,128)(2,1)S(1)}, u32[]{:S(2)}, u32[]{:S(2)}) collective-permute-start(bf16[2,64,256]{2,1,0:T(8,128)(2,1)S(1)} %get-tuple-element.39), channel_id=1, source_target_pairs={{0,16},{16,32},{32,48},{48,64},{64,80},{80,96},{96,112},{112,128},... | collective-permute-start | bytes 196616 | tf_op jit(solution)/shard_map/ppermute | solution.py:309
  29.2 3.0 %shard_map.114 = (f32[2,2,64,256]{3,2,1,0:T(8,128)S(1)}, f32[2,2,64,256]{3,2,1,0:T(8,128)S(1)}) custom-call(s32[2]{0:T(128)S(1)} %copy-done.4, bf16[4,2,128,128]{3,2,1,0:T(8,128)(2,1)S(1)} %collective-permute-done.pown, bf16[4,2,128,128]{3,2,1,0:T(8,128)(2,1)S(1)} %collective-permute-done.2.ppin, bf16[4,2,128,128]{3,2,1,0:T(8,128)(2,1)S(1)} %collective-permute-done.3.pcross, ...), custom_call_target="tpu_custom_call" | custom-call | flops 4000000000 | bytes 262144 | tf_op jit(solution)/shard_map/pallas_call | solution.py:248
  32.2 3.3 %collective-permute-done.5.got = bf16[2,64,256]{2,1,0:T(8,128)(2,1)S(1)} collective-permute-done((bf16[2,64,256]{2,1,0:T(8,128)(2,1)S(1)}, bf16[2,64,256]{2,1,0:T(8,128)(2,1)S(1)}, u32[]{:S(2)}, u32[]{:S(2)}) %collective-permute-start.5) | collective-permute-done | bytes 65568 | tf_op jit(solution)/shard_map/ppermute | solution.py:309
  35.5 0.6 %shard_map.115 = bf16[2,2,64,256]{3,2,1,0:T(8,128)(2,1)S(1)} custom-call(s32[2]{0:T(128)S(1)} %copy-done.4, bf16[2,64,256]{2,1,0:T(8,128)(2,1)S(1)} %collective-permute-done.5.got, f32[2,2,64,256]{3,2,1,0:T(8,128)S(1)} %get-tuple-element.40.below), custom_call_target="tpu_custom_call" | custom-call | flops 1000000 | bytes 262144 | tf_op jit(solution)/shard_map/pallas_call | solution.py:248
  36.1 1.9 %collective-permute-start.6 = (bf16[2,2,64,256]{3,2,1,0:T(8,128)(2,1)S(1)}, bf16[2,2,64,256]{3,2,1,0:T(8,128)(2,1)S(1)}, u32[]{:S(2)}, u32[]{:S(2)}) collective-permute-start(bf16[2,2,64,256]{3,2,1,0:T(8,128)(2,1)S(1)} %shard_map.115), channel_id=1, source_target_pairs={{0,1},{1,2},{2,3},{3,4},{4,5},{5,6},{6,7},{7,8},{8,9},{9,10},{10,1... | collective-permute-start | bytes 393224 | tf_op jit(solution)/shard_map/ppermute | solution.py:311
  38.0 5.6 %collective-permute-done.6.above = bf16[2,2,64,256]{3,2,1,0:T(8,128)(2,1)S(1)} collective-permute-done((bf16[2,2,64,256]{3,2,1,0:T(8,128)(2,1)S(1)}, bf16[2,2,64,256]{3,2,1,0:T(8,128)(2,1)S(1)}, u32[]{:S(2)}, u32[]{:S(2)}) %collective-permute-start.6) | collective-permute-done | bytes 131104 | tf_op jit(solution)/shard_map/ppermute | solution.py:311
  43.6 1.2 %shard_map.116 = bf16[2,2,1,64,256]{4,3,2,1,0:T(8,128)(2,1)} custom-call(s32[2]{0:T(128)S(1)} %copy-done.4, s32[2]{0:T(128)S(1)} %copy-done.6, f32[2,2,64,256]{3,2,1,0:T(8,128)S(1)} %get-tuple-element.38.here, bf16[2,64,256]{2,1,0:T(8,128)(2,1)S(1)} %collective-permute-done.5.got, bf16[2,2,64,256]{3,2,1,0:T(8,128)(2,1)S(1)} %collective-permute-done.6.above), custom_call_target="tpu_custom_call" | custom-call | flops 1000000 | bytes 262144 | tf_op jit(solution)/shard_map/pallas_call | solution.py:248
Async XLA Ops:
  0.0 7.8 %copy-start.3 = (bf16[3,3,3,128,128]{4,3,2,1,0:T(8,128)(2,1)S(1)}, bf16[3,3,3,128,128]{4,3,2,1,0:T(8,128)(2,1)}, u32[]{:S(2)}) copy-start(bf16[3,3,3,128,128]{4,3,2,1,0:T(8,128)(2,1)} %w_one.7) | copy-start | bytes 2654212
  0.0 7.8 %copy-start.4 = (s32[2]{0:T(128)S(1)}, s32[2]{0:T(128)}, u32[]{:S(2)}) copy-start(s32[2]{0:T(128)} %pred_.11) | copy-start | bytes 28
  0.0 7.8 %copy-start.8 = (f32[128]{0:T(128)S(1)}, f32[128]{0:T(128)}, u32[]{:S(2)}) copy-start(f32[128]{0:T(128)} %param.16) | copy-start | bytes 1540
  0.0 7.8 %copy-start.9 = (f32[128]{0:T(128)S(1)}, f32[128]{0:T(128)}, u32[]{:S(2)}) copy-start(f32[128]{0:T(128)} %param.17) | copy-start | bytes 1540
  2.5 3.4 %collective-permute-start.1 = (bf16[2,4,2,128,128]{4,3,2,1,0:T(8,128)(2,1)}, bf16[2,4,2,128,128]{4,3,2,1,0:T(8,128)(2,1)S(1)}, u32[]{:S(2)}, u32[]{:S(2)}) collective-permute-start(bf16[2,4,2,128,128]{4,3,2,1,0:T(8,128)(2,1)} %get-tuple-element.29.own), channel_id=1, source_target_pairs={{0,1},{1,0},{2,3},{3,2},{4,5},{5,4},{6,7},{7,6},{8,9},{9,8},{10,11... | collective-permute-start | bytes 1572872 | tf_op jit(solution)/shard_map/ppermute | solution.py:272
  2.5 12.9 %collective-permute-start = (bf16[4,2,128,128]{3,2,1,0:T(8,128)(2,1)}, bf16[4,2,128,128]{3,2,1,0:T(8,128)(2,1)S(1)}, u32[]{:S(2)}, u32[]{:S(2)}) collective-permute-start(bf16[4,2,128,128]{3,2,1,0:T(8,128)(2,1)} %get-tuple-element.23), channel_id=1, source_target_pairs={{0,16},{16,32},{32,48},{48,64},{64,80},{80,96},{96,112},{112,128},... | collective-permute-start | bytes 786440 | tf_op jit(solution)/shard_map/ppermute | solution.py:271
  5.9 11.9 %collective-permute-start.4 = (bf16[2,4,2,128,128]{4,3,2,1,0:T(8,128)(2,1)}, bf16[2,4,2,128,128]{4,3,2,1,0:T(8,128)(2,1)S(1)}, u32[]{:S(2)}, u32[]{:S(2)}) collective-permute-start(bf16[2,4,2,128,128]{4,3,2,1,0:T(8,128)(2,1)} %get-tuple-element.29.own), channel_id=1, source_target_pairs={{1,2},{2,1},{3,4},{4,3},{5,6},{6,5},{7,8},{8,7},{9,10},{10,9},{11,... | collective-permute-start | bytes 1572872 | tf_op jit(solution)/shard_map/ppermute | solution.py:274
  7.9 1.1 %copy-start.10 = (bf16[2,4,2,128,128]{4,3,2,1,0:T(8,128)(2,1)S(1)}, bf16[2,4,2,128,128]{4,3,2,1,0:T(8,128)(2,1)}, u32[]{:S(2)}) copy-start(bf16[2,4,2,128,128]{4,3,2,1,0:T(8,128)(2,1)} %get-tuple-element.29.own) | copy-start | bytes 1572868
  15.4 6.8 %collective-permute-start.2 = (bf16[4,2,128,128]{3,2,1,0:T(8,128)(2,1)S(1)}, bf16[4,2,128,128]{3,2,1,0:T(8,128)(2,1)S(1)}, u32[]{:S(2)}, u32[]{:S(2)}) collective-permute-start(bf16[4,2,128,128]{3,2,1,0:T(8,128)(2,1)S(1)} %collective-permute-done.pown), channel_id=1, source_target_pairs={{0,1},{1,0},{2,3},{3,2},{4,5},{5,4},{6,7},{7,6},{8,9},{9,8},{10,11... | collective-permute-start | bytes 786440 | tf_op jit(solution)/shard_map/ppermute | solution.py:287
  15.5 8.9 %collective-permute-start.3 = (bf16[4,2,128,128]{3,2,1,0:T(8,128)(2,1)S(1)}, bf16[4,2,128,128]{3,2,1,0:T(8,128)(2,1)S(1)}, u32[]{:S(2)}, u32[]{:S(2)}) collective-permute-start(bf16[4,2,128,128]{3,2,1,0:T(8,128)(2,1)S(1)} %collective-permute-done.pown), channel_id=1, source_target_pairs={{1,2},{2,1},{3,4},{4,3},{5,6},{6,5},{7,8},{8,7},{9,10},{10,9},{11,... | collective-permute-start | bytes 786440 | tf_op jit(solution)/shard_map/ppermute | solution.py:288
  17.8 2.6 %copy-start = (bf16[3,3,3,128,256]{4,3,2,1,0:T(8,128)(2,1)S(1)}, bf16[3,3,3,128,256]{4,3,2,1,0:T(8,128)(2,1)}, u32[]{:S(2)}) copy-start(bf16[3,3,3,128,256]{4,3,2,1,0:T(8,128)(2,1)} %param.20) | copy-start | bytes 5308420
  17.8 2.6 %copy-start.1 = (bf16[3,3,3,128,128]{4,3,2,1,0:T(8,128)(2,1)S(1)}, bf16[3,3,3,128,128]{4,3,2,1,0:T(8,128)(2,1)}, u32[]{:S(2)}) copy-start(bf16[3,3,3,128,128]{4,3,2,1,0:T(8,128)(2,1)} %w_two.5) | copy-start | bytes 2654212
  17.8 2.6 %copy-start.2 = (bf16[2,4,2,128,128]{4,3,2,1,0:T(8,128)(2,1)S(1)}, bf16[2,4,2,128,128]{4,3,2,1,0:T(8,128)(2,1)}, u32[]{:S(2)}) copy-start(bf16[2,4,2,128,128]{4,3,2,1,0:T(8,128)(2,1)} %video.7) | copy-start | bytes 1572868
  17.8 2.6 %copy-start.5 = (f32[128]{0:T(128)S(1)}, f32[128]{0:T(128)}, u32[]{:S(2)}) copy-start(f32[128]{0:T(128)} %param.19) | copy-start | bytes 1540
  17.8 2.6 %copy-start.7 = (f32[256]{0:T(256)S(1)}, f32[256]{0:T(256)}, u32[]{:S(2)}) copy-start(f32[256]{0:T(256)} %param.21) | copy-start | bytes 3076
  20.4 3.9 %copy-start.6 = (s32[2]{0:T(128)S(1)}, s32[2]{0:T(128)}, u32[]{:S(2)}) copy-start(s32[2]{0:T(128)} %frames.5) | copy-start | bytes 28
  27.2 8.3 %collective-permute-start.5 = (bf16[2,64,256]{2,1,0:T(8,128)(2,1)S(1)}, bf16[2,64,256]{2,1,0:T(8,128)(2,1)S(1)}, u32[]{:S(2)}, u32[]{:S(2)}) collective-permute-start(bf16[2,64,256]{2,1,0:T(8,128)(2,1)S(1)} %get-tuple-element.39), channel_id=1, source_target_pairs={{0,16},{16,32},{32,48},{48,64},{64,80},{80,96},{96,112},{112,128},... | collective-permute-start | bytes 196616 | tf_op jit(solution)/shard_map/ppermute | solution.py:309
  36.1 7.5 %collective-permute-start.6 = (bf16[2,2,64,256]{3,2,1,0:T(8,128)(2,1)S(1)}, bf16[2,2,64,256]{3,2,1,0:T(8,128)(2,1)S(1)}, u32[]{:S(2)}, u32[]{:S(2)}) collective-permute-start(bf16[2,2,64,256]{3,2,1,0:T(8,128)(2,1)S(1)} %shard_map.115), channel_id=1, source_target_pairs={{0,1},{1,2},{2,3},{3,4},{4,5},{5,6},{6,7},{7,8},{8,9},{9,10},{10,1... | collective-permute-start | bytes 393224 | tf_op jit(solution)/shard_map/ppermute | solution.py:311

commit v6 on v5

--- a/solution.py
+++ b/solution.py
@@ -219,24 +219,19 @@
     here, below = strided(ys, w_down)
     for t in range(2):
         out[0, t] = here[t] + bias_down[...]
-        below_out[0, t] = below[t]
+        below_out[0, t] = below[t].astype(BF16)
     out[1, 0] = here_b[0] + masked(keep_b, here[2])
     out[1, 1] = here_b[1]
-    below_out[1, 0] = below_b[0] + masked(keep_b, below[2])
-    below_out[1, 1] = below_b[1]
-
-
-def relay_kernel(pred, got, below, below_out):
-    below_out[...] = below[...].astype(BF16)
-    below_out[0, 0] = (below[0, 0] + masked(pred[0] >= 0, got[1].astype(F32))).astype(BF16)
-
-
-def last_kernel(pred, frames, here, got, above, out):
+    below_out[1, 0] = (below_b[0] + masked(keep_b, below[2])).astype(BF16)
+    below_out[1, 1] = below_b[1].astype(BF16)
+
+
+def last_kernel(pred, frames, here, got, above, passed, out):
     for slot in range(2):
         for t in range(2):
             v = here[slot, t] + above[slot, t].astype(F32)
             if slot == 0 and t == 0:
-                v = v + masked(pred[0] >= 0, got[0].astype(F32))
+                v = v + masked(pred[0] >= 0, got[0].astype(F32) + passed[1].astype(F32))
             out[slot, t, 0] = masked(2 * t < frames[slot], v).astype(BF16)
 
 
@@ -303,13 +298,16 @@
         (pred_slot, frames), (near, cross, *before_refs, u2a, sent_b, video, *norm, *stride), 10**9,
     )
     out, below = call(
-        rest_kernel, [both, both], [vmem(hidden(4, 6)), vmem(hidden(4)), vmem(ys)], (pred_slot,),
+        rest_kernel, [both, (both[0], BF16)], [vmem(hidden(4, 6)), vmem(hidden(4)), vmem(ys)], (pred_slot,),
         (*before_refs, u2c, u2a, ya, here_b, below_b, video, *norm, *stride, bias), 4 * 10**9,
     )
+    downward = [(i, i + 1) for i in range(n_space - 1)]
+    above = lax.ppermute(below, "space", downward)
     got = lax.ppermute(sent, "block", onward)
-    [below] = call(relay_kernel, [(both[0], BF16)], [], (pred_slot,), (got, below), 10**6)
-    above = lax.ppermute(below, "space", [(i, i + 1) for i in range(n_space - 1)])
-    [down] = call(last_kernel, [((2, 2, 1, 64, 256), BF16)], [], (pred_slot, frames), (out, got, above), 10**6)
+    passed = lax.ppermute(got, "space", downward)
+    [down] = call(
+        last_kernel, [((2, 2, 1, 64, 256), BF16)], [], (pred_slot, frames), (out, got, above, passed), 10**6
+    )
     return down
 
 

time: 45.1 us -> 48.8 us (1.082)
  waiting for transfers between devices: 15.3 us -> 17.5 us
  starting transfers between devices: 11.2 us -> 13.2 us
  Pallas kernels: 17 us -> 16.4 us
    ppermute x1, waiting for transfers between devices: 3.3 us -> 6.34 us  [local(): got = lax.ppermute(sent, 'block', onward)]
    ppermute x1 -> x2, starting transfers between devices: 1.92 us -> 3.83 us  [the longest x1 1.92 us: local(): above = lax.ppermute(below, 'space', downward)]
    ppermute x1 -> x2, waiting for transfers between devices: 5.57 us -> 4.86 us  [the longest x1 4.86 us: local(): passed = lax.ppermute(got, 'space', downward)]
    pallas_call x8 -> x7, Pallas kernels: 17 us -> 16.4 us  [call(): pl.pallas_call(kernel, out_shape=[jax.ShapeDtypeStruct(shape, dtype) for...]
  transfers between devices with their start and end apart: 7 -> 8, of which waited for: 5 -> 5; matrix products, arithmetic and copies ran while one was open for 0% -> 0% of each run, Pallas kernels for 22% -> 14%
where the time goes in v6:
time: 48.8 us; the launch traced here: 48.5 us
  waiting for transfers between devices  17.5 us (36%)
  Pallas kernels  16.4 us (34%)
  starting transfers between devices  13.2 us (27%)
  local copies, waits for them, and re-layouts  1.09 us (2%)
    pallas_call x7, Pallas kernels, call(): pl.pallas_call(kernel, out_shape=[jax.ShapeDtypeStruct(shape, dtype) for...  16.4 us
    ppermute x1, waiting for transfers between devices, local(): got = lax.ppermute(sent, 'block', onward)  6.34 us
    ppermute x1, waiting for transfers between devices, local(): passed = lax.ppermute(got, 'space', downward)  4.86 us
    ppermute x1, waiting for transfers between devices, local(): pown = lax.ppermute(tail, 'block', onward)  3.94 us
    ppermute x1, starting transfers between devices, local(): pown = lax.ppermute(tail, 'block', onward)  3.43 us
    ppermute x1, starting transfers between devices, local(): pcross = lax.ppermute(pown, 'space', outer)  2.12 us
    ppermute x1, waiting for transfers between devices, local(): pcross = lax.ppermute(pown, 'space', outer)  2.06 us
    ppermute x1, starting transfers between devices, local(): above = lax.ppermute(below, 'space', downward)  1.92 us
  transfers between devices with their start and end apart: 8, of which 5 were waited for; matrix products, arithmetic and copies ran while one was open for 0% of the time, Pallas kernels for 14%

profile of v6, /device:TPU:136, one launch (start us, length us, event | category | flops | bytes accessed | tf_op | source)
XLA Modules:
  0.0 48.5 jit_solution(11950790336019800880)
XLA Ops:
  0.0 0.0 copy-start.3
  0.0 0.0 copy-start.5
  0.0 0.0 copy-start.8
  0.0 0.0 copy-start.9
  0.0 2.5 %shard_map.109 = (bf16[2,4,2,128,128]{4,3,2,1,0:T(8,128)(2,1)}, bf16[4,2,128,128]{3,2,1,0:T(8,128)(2,1)}) custom-call(s32[2]{0:T(128)} %frames.5, bf16[2,4,2,128,128]{4,3,2,1,0:T(8,128)(2,1)} %video.7, f32[1,128]{1,0:T(1,128)} %bitcast.22), custom_call_target="tpu_custom_call" | custom-call | flops 1000000000 | bytes 262144 | tf_op jit(solution)/shard_map/pallas_call | solution.py:243
  2.5 0.0 collective-permute-start.1
  2.5 3.4 %collective-permute-start = (bf16[4,2,128,128]{3,2,1,0:T(8,128)(2,1)}, bf16[4,2,128,128]{3,2,1,0:T(8,128)(2,1)S(1)}, u32[]{:S(2)}, u32[]{:S(2)}) collective-permute-start(bf16[4,2,128,128]{3,2,1,0:T(8,128)(2,1)} %get-tuple-element.23), channel_id=1, source_target_pairs={{0,16},{16,32},{32,48},{48,64},{64,80},{80,96},{96,112},{112,128},... | collective-permute-start | bytes 786440 | tf_op jit(solution)/shard_map/ppermute | solution.py:266
  5.9 0.0 collective-permute-done.1.pin
  5.9 1.9 %collective-permute-start.4 = (bf16[2,4,2,128,128]{4,3,2,1,0:T(8,128)(2,1)}, bf16[2,4,2,128,128]{4,3,2,1,0:T(8,128)(2,1)S(1)}, u32[]{:S(2)}, u32[]{:S(2)}) collective-permute-start(bf16[2,4,2,128,128]{4,3,2,1,0:T(8,128)(2,1)} %get-tuple-element.29.own), channel_id=1, source_target_pairs={{1,2},{2,1},{3,4},{4,3},{5,6},{6,5},{7,8},{8,7},{9,10},{10,9},{11,... | collective-permute-start | bytes 1572872 | tf_op jit(solution)/shard_map/ppermute | solution.py:269
  7.9 0.0 copy-done.3
  7.9 0.0 copy-done.5
  7.9 0.0 copy-done.8
  7.9 0.0 copy-done.9
  7.9 0.0 copy-start.10
  7.9 1.0 %copy-done.10 = bf16[2,4,2,128,128]{4,3,2,1,0:T(8,128)(2,1)S(1)} copy-done((bf16[2,4,2,128,128]{4,3,2,1,0:T(8,128)(2,1)S(1)}, bf16[2,4,2,128,128]{4,3,2,1,0:T(8,128)(2,1)}, u32[]{:S(2)}) %copy-start.10) | copy-done | bytes 524312
  8.9 2.5 %shard_map.110 = (bf16[10,4,128,128]{3,2,1,0:T(8,128)(2,1)S(1)}, bf16[6,2,128,128]{3,2,1,0:T(8,128)(2,1)S(1)}) custom-call(s32[2]{0:T(128)S(1)} %copy-done.5, bf16[2,4,2,128,128]{4,3,2,1,0:T(8,128)(2,1)S(1)} %copy-done.10, bf16[2,4,2,128,128]{4,3,2,1,0:T(8,128)(2,1)S(1)} %collective-permute-done.1.pin, bf16[3,3,3,128,128]{4,3,2,1,0:T(8,128)(2,1)S(1)} %copy-done.3, ...), custom_call_target="tpu_custom_call" | custom-call | flops 10000000000 | bytes 262144 | tf_op jit(solution)/shard_map/pallas_call | solution.py:243
  11.5 3.9 %collective-permute-done.pown = bf16[4,2,128,128]{3,2,1,0:T(8,128)(2,1)S(1)} collective-permute-done((bf16[4,2,128,128]{3,2,1,0:T(8,128)(2,1)}, bf16[4,2,128,128]{3,2,1,0:T(8,128)(2,1)S(1)}, u32[]{:S(2)}, u32[]{:S(2)}) %collective-permute-start) | collective-permute-done | bytes 262176 | tf_op jit(solution)/shard_map/ppermute | solution.py:266
  15.4 0.0 collective-permute-start.2
  15.4 2.1 %collective-permute-start.3 = (bf16[4,2,128,128]{3,2,1,0:T(8,128)(2,1)S(1)}, bf16[4,2,128,128]{3,2,1,0:T(8,128)(2,1)S(1)}, u32[]{:S(2)}, u32[]{:S(2)}) collective-permute-start(bf16[4,2,128,128]{3,2,1,0:T(8,128)(2,1)S(1)} %collective-permute-done.pown), channel_id=1, source_target_pairs={{1,2},{2,1},{3,4},{4,3},{5,6},{6,5},{7,8},{8,7},{9,10},{10,9},{11,... | collective-permute-start | bytes 786440 | tf_op jit(solution)/shard_map/ppermute | solution.py:283
  17.5 0.3 collective-permute-done.4.cross
  17.9 0.0 copy-start
  17.9 0.0 copy-start.1
  17.9 0.0 copy-start.2
  17.9 0.0 copy-start.4
  17.9 0.0 copy-start.7
  17.9 2.5 %shard_map.111 = (bf16[2,4,128,128]{3,2,1,0:T(8,128)(2,1)S(1)}, bf16[6,4,128,128]{3,2,1,0:T(8,128)(2,1)S(1)}) custom-call(s32[2]{0:T(128)S(1)} %copy-done.5, bf16[10,4,128,128]{3,2,1,0:T(8,128)(2,1)S(1)} %get-tuple-element.28.near, bf16[6,2,128,128]{3,2,1,0:T(8,128)(2,1)S(1)} %get-tuple-element.30.mid, ...), custom_call_target="tpu_custom_call" | custom-call | flops 1000000000 | bytes 262144 | tf_op jit(solution)/shard_map/pallas_call | solution.py:243
  20.4 0.0 copy-done
  20.4 0.0 copy-done.1
  20.4 0.0 copy-done.2
  20.4 0.0 copy-done.4
  20.5 0.0 copy-done.7
  20.5 0.0 copy-start.6
  20.5 1.7 %shard_map.112 = (f32[2,64,256]{2,1,0:T(8,128)S(1)}, f32[2,64,256]{2,1,0:T(8,128)S(1)}, f32[2,64,256]{2,1,0:T(8,128)S(1)}) custom-call(bf16[6,4,128,128]{3,2,1,0:T(8,128)(2,1)S(1)} %get-tuple-element.32.u2, bf16[2,4,2,128,128]{4,3,2,1,0:T(8,128)(2,1)S(1)} %copy-done.2, bf16[3,3,3,128,128]{4,3,2,1,0:T(8,128)(2,1)S(1)} %copy-done.1, f32[1,128]{1,0:T(1,128)S(1)} %bitcast.9, ...), custom_call_target="tpu_custom_call" | custom-call | flops 1000000000 | bytes 262144 | tf_op jit(solution)/shard_map/pallas_call | solution.py:243
  22.2 0.0 collective-permute-done.2.ppin
  22.2 2.1 %collective-permute-done.3.pcross = bf16[4,2,128,128]{3,2,1,0:T(8,128)(2,1)S(1)} collective-permute-done((bf16[4,2,128,128]{3,2,1,0:T(8,128)(2,1)S(1)}, bf16[4,2,128,128]{3,2,1,0:T(8,128)(2,1)S(1)}, u32[]{:S(2)}, u32[]{:S(2)}) %collective-permute-start.3) | collective-permute-done | bytes 262176 | tf_op jit(solution)/shard_map/ppermute | solution.py:283
  24.3 0.0 copy-done.6
  24.3 2.9 %shard_map.113 = (bf16[2,4,128,128]{3,2,1,0:T(8,128)(2,1)S(1)}, f32[2,2,136,128]{3,2,1,0:T(8,128)S(1)}, bf16[2,64,256]{2,1,0:T(8,128)(2,1)S(1)}) custom-call(s32[2]{0:T(128)S(1)} %copy-done.5, s32[2]{0:T(128)S(1)} %copy-done.6, bf16[10,4,128,128]{3,2,1,0:T(8,128)(2,1)S(1)} %get-tuple-element.28.near, ...), custom_call_target="tpu_custom_call" | custom-call | flops 1000000000 | bytes 262144 | tf_op jit(solution)/shard_map/pallas_call | solution.py:243
  27.2 3.0 %shard_map.114 = (f32[2,2,64,256]{3,2,1,0:T(8,128)S(1)}, bf16[2,2,64,256]{3,2,1,0:T(8,128)(2,1)S(1)}) custom-call(s32[2]{0:T(128)S(1)} %copy-done.5, bf16[4,2,128,128]{3,2,1,0:T(8,128)(2,1)S(1)} %collective-permute-done.pown, bf16[4,2,128,128]{3,2,1,0:T(8,128)(2,1)S(1)} %collective-permute-done.2.ppin, ...), custom_call_target="tpu_custom_call" | custom-call | flops 4000000000 | bytes 262144 | tf_op jit(solution)/shard_map/pallas_call | solution.py:243
  30.3 1.9 %collective-permute-start.6 = (bf16[2,2,64,256]{3,2,1,0:T(8,128)(2,1)S(1)}, bf16[2,2,64,256]{3,2,1,0:T(8,128)(2,1)S(1)}, u32[]{:S(2)}, u32[]{:S(2)}) collective-permute-start(bf16[2,2,64,256]{3,2,1,0:T(8,128)(2,1)S(1)} %get-tuple-element.40), channel_id=1, source_target_pairs={{0,1},{1,2},{2,3},{3,4},{4,5},{5,6},{6,7},{7,8},{8,9},{9,10},{10,1... | collective-permute-start | bytes 393224 | tf_op jit(solution)/shard_map/ppermute | solution.py:305
  32.2 1.9 %collective-permute-start.5 = (bf16[2,64,256]{2,1,0:T(8,128)(2,1)S(1)}, bf16[2,64,256]{2,1,0:T(8,128)(2,1)S(1)}, u32[]{:S(2)}, u32[]{:S(2)}) collective-permute-start(bf16[2,64,256]{2,1,0:T(8,128)(2,1)S(1)} %get-tuple-element.39), channel_id=1, source_target_pairs={{0,16},{16,32},{32,48},{48,64},{64,80},{80,96},{96,112},{112,128},... | collective-permute-start | bytes 196616 | tf_op jit(solution)/shard_map/ppermute | solution.py:306
  34.1 6.3 %collective-permute-done.5.got = bf16[2,64,256]{2,1,0:T(8,128)(2,1)S(1)} collective-permute-done((bf16[2,64,256]{2,1,0:T(8,128)(2,1)S(1)}, bf16[2,64,256]{2,1,0:T(8,128)(2,1)S(1)}, u32[]{:S(2)}, u32[]{:S(2)}) %collective-permute-start.5) | collective-permute-done | bytes 65568 | tf_op jit(solution)/shard_map/ppermute | solution.py:306
  40.5 1.9 %collective-permute-start.7 = (bf16[2,64,256]{2,1,0:T(8,128)(2,1)S(1)}, bf16[2,64,256]{2,1,0:T(8,128)(2,1)S(1)}, u32[]{:S(2)}, u32[]{:S(2)}) collective-permute-start(bf16[2,64,256]{2,1,0:T(8,128)(2,1)S(1)} %collective-permute-done.5.got), channel_id=1, source_target_pairs={{0,1},{1,2},{2,3},{3,4},{4,5},{5,6},{6,7},{7,8},{8,9},{9,10},{10,1... | collective-permute-start | bytes 196616 | tf_op jit(solution)/shard_map/ppermute | solution.py:307
  42.4 0.0 collective-permute-done.6.above
  42.4 4.9 %collective-permute-done.7.passed = bf16[2,64,256]{2,1,0:T(8,128)(2,1)S(1)} collective-permute-done((bf16[2,64,256]{2,1,0:T(8,128)(2,1)S(1)}, bf16[2,64,256]{2,1,0:T(8,128)(2,1)S(1)}, u32[]{:S(2)}, u32[]{:S(2)}) %collective-permute-start.7) | collective-permute-done | bytes 65568 | tf_op jit(solution)/shard_map/ppermute | solution.py:307
  47.2 1.2 %shard_map.115 = bf16[2,2,1,64,256]{4,3,2,1,0:T(8,128)(2,1)} custom-call(s32[2]{0:T(128)S(1)} %copy-done.5, s32[2]{0:T(128)S(1)} %copy-done.6, f32[2,2,64,256]{3,2,1,0:T(8,128)S(1)} %get-tuple-element.38.here, bf16[2,64,256]{2,1,0:T(8,128)(2,1)S(1)} %collective-permute-done.5.got, bf16[2,2,64,256]{3,2,1,0:T(8,128)(2,1)S(1)} %collective-permute-done.6.above, ...), custom_call_target="tpu_custom_call" | custom-call | flops 1000000 | bytes 262144 | tf_op jit(solution)/shard_map/pallas_call | solution.py:243
Async XLA Ops:
  0.0 7.9 %copy-start.3 = (bf16[3,3,3,128,128]{4,3,2,1,0:T(8,128)(2,1)S(1)}, bf16[3,3,3,128,128]{4,3,2,1,0:T(8,128)(2,1)}, u32[]{:S(2)}) copy-start(bf16[3,3,3,128,128]{4,3,2,1,0:T(8,128)(2,1)} %w_one.7) | copy-start | bytes 2654212
  0.0 7.9 %copy-start.5 = (s32[2]{0:T(128)S(1)}, s32[2]{0:T(128)}, u32[]{:S(2)}) copy-start(s32[2]{0:T(128)} %pred_.9) | copy-start | bytes 28
  0.0 7.9 %copy-start.8 = (f32[128]{0:T(128)S(1)}, f32[128]{0:T(128)}, u32[]{:S(2)}) copy-start(f32[128]{0:T(128)} %param.16) | copy-start | bytes 1540
  0.0 7.9 %copy-start.9 = (f32[128]{0:T(128)S(1)}, f32[128]{0:T(128)}, u32[]{:S(2)}) copy-start(f32[128]{0:T(128)} %param.17) | copy-start | bytes 1540
  2.5 3.4 %collective-permute-start.1 = (bf16[2,4,2,128,128]{4,3,2,1,0:T(8,128)(2,1)}, bf16[2,4,2,128,128]{4,3,2,1,0:T(8,128)(2,1)S(1)}, u32[]{:S(2)}, u32[]{:S(2)}) collective-permute-start(bf16[2,4,2,128,128]{4,3,2,1,0:T(8,128)(2,1)} %get-tuple-element.29.own), channel_id=1, source_target_pairs={{0,1},{1,0},{2,3},{3,2},{4,5},{5,4},{6,7},{7,6},{8,9},{9,8},{10,11... | collective-permute-start | bytes 1572872 | tf_op jit(solution)/shard_map/ppermute | solution.py:267
  2.5 12.9 %collective-permute-start = (bf16[4,2,128,128]{3,2,1,0:T(8,128)(2,1)}, bf16[4,2,128,128]{3,2,1,0:T(8,128)(2,1)S(1)}, u32[]{:S(2)}, u32[]{:S(2)}) collective-permute-start(bf16[4,2,128,128]{3,2,1,0:T(8,128)(2,1)} %get-tuple-element.23), channel_id=1, source_target_pairs={{0,16},{16,32},{32,48},{48,64},{64,80},{80,96},{96,112},{112,128},... | collective-permute-start | bytes 786440 | tf_op jit(solution)/shard_map/ppermute | solution.py:266
  5.9 11.9 %collective-permute-start.4 = (bf16[2,4,2,128,128]{4,3,2,1,0:T(8,128)(2,1)}, bf16[2,4,2,128,128]{4,3,2,1,0:T(8,128)(2,1)S(1)}, u32[]{:S(2)}, u32[]{:S(2)}) collective-permute-start(bf16[2,4,2,128,128]{4,3,2,1,0:T(8,128)(2,1)} %get-tuple-element.29.own), channel_id=1, source_target_pairs={{1,2},{2,1},{3,4},{4,3},{5,6},{6,5},{7,8},{8,7},{9,10},{10,9},{11,... | collective-permute-start | bytes 1572872 | tf_op jit(solution)/shard_map/ppermute | solution.py:269
  7.9 1.1 %copy-start.10 = (bf16[2,4,2,128,128]{4,3,2,1,0:T(8,128)(2,1)S(1)}, bf16[2,4,2,128,128]{4,3,2,1,0:T(8,128)(2,1)}, u32[]{:S(2)}) copy-start(bf16[2,4,2,128,128]{4,3,2,1,0:T(8,128)(2,1)} %get-tuple-element.29.own) | copy-start | bytes 1572868
  15.4 6.8 %collective-permute-start.2 = (bf16[4,2,128,128]{3,2,1,0:T(8,128)(2,1)S(1)}, bf16[4,2,128,128]{3,2,1,0:T(8,128)(2,1)S(1)}, u32[]{:S(2)}, u32[]{:S(2)}) collective-permute-start(bf16[4,2,128,128]{3,2,1,0:T(8,128)(2,1)S(1)} %collective-permute-done.pown), channel_id=1, source_target_pairs={{0,1},{1,0},{2,3},{3,2},{4,5},{5,4},{6,7},{7,6},{8,9},{9,8},{10,11... | collective-permute-start | bytes 786440 | tf_op jit(solution)/shard_map/ppermute | solution.py:282
  15.4 8.9 %collective-permute-start.3 = (bf16[4,2,128,128]{3,2,1,0:T(8,128)(2,1)S(1)}, bf16[4,2,128,128]{3,2,1,0:T(8,128)(2,1)S(1)}, u32[]{:S(2)}, u32[]{:S(2)}) collective-permute-start(bf16[4,2,128,128]{3,2,1,0:T(8,128)(2,1)S(1)} %collective-permute-done.pown), channel_id=1, source_target_pairs={{1,2},{2,1},{3,4},{4,3},{5,6},{6,5},{7,8},{8,7},{9,10},{10,9},{11,... | collective-permute-start | bytes 786440 | tf_op jit(solution)/shard_map/ppermute | solution.py:283
  17.9 2.6 %copy-start = (bf16[3,3,3,128,256]{4,3,2,1,0:T(8,128)(2,1)S(1)}, bf16[3,3,3,128,256]{4,3,2,1,0:T(8,128)(2,1)}, u32[]{:S(2)}) copy-start(bf16[3,3,3,128,256]{4,3,2,1,0:T(8,128)(2,1)} %param.20) | copy-start | bytes 5308420
  17.9 2.6 %copy-start.1 = (bf16[3,3,3,128,128]{4,3,2,1,0:T(8,128)(2,1)S(1)}, bf16[3,3,3,128,128]{4,3,2,1,0:T(8,128)(2,1)}, u32[]{:S(2)}) copy-start(bf16[3,3,3,128,128]{4,3,2,1,0:T(8,128)(2,1)} %w_two.5) | copy-start | bytes 2654212
  17.9 2.6 %copy-start.2 = (bf16[2,4,2,128,128]{4,3,2,1,0:T(8,128)(2,1)S(1)}, bf16[2,4,2,128,128]{4,3,2,1,0:T(8,128)(2,1)}, u32[]{:S(2)}) copy-start(bf16[2,4,2,128,128]{4,3,2,1,0:T(8,128)(2,1)} %video.7) | copy-start | bytes 1572868
  17.9 2.6 %copy-start.4 = (f32[128]{0:T(128)S(1)}, f32[128]{0:T(128)}, u32[]{:S(2)}) copy-start(f32[128]{0:T(128)} %param.19) | copy-start | bytes 1540
  17.9 2.6 %copy-start.7 = (f32[256]{0:T(256)S(1)}, f32[256]{0:T(256)}, u32[]{:S(2)}) copy-start(f32[256]{0:T(256)} %param.21) | copy-start | bytes 3076
  20.5 3.8 %copy-start.6 = (s32[2]{0:T(128)S(1)}, s32[2]{0:T(128)}, u32[]{:S(2)}) copy-start(s32[2]{0:T(128)} %frames.5) | copy-start | bytes 28
  30.3 12.1 %collective-permute-start.6 = (bf16[2,2,64,256]{3,2,1,0:T(8,128)(2,1)S(1)}, bf16[2,2,64,256]{3,2,1,0:T(8,128)(2,1)S(1)}, u32[]{:S(2)}, u32[]{:S(2)}) collective-permute-start(bf16[2,2,64,256]{3,2,1,0:T(8,128)(2,1)S(1)} %get-tuple-element.40), channel_id=1, source_target_pairs={{0,1},{1,2},{2,3},{3,4},{4,5},{5,6},{6,7},{7,8},{8,9},{9,10},{10,1... | collective-permute-start | bytes 393224 | tf_op jit(solution)/shard_map/ppermute | solution.py:305
  32.2 8.3 %collective-permute-start.5 = (bf16[2,64,256]{2,1,0:T(8,128)(2,1)S(1)}, bf16[2,64,256]{2,1,0:T(8,128)(2,1)S(1)}, u32[]{:S(2)}, u32[]{:S(2)}) collective-permute-start(bf16[2,64,256]{2,1,0:T(8,128)(2,1)S(1)} %get-tuple-element.39), channel_id=1, source_target_pairs={{0,16},{16,32},{32,48},{48,64},{64,80},{80,96},{96,112},{112,128},... | collective-permute-start | bytes 196616 | tf_op jit(solution)/shard_map/ppermute | solution.py:306
  40.5 6.8 %collective-permute-start.7 = (bf16[2,64,256]{2,1,0:T(8,128)(2,1)S(1)}, bf16[2,64,256]{2,1,0:T(8,128)(2,1)S(1)}, u32[]{:S(2)}, u32[]{:S(2)}) collective-permute-start(bf16[2,64,256]{2,1,0:T(8,128)(2,1)S(1)} %collective-permute-done.5.got), channel_id=1, source_target_pairs={{0,1},{1,2},{2,3},{3,4},{4,5},{5,6},{6,7},{7,8},{8,9},{9,10},{10,1... | collective-permute-start | bytes 196616 | tf_op jit(solution)/shard_map/ppermute | solution.py:307

commit v7 on v5

--- a/solution.py
+++ b/solution.py
@@ -141,39 +141,49 @@
         ux[at, pl.ds(row, 2)] = masked(keep, src[frame])
 
 
-def strided(ys, w_down):
-    rows = {(f, r): columns(ys, f, r) for f in range(4) for r in range(2)}
-    here, below = {}, {}
-    for kt, read, goes in ((0, (0, 2), (1, 2)), (1, (1, 3), (1, 2)), (2, (0, 2), (0, 1))):
-        upper, under = (jnp.concatenate([rows[f, r] for f in read], axis=0) for r in range(2))
-        parts = (
-            (here, jnp.dot(jnp.concatenate([upper, under], axis=1), w_down[kt, 384:], preferred_element_type=F32)),
-            (below, jnp.dot(under, w_down[kt, :384], preferred_element_type=F32)),
-        )
-        for i, t in enumerate(goes):
-            for sums, value in parts:
-                part = value[i * 64 : i * 64 + 64]
-                sums[t] = sums[t] + part if t in sums else part
+READS = ((0, (0,), (1,)), (1, (1,), (1,)), (2, (0, 2), (0, 1)))
+
+
+def strided(slots, w_down, part):
+    sums = {}
+    for kt, read, goes in READS:
+        under = jnp.concatenate([columns(ys, f, 1) for ys in slots for f in read], axis=0)
+        if part == 0:
+            upper = jnp.concatenate([columns(ys, f, 0) for ys in slots for f in read], axis=0)
+            under, weight = jnp.concatenate([upper, under], axis=1), w_down[kt, 384:]
+        else:
+            weight = w_down[kt, :384]
+        value = jnp.dot(under, weight, preferred_element_type=F32)
+        for slot in range(2):
+            for i, t in enumerate(goes):
+                at = (slot * len(read) + i) * 64
+                piece = value[at : at + 64]
+                sums[slot, t] = sums[slot, t] + piece if (slot, t) in sums else piece
+    return sums
+
+
+def successor(ys, frame, w_down):
+    here, below = 0.0, 0.0
+    for kt in range(2):
+        upper, under = columns(ys, frame + kt, 0), columns(ys, frame + kt, 1)
+        both = jnp.concatenate([upper, under], axis=1)
+        here = here + jnp.dot(both, w_down[kt, 384:], preferred_element_type=F32)
+        below = below + jnp.dot(under, w_down[kt, :384], preferred_element_type=F32)
     return here, below
 
 
-def second_kernel(u2, video, w_two, bias_two, w_down, bias_down, here_b, below_b, sent_b, ys):
+def second_kernel(u2, video, w_two, bias_two, w_down, ys, sent_b):
     ys[:, :, :8] = jnp.zeros((4, 2, 8, 128), F32)
-    for half in range(2):
+    for half in (1, 0):
         summed_rows(u2, w_two, bias_two, 2 * half, video, 1, 2 * half, ys, 2 * half)
-    here, below = strided(ys, w_down)
-    for t in range(2):
-        here_b[t] = here[t] + bias_down[...]
-        below_b[t] = below[t]
-    sent_b[0] = here[2]
-    sent_b[1] = below[2]
+    sent_b[0], sent_b[1] = successor(ys, 2, w_down)
 
 
 def context_kernel(
     pred, frames, near, cross, pown, ppin, pcross, u2a, sent_b, video,
     w_one, bias_one, gain_two, w_two, bias_two, w_down,
-    u2c, ya, sent,
-    ux, us, ys,
+    u2c, ys, sent, sent_a,
+    ux, us,
 ):
     keep = pred[0] >= 0
     parity = lax.rem(lax.axis_index("space"), 2)
@@ -188,55 +198,53 @@
             us[0:2, row + r] = inside(v, row + r == 0, row + r == 3).astype(BF16)
     u2c[...] = us[0:2]
     summed_rows(us, w_two, bias_two, 0, video, 0, 2, ys, 0)
-    ya[...] = ys[...]
-    here, below = 0.0, 0.0
-    for kt in range(2):
-        upper, under = columns(ys, kt, 0), columns(ys, kt, 1)
-        both = jnp.concatenate([upper, under], axis=1)
-        here = here + jnp.dot(both, w_down[kt, 384:], preferred_element_type=F32)
-        below = below + jnp.dot(under, w_down[kt, :384], preferred_element_type=F32)
+    here, below = successor(ys, 0, w_down)
+    sent_a[0] = here
+    sent_a[1] = below
     second = frames[1] > 0
     sent[0] = jnp.where(second, sent_b[0], here).astype(BF16)
     sent[1] = jnp.where(second, sent_b[1], below).astype(BF16)
 
 
 def rest_kernel(
-    pred, pown, ppin, pcross, u2c, u2a, ya, here_b, below_b, video,
-    w_one, bias_one, gain_two, w_two, bias_two, w_down, bias_down,
-    out, below_out,
-    ux, ua, ys,
+    pred, pown, ppin, pcross, u2c, ya, video, w_one, bias_one, gain_two, w_two, bias_two, ys, ux, ua
 ):
-    keep_a, keep_b = pred[0] >= 0, pred[1] >= 0
+    keep = pred[0] >= 0
     for f in range(4):
-        before((pown, ppin, pcross), f, keep_a, ux, f)
+        before((pown, ppin, pcross), f, keep, ux, f)
     ua[2:4] = u2c[...]
     ys[0:2, :, :8] = jnp.zeros((2, 2, 8, 128), F32)
     ys[2:4] = ya[...]
     for row in (0, 2):
         for r, v in hidden_rows(ux, w_one, bias_one, gain_two, 0, row):
-            ua[0:2, row + r] = masked(keep_a, inside(v, row + r == 0, row + r == 3)).astype(BF16)
+            ua[0:2, row + r] = masked(keep, inside(v, row + r == 0, row + r == 3)).astype(BF16)
     summed_rows(ua, w_two, bias_two, 0, video, 0, 0, ys, 0)
-    here, below = strided(ys, w_down)
-    for t in range(2):
-        out[0, t] = here[t] + bias_down[...]
-        below_out[0, t] = below[t]
-    out[1, 0] = here_b[0] + masked(keep_b, here[2])
-    out[1, 1] = here_b[1]
-    below_out[1, 0] = below_b[0] + masked(keep_b, below[2])
-    below_out[1, 1] = below_b[1]
-
-
-def relay_kernel(pred, got, below, below_out):
-    below_out[...] = below[...].astype(BF16)
-    below_out[0, 0] = (below[0, 0] + masked(pred[0] >= 0, got[1].astype(F32))).astype(BF16)
-
-
-def last_kernel(pred, frames, here, got, above, out):
+
+
+def joined(pred, sums, sent_a, got, part):
+    sums[0, 0] += masked(pred[0] >= 0, got[part].astype(F32))
+    sums[1, 0] += masked(pred[1] >= 0, sent_a[part])
+    return sums
+
+
+def relay_kernel(pred, ysa, ysb, sent_a, got, w_down, below):
+    sums = joined(pred, strided((ysa, ysb), w_down, 1), sent_a, got, 1)
+    for slot in range(2):
+        for t in range(2):
+            below[slot, t] = sums[slot, t].astype(BF16)
+
+
+def here_kernel(pred, ysa, ysb, sent_a, got, w_down, bias_down, out):
+    sums = joined(pred, strided((ysa, ysb), w_down, 0), sent_a, got, 0)
+    for slot in range(2):
+        for t in range(2):
+            out[slot, t] = sums[slot, t] + bias_down[...]
+
+
+def last_kernel(frames, here, above, out):
     for slot in range(2):
         for t in range(2):
             v = here[slot, t] + above[slot, t].astype(F32)
-            if slot == 0 and t == 0:
-                v = v + masked(pred[0] >= 0, got[0].astype(F32))
             out[slot, t, 0] = masked(2 * t < frames[slot], v).astype(BF16)
 
 
@@ -291,25 +299,25 @@
         (near, mid, cross, *norm), OUTER,
     )
     before_refs = (pown, ppin, pcross)
-    bias = down_bias.reshape(1, 256)
-    one = ((2, 64, 256), F32)
+    down_weight = down_weight.reshape(3, 1152, 256)
+    pair = ((2, 64, 256), F32)
     ys = ((4, 2, 136, 128), F32)
-    here_b, below_b, sent_b = call(
-        second_kernel, [one, one, one], [vmem(ys)], (), (u2b, video, *stride, bias), SECOND
-    )
     ya = ((2,) + ys[0][1:], F32)
-    u2c, ya, sent = call(
-        context_kernel, [hidden(2), ya, ((2, 64, 256), BF16)], [vmem(hidden(4, 6)), vmem(hidden(4)), vmem(ya)],
+    ysb, sent_b = call(second_kernel, [ys, pair], [], (), (u2b, video, *stride), SECOND)
+    u2c, ya, sent, sent_a = call(
+        context_kernel, [hidden(2), ya, (pair[0], BF16), pair], [vmem(hidden(4, 6)), vmem(hidden(4))],
         (pred_slot, frames), (near, cross, *before_refs, u2a, sent_b, video, *norm, *stride), 10**9,
     )
-    out, below = call(
-        rest_kernel, [both, both], [vmem(hidden(4, 6)), vmem(hidden(4)), vmem(ys)], (pred_slot,),
-        (*before_refs, u2c, u2a, ya, here_b, below_b, video, *norm, *stride, bias), 4 * 10**9,
+    [ysa] = call(
+        rest_kernel, [ys], [vmem(hidden(4, 6)), vmem(hidden(4))], (pred_slot,),
+        (*before_refs, u2c, ya, video, *norm, *stride[:2]), 4 * 10**9,
     )
     got = lax.ppermute(sent, "block", onward)
-    [below] = call(relay_kernel, [(both[0], BF16)], [], (pred_slot,), (got, below), 10**6)
+    ends = (ysa, ysb, sent_a, got, down_weight)
+    [below] = call(relay_kernel, [(both[0], BF16)], [], (pred_slot,), ends, 10**6)
     above = lax.ppermute(below, "space", [(i, i + 1) for i in range(n_space - 1)])
-    [down] = call(last_kernel, [((2, 2, 1, 64, 256), BF16)], [], (pred_slot, frames), (out, got, above), 10**6)
+    [out] = call(here_kernel, [both], [], (pred_slot,), (*ends, down_bias.reshape(1, 256)), 10**9)
+    [down] = call(last_kernel, [((2, 2, 1, 64, 256), BF16)], [], (frames,), (out, above), 10**6)
     return down
 
 

time: 45.1 us -> 45.4 us (level)
  Pallas kernels: 17 us -> 17.5 us
    ppermute x1, waiting for transfers between devices: 5.57 us -> 4.63 us  [local(): lax.ppermute(below, 'space', [(i, i + 1) for i in range(n_space - 1)])]
    pallas_call x8 -> x9, Pallas kernels: 17 us -> 17.5 us  [call(): pl.pallas_call(kernel, out_shape=[jax.ShapeDtypeStruct(shape, dtype) for...]
where the time goes in v7:
time: 45.4 us; the launch traced here: 45.1 us
  Pallas kernels  17.5 us (39%)
  waiting for transfers between devices  15.1 us (33%)
  starting transfers between devices  11.2 us (25%)
  local copies, waits for them, and re-layouts  1.09 us (2%)
    pallas_call x9, Pallas kernels, call(): pl.pallas_call(kernel, out_shape=[jax.ShapeDtypeStruct(shape, dtype) for...  17.5 us
    ppermute x1, waiting for transfers between devices, local(): lax.ppermute(below, 'space', [(i, i + 1) for i in range(n_space - 1)])  4.63 us
    ppermute x1, waiting for transfers between devices, local(): pown = lax.ppermute(tail, 'block', onward)  4.01 us
    ppermute x1, waiting for transfers between devices, local(): got = lax.ppermute(sent, 'block', onward)  3.69 us
    ppermute x1, starting transfers between devices, local(): pown = lax.ppermute(tail, 'block', onward)  3.35 us
    ppermute x1, waiting for transfers between devices, local(): pcross = lax.ppermute(pown, 'space', outer)  2.5 us
    ppermute x1, starting transfers between devices, local(): pcross = lax.ppermute(pown, 'space', outer)  2.12 us
    ppermute x1, starting transfers between devices, local(): got = lax.ppermute(sent, 'block', onward)  1.92 us
  transfers between devices with their start and end apart: 7, of which 5 were waited for; matrix products, arithmetic and copies ran while one was open for 0% of the time, Pallas kernels for 22%

profile of v7, /device:TPU:136, one launch (start us, length us, event | category | flops | bytes accessed | tf_op | source)
XLA Modules:
  0.0 45.1 jit_solution(11942056422476093580)
XLA Ops:
  0.0 0.0 copy-start.3
  0.0 0.0 copy-start.6
  0.0 0.0 copy-start.7
  0.0 0.0 copy-start.8
  0.0 2.5 %shard_map.109 = (bf16[2,4,2,128,128]{4,3,2,1,0:T(8,128)(2,1)}, bf16[4,2,128,128]{3,2,1,0:T(8,128)(2,1)}) custom-call(s32[2]{0:T(128)} %frames.5, bf16[2,4,2,128,128]{4,3,2,1,0:T(8,128)(2,1)} %video.7, f32[1,128]{1,0:T(1,128)} %bitcast.22), custom_call_target="tpu_custom_call" | custom-call | flops 1000000000 | bytes 262144 | tf_op jit(solution)/shard_map/pallas_call | solution.py:256
  2.5 0.0 collective-permute-start.1
  2.5 3.3 %collective-permute-start = (bf16[4,2,128,128]{3,2,1,0:T(8,128)(2,1)}, bf16[4,2,128,128]{3,2,1,0:T(8,128)(2,1)S(1)}, u32[]{:S(2)}, u32[]{:S(2)}) collective-permute-start(bf16[4,2,128,128]{3,2,1,0:T(8,128)(2,1)} %get-tuple-element.21), channel_id=1, source_target_pairs={{0,16},{16,32},{32,48},{48,64},{64,80},{80,96},{96,112},{112,128},... | collective-permute-start | bytes 786440 | tf_op jit(solution)/shard_map/ppermute | solution.py:279
  5.9 0.0 collective-permute-done.1.pin
  5.9 1.9 %collective-permute-start.4 = (bf16[2,4,2,128,128]{4,3,2,1,0:T(8,128)(2,1)}, bf16[2,4,2,128,128]{4,3,2,1,0:T(8,128)(2,1)S(1)}, u32[]{:S(2)}, u32[]{:S(2)}) collective-permute-start(bf16[2,4,2,128,128]{4,3,2,1,0:T(8,128)(2,1)} %get-tuple-element.27.own), channel_id=1, source_target_pairs={{1,2},{2,1},{3,4},{4,3},{5,6},{6,5},{7,8},{8,7},{9,10},{10,9},{11,... | collective-permute-start | bytes 1572872 | tf_op jit(solution)/shard_map/ppermute | solution.py:282
  7.8 0.0 copy-done.3
  7.8 0.0 copy-done.6
  7.8 0.0 copy-done.7
  7.9 0.0 copy-done.8
  7.9 0.0 copy-start.9
  7.9 1.0 %copy-done.9 = bf16[2,4,2,128,128]{4,3,2,1,0:T(8,128)(2,1)S(1)} copy-done((bf16[2,4,2,128,128]{4,3,2,1,0:T(8,128)(2,1)S(1)}, bf16[2,4,2,128,128]{4,3,2,1,0:T(8,128)(2,1)}, u32[]{:S(2)}) %copy-start.9) | copy-done | bytes 524312
  8.9 2.5 %shard_map.110 = (bf16[10,4,128,128]{3,2,1,0:T(8,128)(2,1)S(1)}, bf16[6,2,128,128]{3,2,1,0:T(8,128)(2,1)S(1)}) custom-call(s32[2]{0:T(128)S(1)} %copy-done.6, bf16[2,4,2,128,128]{4,3,2,1,0:T(8,128)(2,1)S(1)} %copy-done.9, bf16[2,4,2,128,128]{4,3,2,1,0:T(8,128)(2,1)S(1)} %collective-permute-done.1.pin, bf16[3,3,3,128,128]{4,3,2,1,0:T(8,128)(2,1)S(1)} %copy-done.3, ...), custom_call_target="tpu_custom_call" | custom-call | flops 10000000000 | bytes 262144 | tf_op jit(solution)/shard_map/pallas_call | solution.py:256
  11.4 4.0 %collective-permute-done.pown = bf16[4,2,128,128]{3,2,1,0:T(8,128)(2,1)S(1)} collective-permute-done((bf16[4,2,128,128]{3,2,1,0:T(8,128)(2,1)}, bf16[4,2,128,128]{3,2,1,0:T(8,128)(2,1)S(1)}, u32[]{:S(2)}, u32[]{:S(2)}) %collective-permute-start) | collective-permute-done | bytes 262176 | tf_op jit(solution)/shard_map/ppermute | solution.py:279
  15.5 0.0 collective-permute-start.2
  15.5 2.1 %collective-permute-start.3 = (bf16[4,2,128,128]{3,2,1,0:T(8,128)(2,1)S(1)}, bf16[4,2,128,128]{3,2,1,0:T(8,128)(2,1)S(1)}, u32[]{:S(2)}, u32[]{:S(2)}) collective-permute-start(bf16[4,2,128,128]{3,2,1,0:T(8,128)(2,1)S(1)} %collective-permute-done.pown), channel_id=1, source_target_pairs={{1,2},{2,1},{3,4},{4,3},{5,6},{6,5},{7,8},{8,7},{9,10},{10,9},{11,... | collective-permute-start | bytes 786440 | tf_op jit(solution)/shard_map/ppermute | solution.py:296
  17.6 0.2 collective-permute-done.4.cross
  17.8 0.0 copy-start
  17.8 0.0 copy-start.1
  17.8 0.0 copy-start.2
  17.8 0.0 copy-start.4
  17.8 2.5 %shard_map.111 = (bf16[2,4,128,128]{3,2,1,0:T(8,128)(2,1)S(1)}, bf16[6,4,128,128]{3,2,1,0:T(8,128)(2,1)S(1)}) custom-call(s32[2]{0:T(128)S(1)} %copy-done.6, bf16[10,4,128,128]{3,2,1,0:T(8,128)(2,1)S(1)} %get-tuple-element.26.near, bf16[6,2,128,128]{3,2,1,0:T(8,128)(2,1)S(1)} %get-tuple-element.28.mid, ...), custom_call_target="tpu_custom_call" | custom-call | flops 1000000000 | bytes 262144 | tf_op jit(solution)/shard_map/pallas_call | solution.py:256
  20.4 0.0 copy-done
  20.4 0.0 copy-done.1
  20.4 0.0 copy-done.2
  20.4 0.0 copy-done.4
  20.4 0.0 copy-start.5
  20.4 1.4 %shard_map.112 = (f32[4,2,136,128]{3,2,1,0:T(8,128)S(1)}, f32[2,64,256]{2,1,0:T(8,128)S(1)}) custom-call(bf16[6,4,128,128]{3,2,1,0:T(8,128)(2,1)S(1)} %get-tuple-element.30.u2, bf16[2,4,2,128,128]{4,3,2,1,0:T(8,128)(2,1)S(1)} %copy-done.2, bf16[3,3,3,128,128]{4,3,2,1,0:T(8,128)(2,1)S(1)} %copy-done.1, f32[1,128]{1,0:T(1,128)S(1)} %bitcast.10, ...), custom_call_target="tpu_custom_call" | custom-call | flops 1000000000 | bytes 262144 | tf_op jit(solution)/shard_map/pallas_call | solution.py:256
  21.8 0.0 collective-permute-done.2.ppin
  21.8 2.5 %collective-permute-done.3.pcross = bf16[4,2,128,128]{3,2,1,0:T(8,128)(2,1)S(1)} collective-permute-done((bf16[4,2,128,128]{3,2,1,0:T(8,128)(2,1)S(1)}, bf16[4,2,128,128]{3,2,1,0:T(8,128)(2,1)S(1)}, u32[]{:S(2)}, u32[]{:S(2)}) %collective-permute-start.3) | collective-permute-done | bytes 262176 | tf_op jit(solution)/shard_map/ppermute | solution.py:296
  24.3 0.0 copy-done.5
  24.4 2.9 %shard_map.113 = (bf16[2,4,128,128]{3,2,1,0:T(8,128)(2,1)S(1)}, f32[2,2,136,128]{3,2,1,0:T(8,128)S(1)}, bf16[2,64,256]{2,1,0:T(8,128)(2,1)S(1)}, f32[2,64,256]{2,1,0:T(8,128)S(1)}) custom-call(s32[2]{0:T(128)S(1)} %copy-done.6, s32[2]{0:T(128)S(1)} %copy-done.5, bf16[10,4,128,128]{3,2,1,0:T(8,128)(2,1)S(1)} %get-tuple-element.26.near, ...), custom_call_target="tpu_custom_call" | custom-call | flops 1000000000 | bytes 262144 | tf_op jit(solution)/shard_map/pallas_call | solution.py:256
  27.2 1.9 %collective-permute-start.5 = (bf16[2,64,256]{2,1,0:T(8,128)(2,1)S(1)}, bf16[2,64,256]{2,1,0:T(8,128)(2,1)S(1)}, u32[]{:S(2)}, u32[]{:S(2)}) collective-permute-start(bf16[2,64,256]{2,1,0:T(8,128)(2,1)S(1)} %get-tuple-element.36), channel_id=1, source_target_pairs={{0,16},{16,32},{32,48},{48,64},{64,80},{80,96},{96,112},{112,128},... | collective-permute-start | bytes 196616 | tf_op jit(solution)/shard_map/ppermute | solution.py:315
  29.2 2.6 %shard_map.114.ysa = f32[4,2,136,128]{3,2,1,0:T(8,128)S(1)} custom-call(s32[2]{0:T(128)S(1)} %copy-done.6, bf16[4,2,128,128]{3,2,1,0:T(8,128)(2,1)S(1)} %collective-permute-done.pown, bf16[4,2,128,128]{3,2,1,0:T(8,128)(2,1)S(1)} %collective-permute-done.2.ppin, bf16[4,2,128,128]{3,2,1,0:T(8,128)(2,1)S(1)} %collective-permute-done.3.pcross, ...), custom_call_target="tpu_custom_call" | custom-call | flops 4000000000 | bytes 262144 | tf_op jit(solution)/shard_map/pallas_call | solution.py:256
  31.8 0.0 copy-start.10
  31.8 3.7 %collective-permute-done.5.got = bf16[2,64,256]{2,1,0:T(8,128)(2,1)S(1)} collective-permute-done((bf16[2,64,256]{2,1,0:T(8,128)(2,1)S(1)}, bf16[2,64,256]{2,1,0:T(8,128)(2,1)S(1)}, u32[]{:S(2)}, u32[]{:S(2)}) %collective-permute-start.5) | collective-permute-done | bytes 65568 | tf_op jit(solution)/shard_map/ppermute | solution.py:315
  35.5 0.8 %shard_map.116 = bf16[2,2,64,256]{3,2,1,0:T(8,128)(2,1)S(1)} custom-call(s32[2]{0:T(128)S(1)} %copy-done.6, f32[4,2,136,128]{3,2,1,0:T(8,128)S(1)} %shard_map.114.ysa, f32[4,2,136,128]{3,2,1,0:T(8,128)S(1)} %get-tuple-element.34.ysb, f32[2,64,256]{2,1,0:T(8,128)S(1)} %get-tuple-element.35.sent_a, bf16[2,64,256]{2,1,0:T(8,128)(2,1)S(1)} %collective-permute-done.5.got, ...), custom_call_target="tpu_custom_call" | custom-call | flops 1000000 | bytes 262144 | tf_op jit(solution)/shard_map/pallas_call | solution.py:256
  36.4 1.9 %collective-permute-start.6 = (bf16[2,2,64,256]{3,2,1,0:T(8,128)(2,1)S(1)}, bf16[2,2,64,256]{3,2,1,0:T(8,128)(2,1)S(1)}, u32[]{:S(2)}, u32[]{:S(2)}) collective-permute-start(bf16[2,2,64,256]{3,2,1,0:T(8,128)(2,1)S(1)} %shard_map.116), channel_id=1, source_target_pairs={{0,1},{1,2},{2,3},{3,4},{4,5},{5,6},{6,7},{7,8},{8,9},{9,10},{10,1... | collective-permute-start | bytes 393224 | tf_op jit(solution)/shard_map/ppermute | solution.py:318
  38.3 0.0 copy-done.10
  38.3 0.9 %shard_map.115.here = f32[2,2,64,256]{3,2,1,0:T(8,128)S(1)} custom-call(s32[2]{0:T(128)S(1)} %copy-done.6, f32[4,2,136,128]{3,2,1,0:T(8,128)S(1)} %shard_map.114.ysa, f32[4,2,136,128]{3,2,1,0:T(8,128)S(1)} %get-tuple-element.34.ysb, f32[2,64,256]{2,1,0:T(8,128)S(1)} %get-tuple-element.35.sent_a, bf16[2,64,256]{2,1,0:T(8,128)(2,1)S(1)} %collective-permute-done.5.got, ...), custom_call_target="tpu_custom_call" | custom-call | flops 1000000000 | bytes 262144 | tf_op jit(solution)/shard_map/pallas_call | solution.py:256
  39.2 4.6 %collective-permute-done.6.above = bf16[2,2,64,256]{3,2,1,0:T(8,128)(2,1)S(1)} collective-permute-done((bf16[2,2,64,256]{3,2,1,0:T(8,128)(2,1)S(1)}, bf16[2,2,64,256]{3,2,1,0:T(8,128)(2,1)S(1)}, u32[]{:S(2)}, u32[]{:S(2)}) %collective-permute-start.6) | collective-permute-done | bytes 131104 | tf_op jit(solution)/shard_map/ppermute | solution.py:318
  43.9 1.2 %shard_map.117 = bf16[2,2,1,64,256]{4,3,2,1,0:T(8,128)(2,1)} custom-call(s32[2]{0:T(128)S(1)} %copy-done.5, f32[2,2,64,256]{3,2,1,0:T(8,128)S(1)} %shard_map.115.here, bf16[2,2,64,256]{3,2,1,0:T(8,128)(2,1)S(1)} %collective-permute-done.6.above), custom_call_target="tpu_custom_call" | custom-call | flops 1000000 | bytes 262144 | tf_op jit(solution)/shard_map/pallas_call | solution.py:256
Async XLA Ops:
  0.0 7.8 %copy-start.3 = (bf16[3,3,3,128,128]{4,3,2,1,0:T(8,128)(2,1)S(1)}, bf16[3,3,3,128,128]{4,3,2,1,0:T(8,128)(2,1)}, u32[]{:S(2)}) copy-start(bf16[3,3,3,128,128]{4,3,2,1,0:T(8,128)(2,1)} %w_one.7) | copy-start | bytes 2654212
  0.0 7.8 %copy-start.6 = (s32[2]{0:T(128)S(1)}, s32[2]{0:T(128)}, u32[]{:S(2)}) copy-start(s32[2]{0:T(128)} %pred_.11) | copy-start | bytes 28
  0.0 7.8 %copy-start.7 = (f32[128]{0:T(128)S(1)}, f32[128]{0:T(128)}, u32[]{:S(2)}) copy-start(f32[128]{0:T(128)} %param.16) | copy-start | bytes 1540
  0.0 7.9 %copy-start.8 = (f32[128]{0:T(128)S(1)}, f32[128]{0:T(128)}, u32[]{:S(2)}) copy-start(f32[128]{0:T(128)} %param.17) | copy-start | bytes 1540
  2.5 3.4 %collective-permute-start.1 = (bf16[2,4,2,128,128]{4,3,2,1,0:T(8,128)(2,1)}, bf16[2,4,2,128,128]{4,3,2,1,0:T(8,128)(2,1)S(1)}, u32[]{:S(2)}, u32[]{:S(2)}) collective-permute-start(bf16[2,4,2,128,128]{4,3,2,1,0:T(8,128)(2,1)} %get-tuple-element.27.own), channel_id=1, source_target_pairs={{0,1},{1,0},{2,3},{3,2},{4,5},{5,4},{6,7},{7,6},{8,9},{9,8},{10,11... | collective-permute-start | bytes 1572872 | tf_op jit(solution)/shard_map/ppermute | solution.py:280
  2.5 12.9 %collective-permute-start = (bf16[4,2,128,128]{3,2,1,0:T(8,128)(2,1)}, bf16[4,2,128,128]{3,2,1,0:T(8,128)(2,1)S(1)}, u32[]{:S(2)}, u32[]{:S(2)}) collective-permute-start(bf16[4,2,128,128]{3,2,1,0:T(8,128)(2,1)} %get-tuple-element.21), channel_id=1, source_target_pairs={{0,16},{16,32},{32,48},{48,64},{64,80},{80,96},{96,112},{112,128},... | collective-permute-start | bytes 786440 | tf_op jit(solution)/shard_map/ppermute | solution.py:279
  5.9 11.9 %collective-permute-start.4 = (bf16[2,4,2,128,128]{4,3,2,1,0:T(8,128)(2,1)}, bf16[2,4,2,128,128]{4,3,2,1,0:T(8,128)(2,1)S(1)}, u32[]{:S(2)}, u32[]{:S(2)}) collective-permute-start(bf16[2,4,2,128,128]{4,3,2,1,0:T(8,128)(2,1)} %get-tuple-element.27.own), channel_id=1, source_target_pairs={{1,2},{2,1},{3,4},{4,3},{5,6},{6,5},{7,8},{8,7},{9,10},{10,9},{11,... | collective-permute-start | bytes 1572872 | tf_op jit(solution)/shard_map/ppermute | solution.py:282
  7.9 1.1 %copy-start.9 = (bf16[2,4,2,128,128]{4,3,2,1,0:T(8,128)(2,1)S(1)}, bf16[2,4,2,128,128]{4,3,2,1,0:T(8,128)(2,1)}, u32[]{:S(2)}) copy-start(bf16[2,4,2,128,128]{4,3,2,1,0:T(8,128)(2,1)} %get-tuple-element.27.own) | copy-start | bytes 1572868
  15.5 6.4 %collective-permute-start.2 = (bf16[4,2,128,128]{3,2,1,0:T(8,128)(2,1)S(1)}, bf16[4,2,128,128]{3,2,1,0:T(8,128)(2,1)S(1)}, u32[]{:S(2)}, u32[]{:S(2)}) collective-permute-start(bf16[4,2,128,128]{3,2,1,0:T(8,128)(2,1)S(1)} %collective-permute-done.pown), channel_id=1, source_target_pairs={{0,1},{1,0},{2,3},{3,2},{4,5},{5,4},{6,7},{7,6},{8,9},{9,8},{10,11... | collective-permute-start | bytes 786440 | tf_op jit(solution)/shard_map/ppermute | solution.py:295
  15.5 8.9 %collective-permute-start.3 = (bf16[4,2,128,128]{3,2,1,0:T(8,128)(2,1)S(1)}, bf16[4,2,128,128]{3,2,1,0:T(8,128)(2,1)S(1)}, u32[]{:S(2)}, u32[]{:S(2)}) collective-permute-start(bf16[4,2,128,128]{3,2,1,0:T(8,128)(2,1)S(1)} %collective-permute-done.pown), channel_id=1, source_target_pairs={{1,2},{2,1},{3,4},{4,3},{5,6},{6,5},{7,8},{8,7},{9,10},{10,9},{11,... | collective-permute-start | bytes 786440 | tf_op jit(solution)/shard_map/ppermute | solution.py:296
  17.8 2.6 %copy-start = (bf16[3,3,3,128,256]{4,3,2,1,0:T(8,128)(2,1)S(1)}, bf16[3,3,3,128,256]{4,3,2,1,0:T(8,128)(2,1)}, u32[]{:S(2)}) copy-start(bf16[3,3,3,128,256]{4,3,2,1,0:T(8,128)(2,1)} %param.20) | copy-start | bytes 5308420
  17.8 2.6 %copy-start.1 = (bf16[3,3,3,128,128]{4,3,2,1,0:T(8,128)(2,1)S(1)}, bf16[3,3,3,128,128]{4,3,2,1,0:T(8,128)(2,1)}, u32[]{:S(2)}) copy-start(bf16[3,3,3,128,128]{4,3,2,1,0:T(8,128)(2,1)} %w_two.5) | copy-start | bytes 2654212
  17.8 2.6 %copy-start.2 = (bf16[2,4,2,128,128]{4,3,2,1,0:T(8,128)(2,1)S(1)}, bf16[2,4,2,128,128]{4,3,2,1,0:T(8,128)(2,1)}, u32[]{:S(2)}) copy-start(bf16[2,4,2,128,128]{4,3,2,1,0:T(8,128)(2,1)} %video.7) | copy-start | bytes 1572868
  17.8 2.6 %copy-start.4 = (f32[128]{0:T(128)S(1)}, f32[128]{0:T(128)}, u32[]{:S(2)}) copy-start(f32[128]{0:T(128)} %param.19) | copy-start | bytes 1540
  20.4 3.9 %copy-start.5 = (s32[2]{0:T(128)S(1)}, s32[2]{0:T(128)}, u32[]{:S(2)}) copy-start(s32[2]{0:T(128)} %frames.5) | copy-start | bytes 28
  27.2 8.3 %collective-permute-start.5 = (bf16[2,64,256]{2,1,0:T(8,128)(2,1)S(1)}, bf16[2,64,256]{2,1,0:T(8,128)(2,1)S(1)}, u32[]{:S(2)}, u32[]{:S(2)}) collective-permute-start(bf16[2,64,256]{2,1,0:T(8,128)(2,1)S(1)} %get-tuple-element.36), channel_id=1, source_target_pairs={{0,16},{16,32},{32,48},{48,64},{64,80},{80,96},{96,112},{112,128},... | collective-permute-start | bytes 196616 | tf_op jit(solution)/shard_map/ppermute | solution.py:315
  31.8 6.5 %copy-start.10 = (f32[256]{0:T(256)S(1)}, f32[256]{0:T(256)}, u32[]{:S(2)}) copy-start(f32[256]{0:T(256)} %param.21) | copy-start | bytes 3076
  36.4 7.5 %collective-permute-start.6 = (bf16[2,2,64,256]{3,2,1,0:T(8,128)(2,1)S(1)}, bf16[2,2,64,256]{3,2,1,0:T(8,128)(2,1)S(1)}, u32[]{:S(2)}, u32[]{:S(2)}) collective-permute-start(bf16[2,2,64,256]{3,2,1,0:T(8,128)(2,1)S(1)} %shard_map.116), channel_id=1, source_target_pairs={{0,1},{1,2},{2,3},{3,4},{4,5},{5,6},{6,7},{7,8},{8,9},{9,10},{10,1... | collective-permute-start | bytes 393224 | tf_op jit(solution)/shard_map/ppermute | solution.py:318
